TPU v7x, 512 devices: a whole 4x8x8 slice. The times are simulated.
512 devices in a mesh: space: 128 (over z, y, core), feat: 4 (over x).
Axes of the slice: x: 4, y: 8, z: 8, core: 2. Of those that a mesh axis runs over, the one named last changes fastest.
Arguments:
- node: bfloat16 [32768, 512], P('space', 'feat'), may hold values from -6 to 6
- edge_feat: bfloat16 [65536, 512], P('space'), may hold values from -24 to 24
- agg_grad: bfloat16 [32768, 512], P('space', 'feat'), may hold values from -24 to 24
- w_send: bfloat16 [512, 512], P(None, 'feat'), may hold values from -0.25 to 0.25
- w_recv: bfloat16 [512, 512], P(None, 'feat'), may hold values from -0.25 to 0.25
- w_edge: bfloat16 [512, 512], P(None, 'feat'), may hold values from -0.25 to 0.25
- w_out: bfloat16 [512, 512], P(None, 'feat'), may hold values from -0.25 to 0.25
- receivers: int32 [65536], P('space'), may hold values from 0 to 255
- edge_slot: int32 [65536], P('space'), may hold values from 0 to 511, as said below
- send_rows: int32 [128, 512], P('space'), may hold values from 0 to 255, as said below
Outputs:
- node_grad: float32 [32768, 512], P('space', 'feat')
- edge_grad: float32 [65536, 512], P('space', 'feat')
- grad_send: float32 [512, 512], P('space', 'feat')
- grad_recv: float32 [512, 512], P('space', 'feat')
- grad_edge: float32 [512, 512], P('space', 'feat')
- grad_out: float32 [512, 512], P('space', 'feat')
Inputs may be any that keep to these rules, and one draw needn't show every extreme that they name: `edge_slot`: slot s = p * 4 + k of an edge of region d names the sender node p * 256 + send_rows[p, d * 4 + k]. Within each block send_rows[p, d * 4 to (d + 1) * 4 - 1] the rows are distinct.
All inputs are finite; a program needn't handle non-finite values.
Results may differ from a plain program's by a relative error of at most 0.0029.
Values may be sent and summed in bfloat16 or wider, within the bound.
No kernel may reach another device: no remote copies, remote signals or barrier semaphores. Data moves between devices by JAX's collectives and lax.ppermute only.
A program may use at most 64 MiB of HBM per device.

v0:
```python
import jax
import jax.numpy as jnp
from jax import lax
from jax.sharding import PartitionSpec as P


def contract_rows(left, right):
    return lax.dot_general(
        left, right, (((0,), (0,)), ((), ())), preferred_element_type=jnp.float32
    )


def local(
    node, edge_feat, agg_grad, w_send, w_recv, w_edge, w_out, receivers, edge_slot, send_rows
):
    spaces = lax.axis_size("space")
    slot_count = send_rows.shape[1]
    capacity = slot_count // spaces
    quarter = node.shape[1]
    node_count = node.shape[0]
    node_full, grad_full, send_full, recv_full, edge_full = (
        lax.all_gather(node, "feat", axis=1, tiled=True),
        lax.all_gather(agg_grad, "feat", axis=1, tiled=True),
        lax.all_gather(w_send, "feat", axis=1, tiled=True),
        lax.all_gather(w_recv, "feat", axis=1, tiled=True),
        lax.all_gather(w_edge, "feat", axis=1, tiled=True),
    )
    outgoing = send_rows[0]
    picked = jnp.take(node_full, outgoing, axis=0)
    arrived = lax.all_to_all(
        picked.reshape(spaces, capacity, picked.shape[1]),
        "space",
        split_axis=0,
        concat_axis=0,
        tiled=True,
    )
    slot_rows = arrived.reshape(slot_count, picked.shape[1])
    sender_rows = jnp.take(slot_rows, edge_slot, axis=0)
    receiver_rows = jnp.take(node_full, receivers, axis=0)
    message_grad = jnp.take(grad_full, receivers, axis=0)
    pre_act = (
        jnp.dot(sender_rows, w_send, preferred_element_type=jnp.float32)
        + jnp.dot(receiver_rows, w_recv, preferred_element_type=jnp.float32)
        + jnp.dot(edge_feat, w_edge, preferred_element_type=jnp.float32)
    )
    gate_sig = jax.nn.sigmoid(pre_act)
    activation = (pre_act * gate_sig).astype(jnp.bfloat16)
    act_grad = jnp.dot(message_grad, w_out, preferred_element_type=jnp.float32)
    hidden_grad = (act_grad * gate_sig * (1.0 + pre_act * (1.0 - gate_sig))).astype(jnp.bfloat16)
    row_offset = lax.axis_index("feat") * quarter
    send_slice = lax.dynamic_slice_in_dim(send_full, row_offset, quarter, 0)
    recv_slice = lax.dynamic_slice_in_dim(recv_full, row_offset, quarter, 0)
    edge_slice = lax.dynamic_slice_in_dim(edge_full, row_offset, quarter, 0)
    piece = lax.all_gather(hidden_grad, "feat", axis=1, tiled=True)

    def one_term(weight_rows):
        return lax.dot_general(
            piece, weight_rows, (((1,), (1,)), ((), ())), preferred_element_type=jnp.float32
        )

    send_terms = one_term(send_slice)
    recv_terms = one_term(recv_slice)
    edge_grad = one_term(edge_slice)

    def one_part(left, right):
        return contract_rows(left, right)

    summed = lax.psum_scatter(
        jnp.concatenate(
            [
                one_part(sender_rows, hidden_grad),
                one_part(receiver_rows, hidden_grad),
                one_part(edge_feat, hidden_grad),
                one_part(message_grad, activation),
            ],
            axis=1,
        ),
        "space",
        scatter_dimension=0,
        tiled=True,
    )
    grad_send = summed[:, 0:quarter]
    grad_recv = summed[:, quarter : 2 * quarter]
    grad_edge = summed[:, 2 * quarter : 3 * quarter]
    grad_out = summed[:, 3 * quarter : 4 * quarter]
    slot_sums = jax.ops.segment_sum(send_terms, edge_slot, num_segments=slot_count)
    returned = lax.all_to_all(
        slot_sums.reshape(spaces, capacity, quarter),
        "space",
        split_axis=0,
        concat_axis=0,
        tiled=True,
    )
    returned = returned.reshape(slot_count, quarter)
    node_grad = jax.ops.segment_sum(
        returned, outgoing, num_segments=node_count
    ) + jax.ops.segment_sum(recv_terms, receivers, num_segments=node_count)
    return (node_grad, edge_grad, grad_send, grad_recv, grad_edge, grad_out)


def solution(mesh):
    placed = (
        P("space", "feat"),
        P("space", None),
        P("space", "feat"),
        P(None, "feat"),
        P(None, "feat"),
        P(None, "feat"),
        P(None, "feat"),
        P("space"),
        P("space"),
        P("space", None),
    )
    return jax.shard_map(
        local,
        mesh=mesh,
        in_specs=placed,
        out_specs=(
            P("space", "feat"),
            P("space", "feat"),
            P("space", "feat"),
            P("space", "feat"),
            P("space", "feat"),
            P("space", "feat"),
        ),
        check_vma=False,
    )
```

profile of v0, /device:TPU:1, one launch (start us, length us, event | category | flops | bytes accessed | tf_op | source)
XLA Modules:
  0.0 314.9 jit_solution(8643704482623242015)
XLA Ops:
  7.2 0.7 compare_select_fusion
  8.0 10.5 %all_gather.19 = bf16[256,512]{1,0:T(8,128)(2,1)S(1)} all-gather(bf16[256,128]{1,0:T(8,128)(2,1)} %param.12), channel_id=1, replica_groups=mesh['space'=128,'feat'=4] {'feat'}, dimensions={1}, use_global_device_ids=true | all-gather | bytes 327680 | tf_op jit(solution)/shard_map/all_gather | solution.py:22
  18.5 2.0 gather_fusion.2
  20.6 0.9 reshape.34
  21.5 20.3 %all-to-all-start = ((bf16[128,4,512]{2,1,0:T(4,128)(2,1)}), bf16[128,4,512]{2,1,0:T(4,128)(2,1)S(1)}, u32[]{:S(2)}, u32[]{:S(2)}) async-start(bf16[128,4,512]{2,1,0:T(4,128)(2,1)} %reshape.34), calls=%async_computation | async-start | bytes 1048576 | tf_op jit(solution)/shard_map/all_to_all | solution.py:30
  42.6 2.0 gather_fusion.3
  44.6 10.1 %all_gather.18 = bf16[256,512]{1,0:T(8,128)(2,1)S(1)} all-gather(bf16[256,128]{1,0:T(8,128)(2,1)S(1)} %copy-done.5), channel_id=1, replica_groups=mesh['space'=128,'feat'=4] {'feat'}, dimensions={1}, use_global_device_ids=true | all-gather | bytes 327680 | tf_op jit(solution)/shard_map/all_gather | solution.py:23
  54.7 2.6 gather_fusion.1
  57.4 10.3 %all_gather.21 = bf16[512,512]{1,0:T(8,128)(2,1)S(1)} all-gather(bf16[512,128]{1,0:T(8,128)(2,1)S(1)} %copy-done.3), channel_id=1, replica_groups=mesh['space'=128,'feat'=4] {'feat'}, dimensions={1}, use_global_device_ids=true | all-gather | bytes 655360 | tf_op jit(solution)/shard_map/all_gather | solution.py:24
  67.6 12.1 %all_gather.22 = bf16[512,512]{1,0:T(8,128)(2,1)S(1)} all-gather(bf16[512,128]{1,0:T(8,128)(2,1)S(1)} %copy-done.4), channel_id=1, replica_groups=mesh['space'=128,'feat'=4] {'feat'}, dimensions={1}, use_global_device_ids=true | all-gather | bytes 655360 | tf_op jit(solution)/shard_map/all_gather | solution.py:25
  79.8 2.0 gather_fusion
  83.4 0.7 copy-done.1
  85.8 9.7 %all_gather.20 = bf16[512,512]{1,0:T(8,128)(2,1)S(1)} all-gather(bf16[512,128]{1,0:T(8,128)(2,1)S(1)} %fusion.1), channel_id=1, replica_groups=mesh['space'=128,'feat'=4] {'feat'}, dimensions={1}, use_global_device_ids=true | all-gather | bytes 655360 | tf_op jit(solution)/shard_map/all_gather | solution.py:54
  95.5 1.1 pad_maximum_fusion
  97.0 2.9 scatter_custom_fusion
  99.9 22.0 %all-to-all-start.1 = ((f32[128,4,128]{2,1,0:T(4,128)}), f32[128,4,128]{2,1,0:T(4,128)S(1)}, u32[]{:S(2)}, u32[]{:S(2)}) async-start(f32[128,4,128]{2,1,0:T(4,128)} %bitcast.1), calls=%async_computation.1 | async-start | bytes 524288 | tf_op jit(solution)/shard_map/all_to_all | solution.py:87
  121.9 11.7 %all_gather.23 = bf16[512,512]{1,0:T(8,128)(2,1)S(1)} all-gather(bf16[512,128]{1,0:T(8,128)(2,1)S(1)} %copy-done.2), channel_id=1, replica_groups=mesh['space'=128,'feat'=4] {'feat'}, dimensions={1}, use_global_device_ids=true | all-gather | bytes 655360 | tf_op jit(solution)/shard_map/all_gather | solution.py:26
  133.6 1.3 dynamic-slice
  135.8 2.3 scatter_custom_fusion.2
  138.1 1.0 fusion.6
  139.1 2.3 scatter_custom_fusion.1
  141.4 0.7 add.49
  142.0 162.3 %all-reduce.3.cloned.1.call-done = f32[512,512]{0,1:T(8,128)} async-done(((f32[512,512]{0,1:T(8,128)}), f32[512,512]{0,1:T(8,128)}) %all-reduce.3.cloned.1.call-update) | async-done | bytes 1048592
  304.4 1.1 fusion.29
  (47 shorter events, 7.5 us)
Async XLA Ops:
  7.2 75.4 %copy-start = (bf16[512,512]{1,0:T(8,128)(2,1)S(1)}, bf16[512,512]{1,0:T(8,128)(2,1)}, u32[]{:S(2)}) copy-start(bf16[512,512]{1,0:T(8,128)(2,1)} %param.13) | copy-start | bytes 1572868
  7.2 0.8 copy-start.8
  21.5 20.4 %copy-start.6 = (s32[512]{0:T(512)S(1)}, s32[512]{0:T(512)}, u32[]{:S(2)}) copy-start(s32[512]{0:T(512)} %param.20) | copy-start | bytes 6148
  21.5 58.2 %all-to-all-start = ((bf16[128,4,512]{2,1,0:T(4,128)(2,1)}), bf16[128,4,512]{2,1,0:T(4,128)(2,1)S(1)}, u32[]{:S(2)}, u32[]{:S(2)}) async-start(bf16[128,4,512]{2,1,0:T(4,128)(2,1)} %reshape.34), calls=%async_computation | async-start | bytes 1048576 | tf_op jit(solution)/shard_map/all_to_all | solution.py:30
  41.8 262.5 %all-reduce.3.cloned.1.call-start = ((), (), s32[]{:S(2)}) async-start(), calls=%async_computation.2 | async-start | bytes 2097152
  41.9 0.7 copy-start.7
  42.6 2.0 copy-start.5
  54.7 2.6 copy-start.3
  57.3 10.3 %copy-start.4 = (bf16[512,128]{1,0:T(8,128)(2,1)S(1)}, bf16[512,128]{1,0:T(8,128)(2,1)}, u32[]{:S(2)}) copy-start(bf16[512,128]{1,0:T(8,128)(2,1)} %param.16) | copy-start | bytes 393220
  82.2 0.9 copy-start.2
  83.1 1.0 copy-start.1
  83.1 1.1 copy-start.9
  99.9 39.2 %all-to-all-start.1 = ((f32[128,4,128]{2,1,0:T(4,128)}), f32[128,4,128]{2,1,0:T(4,128)S(1)}, u32[]{:S(2)}, u32[]{:S(2)}) async-start(f32[128,4,128]{2,1,0:T(4,128)} %bitcast.1), calls=%async_computation.1 | async-start | bytes 524288 | tf_op jit(solution)/shard_map/all_to_all | solution.py:87
Sparse Core Ops, SparseCore 0:
  96.8 207.5 all-reduce.2
where the time goes:
time: 316 us; the launch traced here: 315 us
  waiting for transfers between devices  162 us (51%)
  blocking collectives  64.3 us (20%)
  starting transfers between devices  42.4 us (13%)
  local copies, waits for them, and re-layouts  16.5 us (5%)
  between operations  14.9 us (5%)
  other arithmetic  10.2 us (3%)
  matrix products  4.25 us (1%)
    unnamed x2, waiting for transfers between devices  162 us
    all_to_all x1, starting transfers between devices, local(): lax.all_to_all(slot_sums.reshape(spaces, capacity, quarter), 'space', spl...  22 us
    all_to_all x1, starting transfers between devices, local(): lax.all_to_all(picked.reshape(spaces, capacity, picked.shape[1]), 'space'...  20.3 us
    all_gather x1, blocking collectives, local(): lax.all_gather(w_recv, 'feat', axis=1, tiled=True)  12.1 us
    all_gather x1, blocking collectives, local(): lax.all_gather(w_edge, 'feat', axis=1, tiled=True)  11.7 us
    all_gather x1, blocking collectives, local(): lax.all_gather(node, 'feat', axis=1, tiled=True)  10.5 us
    all_gather x1, blocking collectives, local(): lax.all_gather(w_send, 'feat', axis=1, tiled=True)  10.3 us
    all_gather x1, blocking collectives, local(): lax.all_gather(agg_grad, 'feat', axis=1, tiled=True)  10.1 us
  transfers between devices with their start and end apart: 3, of which 1 were waited for; matrix products, arithmetic and copies ran while one was open for 5% of the time, Pallas kernels for 0%

commit v1 on v0

v1 whole, which is shorter than its diff:
```python
import jax
import jax.numpy as jnp
from jax import lax
from jax.experimental import pallas as pl
from jax.experimental.pallas import tpu as pltpu
from jax.sharding import PartitionSpec as P

F32 = jnp.float32
BF16 = jnp.bfloat16
LANES = 128


def mm(a, b):
    return jnp.dot(a, b, preferred_element_type=F32)


def mm_nt(a, b):
    return lax.dot_general(a, b, (((1,), (1,)), ((), ())), preferred_element_type=F32)


def mm_tn(a, b):
    return lax.dot_general(a, b, (((0,), (0,)), ((), ())), preferred_element_type=F32)


def hot(mask):
    return jnp.where(mask, 1.0, 0.0).astype(BF16)


def hot_by_column(row, rows):
    shape = (rows, row.shape[1])
    return hot(lax.broadcasted_iota(jnp.int32, shape, 0) == row)


def hot_by_row(row, columns):
    count = row.shape[1]
    column = jnp.broadcast_to(row, (LANES, count)).T
    lane = lax.broadcasted_iota(jnp.int32, (count, LANES), 1)
    parts = [hot(column == lane + start) for start in range(0, columns, LANES)]
    return jnp.concatenate(parts, axis=1)


def join(ref, start, size):
    return jnp.concatenate([ref[q, start : start + size, :] for q in range(ref.shape[0])], axis=1)


def split_high_low(x):
    high = x.astype(BF16)
    return high, (x - high.astype(F32)).astype(BF16)


def first_kernel(node, agg, w_send, w_recv, w_edge, rows, shared, picked):
    count, quarter = node.shape
    for q in range(shared.shape[0]):
        block = slice(q * quarter, (q + 1) * quarter)
        shared[q, 0:count, :] = node[...]
        shared[q, count : 2 * count, :] = agg[...]
        for i, weight in enumerate((w_send, w_recv, w_edge)):
            start = 2 * count + i * quarter
            shared[q, start : start + quarter, :] = weight[block, :]
    picked[...] = mm(hot_by_row(rows[...], count), node[...]).astype(BF16)


def receiver_kernel(
    shared, edge_feat, w_recv, w_edge, w_out, receivers, slots,
    receiver_rows, message_grad, pre_part, act_grad, slot_hot,
):
    count = shared.shape[1] - 3 * LANES
    count = count // 2
    receive = hot_by_row(receivers[...], count)
    receiver_rows[...] = mm(receive, join(shared, 0, count)).astype(BF16)
    message_grad[...] = mm(receive, join(shared, count, count)).astype(BF16)
    pre_part[...] = mm(receiver_rows[...], w_recv[...]) + mm(edge_feat[...], w_edge[...])
    act_grad[...] = mm(message_grad[...], w_out[...])
    slot_hot[...] = hot_by_row(slots[...], slot_hot.shape[1])


def hidden_kernel(
    slot_rows, slot_hot, w_send, pre_part, act_grad, sender_rows, hidden, activation
):
    sender_rows[...] = mm(slot_hot[...], join(slot_rows, 0, slot_rows.shape[1])).astype(BF16)
    pre_act = mm(sender_rows[...], w_send[...]) + pre_part[...]
    gate = jax.nn.sigmoid(pre_act)
    activation[...] = (pre_act * gate).astype(BF16)
    grad = (act_grad[...] * gate * (1.0 + pre_act * (1.0 - gate))).astype(BF16)
    for q in range(hidden.shape[0]):
        hidden[q] = grad


def weight_kernel(
    core, sender_rows, receiver_rows, edge_feat, message_grad, hidden, activation, kept, given
):
    grad = hidden[0]
    size = sender_rows.shape[1]
    mine = core[0] == 0
    for i, (low, high, high_right) in enumerate(
        (
            (sender_rows, edge_feat, grad),
            (receiver_rows, message_grad, activation[...]),
        )
    ):
        low_sum = mm_tn(low[...], grad)
        high_sum = mm_tn(high[...], high_right)
        kept[i * size : (i + 1) * size, :] = jnp.where(mine, low_sum, high_sum)
        given[i * size : (i + 1) * size, :] = jnp.where(mine, high_sum, low_sum)


def payload_kernel(hidden, shared, slots, kept, taken, payload):
    size = kept.shape[0] // 2
    quarter = kept.shape[1]
    weights = shared.shape[1] - 3 * LANES
    w_send = join(shared, weights, LANES)
    sums = mm(hot_by_column(slots[...], payload.shape[0]), join(hidden, 0, hidden.shape[1]))
    high, low = split_high_low(sums)
    terms = mm_nt(high, w_send) + mm_nt(low, w_send)
    high, low = split_high_low(terms)
    payload[:, 0:quarter] = (kept[0:size, :] + taken[0:size, :]).astype(BF16)
    payload[:, quarter : 2 * quarter] = (kept[size:, :] + taken[size:, :]).astype(BF16)
    payload[:, 2 * quarter : 3 * quarter] = high
    payload[:, 3 * quarter : 4 * quarter] = low


def edge_kernel(hidden, shared, receivers, edge_grad, recv_part):
    full = join(hidden, 0, hidden.shape[1])
    weights = shared.shape[1] - 3 * LANES
    edge_grad[...] = mm_nt(full, join(shared, weights + 2 * LANES, LANES))
    sums = mm(hot_by_column(receivers[...], recv_part.shape[0]), full)
    high, low = split_high_low(sums)
    w_recv = join(shared, weights + LANES, LANES)
    recv_part[...] = mm_nt(high, w_recv) + mm_nt(low, w_recv)


def last_kernel(arrived, rows, recv_part, node_grad, grad_send, grad_recv, grad_edge, grad_out):
    quarter = node_grad.shape[1]
    slots = arrived.shape[0]
    back = mm(hot_by_column(rows[...], node_grad.shape[0]), arrived[:, 2 * quarter : 4 * quarter])
    node_grad[...] = recv_part[...] + (back[:, 0:quarter] + back[:, quarter:])
    shape = (8, slots)
    place = lax.broadcasted_iota(jnp.int32, shape, 1) % 8
    pick = hot(place == lax.broadcasted_iota(jnp.int32, shape, 0))
    sums = mm(pick, arrived[:, 0 : 2 * quarter])
    grad_send[...] = sums[0:4, 0:quarter]
    grad_recv[...] = sums[0:4, quarter:]
    grad_edge[...] = sums[4:8, 0:quarter]
    grad_out[...] = sums[4:8, quarter:]


def call(kernel, outs, *operands, scalars=0, flops=0):
    vmem = pl.BlockSpec(memory_space=pltpu.VMEM)
    smem = pl.BlockSpec(memory_space=pltpu.SMEM)
    moved = sum(x.size * x.dtype.itemsize for x in operands)
    moved += sum(x.size * x.dtype.itemsize for x in outs)
    return pl.pallas_call(
        kernel,
        out_shape=list(outs),
        in_specs=[smem] * scalars + [vmem] * (len(operands) - scalars),
        out_specs=[vmem] * len(outs),
        compiler_params=pltpu.CompilerParams(vmem_limit_bytes=24 * 1024 * 1024),
        cost_estimate=pl.CostEstimate(flops=flops, bytes_accessed=moved, transcendentals=0),
    )(*operands)


def local(
    node, edge_feat, agg_grad, w_send, w_recv, w_edge, w_out, receivers, edge_slot, send_rows
):
    spaces = lax.axis_size("space")
    feats = lax.axis_size("feat")
    slot_count = send_rows.shape[1]
    capacity = slot_count // spaces
    node_count, quarter = node.shape
    edges, width = edge_feat.shape
    sds = jax.ShapeDtypeStruct
    receivers = receivers.reshape(1, edges)
    slots = edge_slot.reshape(1, edges)
    core = (lax.axis_index("space") % 2).reshape(1)

    def over_feat(x):
        return lax.all_to_all(x, "feat", split_axis=0, concat_axis=0, tiled=True)

    def over_space(x):
        lanes = x.shape[1]
        moved = lax.all_to_all(
            x.reshape(spaces, capacity, lanes), "space", split_axis=0, concat_axis=0, tiled=True
        )
        return moved.reshape(slot_count, lanes)

    shared, picked = call(
        first_kernel,
        (
            sds((feats, 2 * node_count + 3 * quarter, quarter), BF16),
            sds((slot_count, quarter), BF16),
        ),
        node, agg_grad, w_send, w_recv, w_edge, send_rows,
        flops=2 * slot_count * node_count * quarter,
    )
    shared = over_feat(shared)
    arrived = over_space(picked)
    receiver_rows, message_grad, pre_part, act_grad, slot_hot = call(
        receiver_kernel,
        (
            sds((edges, width), BF16),
            sds((edges, width), BF16),
            sds((edges, quarter), F32),
            sds((edges, quarter), F32),
            sds((edges, slot_count), BF16),
        ),
        shared, edge_feat, w_recv, w_edge, w_out, receivers, slots,
        flops=4 * edges * width * (node_count + 2 * quarter),
    )
    slot_rows = over_feat(jnp.broadcast_to(arrived[None], (feats, slot_count, quarter)))
    sender_rows, hidden, activation = call(
        hidden_kernel,
        (
            sds((edges, width), BF16),
            sds((feats, edges, quarter), BF16),
            sds((edges, quarter), BF16),
        ),
        slot_rows, slot_hot, w_send, pre_part, act_grad,
        flops=2 * edges * width * (slot_count + quarter),
    )
    hidden_full = over_feat(hidden)
    kept, given = call(
        weight_kernel,
        (sds((2 * width, quarter), F32), sds((2 * width, quarter), F32)),
        core, sender_rows, receiver_rows, edge_feat, message_grad, hidden, activation,
        scalars=1,
        flops=8 * edges * width * quarter,
    )
    taken = lax.ppermute(given, "space", [(i, i ^ 1) for i in range(spaces)])
    (payload,) = call(
        payload_kernel,
        (sds((slot_count, 4 * quarter), BF16),),
        hidden_full, shared, slots, kept, taken,
        flops=2 * slot_count * width * (edges + 2 * quarter),
    )
    returned = over_space(payload)
    edge_grad, recv_part = call(
        edge_kernel,
        (sds((edges, quarter), F32), sds((node_count, quarter), F32)),
        hidden_full, shared, receivers,
        flops=2 * edges * width * (node_count + 2 * quarter),
    )
    small = sds((width // spaces, quarter), F32)
    node_grad, grad_send, grad_recv, grad_edge, grad_out = call(
        last_kernel,
        (sds((node_count, quarter), F32), small, small, small, small),
        returned, send_rows, recv_part,
        flops=4 * node_count * slot_count * quarter,
    )
    return (node_grad, edge_grad, grad_send, grad_recv, grad_edge, grad_out)


def solution(mesh):
    placed = (
        P("space", "feat"),
        P("space", None),
        P("space", "feat"),
        P(None, "feat"),
        P(None, "feat"),
        P(None, "feat"),
        P(None, "feat"),
        P("space"),
        P("space"),
        P("space", None),
    )
    return jax.shard_map(
        local,
        mesh=mesh,
        in_specs=placed,
        out_specs=(P("space", "feat"),) * 6,
        check_vma=False,
    )
```

time: 316 us -> 118 us (0.37)
  waiting for transfers between devices: 162 us -> 21 us
  starting transfers between devices: 42.4 us -> 14.8 us
  between operations: 14.9 us -> 0.77 us
  other arithmetic: 10.2 us -> 0 us
  Pallas kernels: 0 us -> 6.01 us
  blocking collectives: 64.3 us -> 59.3 us
  matrix products: 4.25 us -> 0 us
    unnamed x2 -> x0, waiting for transfers between devices: 162 us -> none
    all_gather x6 -> x0, blocking collectives: 64.3 us -> none  [the longest x1 12.1 us: local(): lax.all_gather(w_recv, 'feat', axis=1, tiled=True)]
    all_to_all x0 -> x3, blocking collectives: none -> 59.3 us  [the longest x1 31 us: over_space(): lax.all_to_all(x.reshape(spaces, capacity, lanes), 'space', split_axis=0,...]
    all_to_all x2, starting transfers between devices: 42.4 us -> 9.86 us  [the longest x1 6.26 us: over_space(): lax.all_to_all(x.reshape(spaces, capacity, lanes), 'space', split_axis=0,...]
    all_to_all x2, waiting for transfers between devices: 0.01 us -> 21 us  [the longest x1 19.4 us: over_space(): lax.all_to_all(x.reshape(spaces, capacity, lanes), 'space', split_axis=0,...]
    gather x4 -> x0, local copies, waits for them, and re-layouts: 8.52 us -> none  [the longest x1 2.61 us: local(): message_grad = jnp.take(grad_full, receivers, axis=0)]
    scatter-add x3 -> x0, other arithmetic: 7.47 us -> none  [the longest x1 2.91 us: local(): jax.ops.segment_sum(send_terms, edge_slot, num_segments=slot_count)]
    unnamed x25 -> x36, local copies, waits for them, and re-layouts: 5.86 us -> 13.2 us
  transfers between devices with their start and end apart: 3 -> 3, of which waited for: 1 -> 2; matrix products, arithmetic and copies ran while one was open for 5% -> 0% of each run, Pallas kernels for 0% -> 2%
where the time goes in v1:
time: 118 us; the launch traced here: 117 us
  blocking collectives  59.3 us (50%)
  waiting for transfers between devices  21 us (18%)
  local copies, waits for them, and re-layouts  15.1 us (13%)
  starting transfers between devices  14.8 us (13%)
  Pallas kernels  6.01 us (5%)
    all_to_all x1, blocking collectives, over_space(): lax.all_to_all(x.reshape(spaces, capacity, lanes), 'space', split_axis=0,...  31 us
    all_to_all x2, blocking collectives, over_feat(): return lax.all_to_all(x, 'feat', split_axis=0, concat_axis=0, tiled=True)  28.3 us
    all_to_all x1, waiting for transfers between devices, over_space(): lax.all_to_all(x.reshape(spaces, capacity, lanes), 'space', split_axis=0,...  19.4 us
    unnamed x36, local copies, waits for them, and re-layouts  13.2 us
    all_to_all x1, starting transfers between devices, over_space(): lax.all_to_all(x.reshape(spaces, capacity, lanes), 'space', split_axis=0,...  6.26 us
    pallas_call x7, Pallas kernels, call(): pl.pallas_call(kernel, out_shape=list(outs), in_specs=[smem] * scalars +...  6.01 us
    ppermute x1, starting transfers between devices, local(): taken = lax.ppermute(given, 'space', [(i, i ^ 1) for i in range(spaces)])  4.96 us
    all_to_all x1, starting transfers between devices, over_feat(): return lax.all_to_all(x, 'feat', split_axis=0, concat_axis=0, tiled=True)  3.6 us
  transfers between devices with their start and end apart: 3, of which 2 were waited for; matrix products, arithmetic and copies ran while one was open for 0% of the time, Pallas kernels for 2%

profile of v1, /device:TPU:1, one launch (start us, length us, event | category | flops | bytes accessed | tf_op | source)
XLA Modules:
  0.0 117.0 jit_solution(9202547604416035383)
XLA Ops:
  0.6 0.9 copy-done.1
  1.5 0.9 copy-done.7
  2.4 0.9 copy-done.9
  3.4 0.8 copy-done.11
  6.0 31.0 %all_to_all.25 = bf16[128,4,128]{2,1,0:T(4,128)(2,1)S(1)} all-to-all(bf16[128,4,128]{2,1,0:T(4,128)(2,1)S(1)} %bitcast.5), channel_id=1, replica_groups=mesh['space'=128,'feat'=4] {'space'}, dimensions={0} | all-to-all | bytes 262144 | tf_op jit(solution)/shard_map/all_to_all | solution.py:181
  37.0 16.6 %all_to_all.26.shared = bf16[4,896,128]{2,1,0:T(8,128)(2,1)S(1)} all-to-all(bf16[4,896,128]{2,1,0:T(8,128)(2,1)S(1)} %get-tuple-element.26), channel_id=1, replica_groups=mesh['space'=128,'feat'=4] {'feat'}, dimensions={0} | all-to-all | bytes 1835008 | tf_op jit(solution)/shard_map/all_to_all | solution.py:177
  53.6 0.9 broadcast_in_dim.8
  54.5 3.6 %all-to-all-start.1 = ((bf16[4,512,128]{2,1,0:T(8,128)(2,1)}), bf16[4,512,128]{2,1,0:T(8,128)(2,1)S(1)}, u32[]{:S(2)}, u32[]{:S(2)}) async-start(bf16[4,512,128]{2,1,0:T(8,128)(2,1)} %broadcast_in_dim.8), calls=%async_computation.1 | async-start | bytes 1048576 | tf_op jit(solution)/shard_map/all_to_all | solution.py:177
  58.8 0.9 copy-done.8
  59.7 0.9 copy-done.10
  60.6 0.9 copy-done.17
  61.5 0.9 shard_map.146
  63.8 1.6 %all-to-all-done.1.slot_rows = bf16[4,512,128]{2,1,0:T(8,128)(2,1)S(1)} async-done(((bf16[4,512,128]{2,1,0:T(8,128)(2,1)}), bf16[4,512,128]{2,1,0:T(8,128)(2,1)S(1)}, u32[]{:S(2)}, u32[]{:S(2)}) %all-to-all-start.1) | async-done | bytes 524320 | tf_op jit(solution)/shard_map/all_to_all | solution.py:177
  65.4 0.9 copy-done.2
  66.3 0.9 copy-done.4
  67.3 0.9 copy-done.6
  69.7 5.0 %collective-permute-start = (f32[1024,128]{1,0:T(8,128)S(1)}, f32[1024,128]{1,0:T(8,128)S(1)}, u32[]{:S(2)}, u32[]{:S(2)}) collective-permute-start(f32[1024,128]{1,0:T(8,128)S(1)} %get-tuple-element.36), channel_id=1, source_target_pairs={{0,4},{4,0},{8,12},{12,8},{16,20},{20,16},{24,28},{28,24},{32,36},... | collective-permute-start | bytes 1572872 | tf_op jit(solution)/shard_map/ppermute | solution.py:228
  74.7 11.7 %all_to_all.27.hidden = bf16[4,512,128]{2,1,0:T(8,128)(2,1)S(1)} all-to-all(bf16[4,512,128]{2,1,0:T(8,128)(2,1)S(1)} %get-tuple-element.30.hidden), channel_id=1, replica_groups=mesh['space'=128,'feat'=4] {'feat'}, dimensions={0} | all-to-all | bytes 1048576 | tf_op jit(solution)/shard_map/all_to_all | solution.py:177
  86.4 1.1 shard_map.149
  87.5 0.9 reshape.35
  88.5 6.3 %all-to-all-start.4 = ((bf16[128,4,512]{2,1,0:T(4,128)(2,1)}), bf16[128,4,512]{2,1,0:T(4,128)(2,1)S(1)}, u32[]{:S(2)}, u32[]{:S(2)}) async-start(bf16[128,4,512]{2,1,0:T(4,128)(2,1)} %reshape.35), calls=%async_computation.4 | async-start | bytes 1048576 | tf_op jit(solution)/shard_map/all_to_all | solution.py:181
  94.7 1.3 %shard_map.150 = (f32[512,128]{1,0:T(8,128)}, f32[256,128]{1,0:T(8,128)S(1)}) custom-call(bf16[4,512,128]{2,1,0:T(8,128)(2,1)S(1)} %all_to_all.27.hidden, bf16[4,896,128]{2,1,0:T(8,128)(2,1)S(1)} %all_to_all.26.shared, s32[1,512]{1,0:T(1,128)S(1)} %bitcast.9), custom_call_target="tpu_custom_call" | custom-call | flops 268435456 | bytes 1837056 | tf_op jit(solution)/shard_map/pallas_call | solution.py:152
  96.1 19.4 %all-to-all-done.4 = bf16[128,4,512]{2,1,0:T(4,128)(2,1)S(1)} async-done(((bf16[128,4,512]{2,1,0:T(4,128)(2,1)}), bf16[128,4,512]{2,1,0:T(4,128)(2,1)S(1)}, u32[]{:S(2)}, u32[]{:S(2)}) %all-to-all-start.4) | async-done | bytes 524320 | tf_op jit(solution)/shard_map/all_to_all | solution.py:181
  116.1 0.9 shard_map.151
  (31 shorter events, 6.1 us)
Async XLA Ops:
  0.6 0.9 copy-start.1
  1.5 0.9 copy-start.7
  2.4 0.9 copy-start.9
  3.3 0.8 copy-start.11
  4.2 0.8 copy-start.12
  5.0 0.7 copy-start.13
  54.5 3.6 %copy-start = (bf16[512,512]{1,0:T(8,128)(2,1)S(1)}, bf16[512,512]{1,0:T(8,128)(2,1)}, u32[]{:S(2)}) copy-start(bf16[512,512]{1,0:T(8,128)(2,1)} %edge_feat.3) | copy-start | bytes 1572868
  54.5 3.6 %copy-start.16 = (s32[512]{0:T(512)S(1)}, s32[512]{0:T(512)}, u32[]{:S(2)}) copy-start(s32[512]{0:T(512)} %param.17) | copy-start | bytes 6148
  54.5 11.0 %all-to-all-start.1 = ((bf16[4,512,128]{2,1,0:T(8,128)(2,1)}), bf16[4,512,128]{2,1,0:T(8,128)(2,1)S(1)}, u32[]{:S(2)}, u32[]{:S(2)}) async-start(bf16[4,512,128]{2,1,0:T(8,128)(2,1)} %broadcast_in_dim.8), calls=%async_computation.1 | async-start | bytes 1048576 | tf_op jit(solution)/shard_map/all_to_all | solution.py:177
  58.1 0.7 copy-start.15
  58.8 0.9 copy-start.8
  59.7 0.9 copy-start.10
  60.6 0.9 copy-start.17
  62.4 0.7 copy-start.3
  63.1 0.7 copy-start.5
  65.4 0.9 copy-start.2
  66.3 0.9 copy-start.4
  67.3 0.9 copy-start.6
  69.7 16.7 %collective-permute-start = (f32[1024,128]{1,0:T(8,128)S(1)}, f32[1024,128]{1,0:T(8,128)S(1)}, u32[]{:S(2)}, u32[]{:S(2)}) collective-permute-start(f32[1024,128]{1,0:T(8,128)S(1)} %get-tuple-element.36), channel_id=1, source_target_pairs={{0,4},{4,0},{8,12},{12,8},{16,20},{20,16},{24,28},{28,24},{32,36},... | collective-permute-start | bytes 1572872 | tf_op jit(solution)/shard_map/ppermute | solution.py:228
  88.5 27.0 %all-to-all-start.4 = ((bf16[128,4,512]{2,1,0:T(4,128)(2,1)}), bf16[128,4,512]{2,1,0:T(4,128)(2,1)S(1)}, u32[]{:S(2)}, u32[]{:S(2)}) async-start(bf16[128,4,512]{2,1,0:T(4,128)(2,1)} %reshape.35), calls=%async_computation.4 | async-start | bytes 1048576 | tf_op jit(solution)/shard_map/all_to_all | solution.py:181
  115.4 0.7 copy-start.14

commit v2 on v1

v2 whole, which is shorter than its diff:
```python
import jax
import jax.numpy as jnp
from jax import lax
from jax.experimental import pallas as pl
from jax.experimental.pallas import tpu as pltpu
from jax.sharding import PartitionSpec as P

F32 = jnp.float32
BF16 = jnp.bfloat16
LANES = 128


def mm(a, b):
    return jnp.dot(a, b, preferred_element_type=F32)


def mm_nt(a, b):
    return lax.dot_general(a, b, (((1,), (1,)), ((), ())), preferred_element_type=F32)


def mm_tn(a, b):
    return lax.dot_general(a, b, (((0,), (0,)), ((), ())), preferred_element_type=F32)


def hot(mask):
    return jnp.where(mask, 1.0, 0.0).astype(BF16)


def hot_by_column(row, rows):
    shape = (rows, row.shape[1])
    return hot(lax.broadcasted_iota(jnp.int32, shape, 0) == row)


def hot_by_row(row, columns):
    count = row.shape[1]
    column = jnp.broadcast_to(row, (LANES, count)).T
    lane = lax.broadcasted_iota(jnp.int32, (count, LANES), 1)
    parts = [hot(column == lane + start) for start in range(0, columns, LANES)]
    return jnp.concatenate(parts, axis=1)


def fetch(sems, *pairs):
    copies = [pltpu.make_async_copy(src, dst, sems.at[i]) for i, (src, dst) in enumerate(pairs)]
    for copy in copies:
        copy.start()
    return copies


def join(ref, start, size):
    return jnp.concatenate([ref[q, start : start + size, :] for q in range(ref.shape[0])], axis=1)


def split_high_low(x):
    high = x.astype(BF16)
    return high, (x - high.astype(F32)).astype(BF16)


def first_kernel(node, agg, rows, own, picked, rows_here, sems):
    count = node.shape[0]
    copies = fetch(
        sems,
        (rows, rows_here),
        (node, own.at[0:count, :]),
        (agg, own.at[count : 2 * count, :]),
    )
    copies[0].wait()
    pick = hot_by_row(rows_here[...], count)
    copies[1].wait()
    picked[...] = mm(pick, own[0:count, :]).astype(BF16)
    copies[2].wait()


def spread_kernel(rows, after, spread):
    del after
    for q in range(spread.shape[0]):
        spread[q] = rows[...]


def middle_kernel(
    core, shared, slot_rows, edge_feat, w_send, w_recv, w_edge, w_out, receivers, slots,
    kept, given, slot_sums, hidden,
):
    count = shared.shape[1] // 2
    size = edge_feat.shape[1]
    receive = hot_by_row(receivers[...], count)
    receiver_rows = mm(receive, join(shared, 0, count)).astype(BF16)
    message_grad = mm(receive, join(shared, count, count)).astype(BF16)
    act_grad = mm(message_grad, w_out[...])
    pre_act = mm(receiver_rows, w_recv[...]) + mm(edge_feat[...], w_edge[...])
    slot_hot = hot_by_row(slots[...], slot_rows.shape[1])
    sender_rows = mm(slot_hot, join(slot_rows, 0, slot_rows.shape[1])).astype(BF16)
    pre_act += mm(sender_rows, w_send[...])
    gate = jax.nn.sigmoid(pre_act)
    activation = (pre_act * gate).astype(BF16)
    grad = (act_grad * gate * (1.0 + pre_act * (1.0 - gate))).astype(BF16)
    hidden[...] = grad
    mine = core[0] == 0
    for i, (low, high, high_right) in enumerate(
        (
            (sender_rows, edge_feat[...], grad),
            (receiver_rows, message_grad, activation),
        )
    ):
        low_sum = mm_tn(low, grad)
        high_sum = mm_tn(high, high_right)
        kept[i * size : (i + 1) * size, :] = jnp.where(mine, low_sum, high_sum)
        given[i * size : (i + 1) * size, :] = jnp.where(mine, high_sum, low_sum)
    slot_sums[...] = mm(hot_by_column(slots[...], slot_sums.shape[0]), grad).astype(BF16)


def payload_kernel(kept, taken, sums, payload):
    size = kept.shape[0] // 2
    quarter = kept.shape[1]
    payload[:, 0:quarter] = (kept[0:size, :] + taken[0:size, :]).astype(BF16)
    payload[:, quarter : 2 * quarter] = (kept[size:, :] + taken[size:, :]).astype(BF16)
    payload[:, 2 * quarter : 3 * quarter] = sums[...]


def edge_kernel(place, hidden, w_edge, receivers, mine, *rest):
    *theirs, recv_sums = rest
    quarter = mine.shape[1]
    feats = 1 + len(theirs)
    for step, out in enumerate((mine, *theirs)):
        start = pl.multiple_of(lax.rem(place[0] + step, feats) * quarter, quarter)
        part = mm_nt(hidden[...], w_edge[pl.ds(start, quarter), :])
        out[...] = part.astype(out.dtype)
    recv_sums[...] = mm(hot_by_column(receivers[...], recv_sums.shape[0]), hidden[...])


def node_part_kernel(
    arrived, rows, recv_sums, w_send, w_recv, mine, *rest
):
    *theirs, parts, edge_grad, grad_send, grad_recv, grad_edge, grad_out = rest
    quarter = recv_sums.shape[1]
    back = mm(
        hot_by_column(rows[...], recv_sums.shape[0]), arrived[:, 2 * quarter : 3 * quarter]
    )
    total = 0.0
    for sums, weight in ((back, w_send), (recv_sums[...], w_recv)):
        high, low = split_high_low(sums)
        total += mm_nt(high, weight[...]) + mm_nt(low, weight[...])
    for q in range(parts.shape[0]):
        parts[q] = total[:, q * quarter : (q + 1) * quarter].astype(BF16)
    edge_total = mine[...]
    for part in theirs:
        edge_total += part[...].astype(F32)
    edge_grad[...] = edge_total
    shape = (8, arrived.shape[0])
    place = lax.broadcasted_iota(jnp.int32, shape, 1) % 8
    pick = hot(place == lax.broadcasted_iota(jnp.int32, shape, 0))
    sums = mm(pick, arrived[:, 0 : 2 * quarter])
    grad_send[...] = sums[0:4, 0:quarter]
    grad_recv[...] = sums[0:4, quarter:]
    grad_edge[...] = sums[4:8, 0:quarter]
    grad_out[...] = sums[4:8, quarter:]


def node_sum_kernel(parts, node_grad):
    total = parts[0].astype(F32)
    for q in range(1, parts.shape[0]):
        total += parts[q].astype(F32)
    node_grad[...] = total


ANY = pl.BlockSpec(memory_space=pl.ANY)
VMEM = pl.BlockSpec(memory_space=pltpu.VMEM)
SMEM = pl.BlockSpec(memory_space=pltpu.SMEM)


def call(kernel, outs, *operands, places=None, scratch=(), flops=0, limit=24 * 1024 * 1024):
    moved = sum(x.size * x.dtype.itemsize for x in operands)
    moved += sum(x.size * x.dtype.itemsize for x in outs)
    return pl.pallas_call(
        kernel,
        out_shape=list(outs),
        in_specs=list(places or [VMEM] * len(operands)),
        out_specs=[VMEM] * len(outs),
        scratch_shapes=list(scratch),
        compiler_params=pltpu.CompilerParams(vmem_limit_bytes=limit),
        cost_estimate=pl.CostEstimate(flops=flops, bytes_accessed=moved, transcendentals=0),
    )(*operands)


def local(
    node, edge_feat, agg_grad, w_send, w_recv, w_edge, w_out, receivers, edge_slot, send_rows
):
    spaces = lax.axis_size("space")
    feats = lax.axis_size("feat")
    slot_count = send_rows.shape[1]
    capacity = slot_count // spaces
    node_count, quarter = node.shape
    edges, width = edge_feat.shape
    sds = jax.ShapeDtypeStruct
    receivers = receivers.reshape(1, edges)
    slots = edge_slot.reshape(1, edges)
    core = (lax.axis_index("space") % 2).reshape(1)
    place = lax.axis_index("feat").reshape(1)

    def over_feat(x):
        return lax.all_to_all(x, "feat", split_axis=0, concat_axis=0, tiled=True)

    def over_space(x):
        lanes = x.shape[1]
        moved = lax.all_to_all(
            x.reshape(spaces, capacity, lanes), "space", split_axis=0, concat_axis=0, tiled=True
        )
        return moved.reshape(slot_count, lanes)

    own, picked = call(
        first_kernel,
        (sds((2 * node_count, quarter), BF16), sds((slot_count, quarter), BF16)),
        node, agg_grad, send_rows,
        places=[ANY] * 3,
        scratch=[pltpu.VMEM(send_rows.shape, jnp.int32), pltpu.SemaphoreType.DMA((3,))],
        flops=2 * slot_count * node_count * quarter,
        limit=60 * 1024 * 1024,
    )
    arrived = over_space(picked)
    shared = lax.all_gather(own, "feat", axis=0, tiled=False)
    (spread,) = call(
        spread_kernel,
        (sds((feats, slot_count, quarter), BF16),),
        arrived, shared,
        places=[VMEM, ANY],
    )
    slot_rows = over_feat(spread)
    kept, given, slot_sums, hidden = call(
        middle_kernel,
        (
            sds((2 * width, quarter), F32),
            sds((2 * width, quarter), F32),
            sds((slot_count, quarter), BF16),
            sds((edges, quarter), BF16),
        ),
        core, shared, slot_rows, edge_feat, w_send, w_recv, w_edge, w_out, receivers, slots,
        places=[SMEM] + [VMEM] * 9,
        flops=2 * edges * width * (2 * node_count + 2 * slot_count + 8 * quarter),
    )
    taken = lax.ppermute(given, "space", [(i, i ^ 1) for i in range(spaces)])
    (payload,) = call(
        payload_kernel, (sds((slot_count, 3 * quarter), BF16),), kept, taken, slot_sums
    )
    payload, hidden = lax.optimization_barrier((payload, hidden))
    returned = over_space(payload)
    part = sds((edges, quarter), BF16)
    mine, *theirs, recv_sums = call(
        edge_kernel,
        (sds((edges, quarter), F32), *[part] * (feats - 1), sds((node_count, quarter), F32)),
        place, hidden, w_edge, receivers,
        places=[SMEM] + [VMEM] * 3,
        flops=2 * edges * quarter * (width + node_count),
    )
    theirs = [
        lax.ppermute(x, "feat", [(i, (i + step) % feats) for i in range(feats)])
        for step, x in enumerate(theirs, 1)
    ]
    small = sds((width // spaces, quarter), F32)
    parts, edge_grad, grad_send, grad_recv, grad_edge, grad_out = call(
        node_part_kernel,
        (
            sds((feats, node_count, quarter), BF16),
            sds((edges, quarter), F32),
            small, small, small, small,
        ),
        returned, send_rows, recv_sums, w_send, w_recv, mine, *theirs,
        flops=2 * node_count * quarter * (slot_count + 4 * width),
    )
    (node_grad,) = call(
        node_sum_kernel, (sds((node_count, quarter), F32),), over_feat(parts)
    )
    return (node_grad, edge_grad, grad_send, grad_recv, grad_edge, grad_out)


def solution(mesh):
    placed = (
        P("space", "feat"),
        P("space", None),
        P("space", "feat"),
        P(None, "feat"),
        P(None, "feat"),
        P(None, "feat"),
        P(None, "feat"),
        P("space"),
        P("space"),
        P("space", None),
    )
    return jax.shard_map(
        local,
        mesh=mesh,
        in_specs=placed,
        out_specs=(P("space", "feat"),) * 6,
        check_vma=False,
    )
```

time: 118 us -> 99.2 us (0.84)
  blocking collectives: 59.3 us -> 20.6 us
  starting transfers between devices: 14.8 us -> 48.3 us
  local copies, waits for them, and re-layouts: 15.1 us -> 2.26 us
  waiting for transfers between devices: 21 us -> 19.2 us
  Pallas kernels: 6.01 us -> 7.49 us
    all_to_all x1 -> x0, blocking collectives: 31 us -> none  [over_space(): lax.all_to_all(x.reshape(spaces, capacity, lanes), 'space', split_axis=0,...]
    all_to_all x1 -> x2, starting transfers between devices: 6.26 us -> 31.1 us  [over_space(): lax.all_to_all(x.reshape(spaces, capacity, lanes), 'space', split_axis=0,...]
    all_to_all x2 -> x1, blocking collectives: 28.3 us -> 8.78 us  [over_feat(): return lax.all_to_all(x, 'feat', split_axis=0, concat_axis=0, tiled=True)]
    unnamed x36 -> x18, local copies, waits for them, and re-layouts: 13.2 us -> 1.32 us
    all_gather x0 -> x1, blocking collectives: none -> 11.8 us  [local(): shared = lax.all_gather(own, 'feat', axis=0, tiled=False)]
    all_to_all x1 -> x2, waiting for transfers between devices: 19.4 us -> 10 us  [over_space(): lax.all_to_all(x.reshape(spaces, capacity, lanes), 'space', split_axis=0,...]
    ppermute x0 -> x3, starting transfers between devices: none -> 8.41 us  [local(): lax.ppermute(x, 'feat', [(i, (i + step) % feats) for i in range(feats)])]
    all_to_all x1, waiting for transfers between devices: 1.62 us -> 7.67 us  [over_feat(): return lax.all_to_all(x, 'feat', split_axis=0, concat_axis=0, tiled=True)]
  transfers between devices with their start and end apart: 3 -> 7, of which waited for: 2 -> 4; matrix products, arithmetic and copies ran while one was open for 0% -> 0% of each run, Pallas kernels for 2% -> 0%
where the time goes in v2:
time: 99.2 us; the launch traced here: 98.7 us
  starting transfers between devices  48.3 us (49%)
  blocking collectives  20.6 us (21%)
  waiting for transfers between devices  19.2 us (19%)
  Pallas kernels  7.49 us (8%)
  local copies, waits for them, and re-layouts  2.26 us (2%)
    all_to_all x2, starting transfers between devices, over_space(): lax.all_to_all(x.reshape(spaces, capacity, lanes), 'space', split_axis=0,...  31.1 us
    all_gather x1, blocking collectives, local(): shared = lax.all_gather(own, 'feat', axis=0, tiled=False)  11.8 us
    all_to_all x2, waiting for transfers between devices, over_space(): lax.all_to_all(x.reshape(spaces, capacity, lanes), 'space', split_axis=0,...  10 us
    all_to_all x1, blocking collectives, over_feat(): return lax.all_to_all(x, 'feat', split_axis=0, concat_axis=0, tiled=True)  8.78 us
    ppermute x3, starting transfers between devices, local(): lax.ppermute(x, 'feat', [(i, (i + step) % feats) for i in range(feats)])  8.41 us
    all_to_all x1, waiting for transfers between devices, over_feat(): return lax.all_to_all(x, 'feat', split_axis=0, concat_axis=0, tiled=True)  7.67 us
    pallas_call x7, Pallas kernels, call(): pl.pallas_call(kernel, out_shape=list(outs), in_specs=list(places or [VME...  7.49 us
    ppermute x1, starting transfers between devices, local(): taken = lax.ppermute(given, 'space', [(i, i ^ 1) for i in range(spaces)])  4.68 us
  transfers between devices with their start and end apart: 7, of which 4 were waited for; matrix products, arithmetic and copies ran while one was open for 0% of the time, Pallas kernels for 0%

profile of v2, /device:TPU:1, one launch (start us, length us, event | category | flops | bytes accessed | tf_op | source)
XLA Modules:
  0.0 98.7 jit_solution(7677523893095175059)
XLA Ops:
  0.6 1.8 %shard_map.145 = (bf16[512,128]{1,0:T(8,128)(2,1)}, bf16[512,128]{1,0:T(8,128)(2,1)}) custom-call(bf16[256,128]{1,0:T(8,128)(2,1)} %node.1, bf16[256,128]{1,0:T(8,128)(2,1)} %agg.1, s32[1,512]{1,0:T(1,128)} %rows.3), custom_call_target="tpu_custom_call" | custom-call | flops 33554432 | bytes 395264 | tf_op jit(solution)/shard_map/pallas_call | solution.py:173
  2.5 18.6 %all-to-all-start = ((bf16[128,4,128]{2,1,0:T(4,128)(2,1)}), bf16[128,4,128]{2,1,0:T(4,128)(2,1)S(1)}, u32[]{:S(2)}, u32[]{:S(2)}) async-start(bf16[128,4,128]{2,1,0:T(4,128)(2,1)} %bitcast.13), calls=%async_computation | async-start | bytes 262144 | tf_op jit(solution)/shard_map/all_to_all | solution.py:204
  21.0 11.8 %all-gather = bf16[2048,128]{1,0:T(8,128)(2,1)S(1)} all-gather(bf16[512,128]{1,0:T(8,128)(2,1)S(1)} %copy-done.8), channel_id=2, replica_groups=mesh['space'=128,'feat'=4] {'feat'}, dimensions={0}, use_global_device_ids=true | all-gather | bytes 655360 | tf_op jit(solution)/shard_map/all_gather | solution.py:219
  32.8 0.9 all-to-all-done
  33.8 0.9 shard_map.146
  34.7 4.2 %all-to-all-start.1 = ((bf16[4,512,128]{2,1,0:T(8,128)(2,1)}), bf16[4,512,128]{2,1,0:T(8,128)(2,1)S(1)}, u32[]{:S(2)}, u32[]{:S(2)}) async-start(bf16[4,512,128]{2,1,0:T(8,128)(2,1)} %shard_map.146), calls=%async_computation.1 | async-start | bytes 1048576 | tf_op jit(solution)/shard_map/all_to_all | solution.py:200
  38.8 7.7 %all-to-all-done.1.slot_rows = bf16[4,512,128]{2,1,0:T(8,128)(2,1)S(1)} async-done(((bf16[4,512,128]{2,1,0:T(8,128)(2,1)}), bf16[4,512,128]{2,1,0:T(8,128)(2,1)S(1)}, u32[]{:S(2)}, u32[]{:S(2)}) %all-to-all-start.1) | async-done | bytes 524320 | tf_op jit(solution)/shard_map/all_to_all | solution.py:200
  46.5 0.6 copy-done.6
  47.2 2.4 %shard_map.147 = (f32[1024,128]{1,0:T(8,128)S(1)}, f32[1024,128]{1,0:T(8,128)S(1)}, bf16[512,128]{1,0:T(8,128)(2,1)S(1)}, bf16[512,128]{1,0:T(8,128)(2,1)S(1)}) custom-call(s32[1]{0:T(128)} %bitcast.core, bf16[4,512,128]{2,1,0:T(8,128)(2,1)S(1)} %bitcast.8, bf16[4,512,128]{2,1,0:T(8,128)(2,1)S(1)} %all-to-all-done.1.slot_rows, ...), custom_call_target="tpu_custom_call" | custom-call | flops 1342177280 | bytes 3411972 | tf_op jit(solution)/shard_map/pallas_call | solution.py:173
  49.6 4.7 %collective-permute-start = (f32[1024,128]{1,0:T(8,128)S(1)}, f32[1024,128]{1,0:T(8,128)S(1)}, u32[]{:S(2)}, u32[]{:S(2)}) collective-permute-start(f32[1024,128]{1,0:T(8,128)S(1)} %get-tuple-element.28), channel_id=1, source_target_pairs={{0,4},{4,0},{8,12},{12,8},{16,20},{20,16},{24,28},{28,24},{32,36},... | collective-permute-start | bytes 1572872 | tf_op jit(solution)/shard_map/ppermute | solution.py:239
  54.2 1.5 %collective-permute-done.taken = f32[1024,128]{1,0:T(8,128)S(1)} collective-permute-done((f32[1024,128]{1,0:T(8,128)S(1)}, f32[1024,128]{1,0:T(8,128)S(1)}, u32[]{:S(2)}, u32[]{:S(2)}) %collective-permute-start) | collective-permute-done | bytes 524320 | tf_op jit(solution)/shard_map/ppermute | solution.py:239
  55.8 0.1 shard_map.148
  55.9 0.8 reshape.41
  56.7 12.5 %all-to-all-start.2 = ((bf16[128,4,384]{2,1,0:T(4,128)(2,1)}), bf16[128,4,384]{2,1,0:T(4,128)(2,1)S(1)}, u32[]{:S(2)}, u32[]{:S(2)}) async-start(bf16[128,4,384]{2,1,0:T(4,128)(2,1)} %reshape.41), calls=%async_computation.2 | async-start | bytes 786432 | tf_op jit(solution)/shard_map/all_to_all | solution.py:204
  69.2 0.4 shard_map.149
  69.6 2.2 %collective-permute-start.1 = (bf16[512,128]{1,0:T(8,128)(2,1)S(1)}, bf16[512,128]{1,0:T(8,128)(2,1)S(1)}, u32[]{:S(2)}, u32[]{:S(2)}) collective-permute-start(bf16[512,128]{1,0:T(8,128)(2,1)S(1)} %get-tuple-element.35), channel_id=1, source_target_pairs={{0,1},{1,2},{2,3},{3,0},{4,5},{5,6},{6,7},{7,4},{8,9},{9,10},{10,1... | collective-permute-start | bytes 393224 | tf_op jit(solution)/shard_map/ppermute | solution.py:254
  71.8 3.7 %collective-permute-start.2 = (bf16[512,128]{1,0:T(8,128)(2,1)S(1)}, bf16[512,128]{1,0:T(8,128)(2,1)S(1)}, u32[]{:S(2)}, u32[]{:S(2)}) collective-permute-start(bf16[512,128]{1,0:T(8,128)(2,1)S(1)} %get-tuple-element.36), channel_id=1, source_target_pairs={{0,2},{1,3},{2,0},{3,1},{4,6},{5,7},{6,4},{7,5},{8,10},{9,11},{10,... | collective-permute-start | bytes 393224 | tf_op jit(solution)/shard_map/ppermute | solution.py:254
  75.5 2.5 %collective-permute-start.3 = (bf16[512,128]{1,0:T(8,128)(2,1)S(1)}, bf16[512,128]{1,0:T(8,128)(2,1)S(1)}, u32[]{:S(2)}, u32[]{:S(2)}) collective-permute-start(bf16[512,128]{1,0:T(8,128)(2,1)S(1)} %get-tuple-element.37), channel_id=1, source_target_pairs={{0,3},{1,0},{2,1},{3,2},{4,7},{5,4},{6,5},{7,6},{8,11},{9,8},{10,9... | collective-permute-start | bytes 393224 | tf_op jit(solution)/shard_map/ppermute | solution.py:254
  78.1 9.1 %all-to-all-done.2 = bf16[128,4,384]{2,1,0:T(4,128)(2,1)S(1)} async-done(((bf16[128,4,384]{2,1,0:T(4,128)(2,1)}), bf16[128,4,384]{2,1,0:T(4,128)(2,1)S(1)}, u32[]{:S(2)}, u32[]{:S(2)}) %all-to-all-start.2) | async-done | bytes 393248 | tf_op jit(solution)/shard_map/all_to_all | solution.py:204
  87.1 0.1 reshape.42.arrived
  87.3 0.6 copy-done.2
  87.9 1.3 %shard_map.150 = (bf16[4,256,128]{2,1,0:T(8,128)(2,1)S(1)}, f32[512,128]{1,0:T(8,128)}, f32[4,128]{1,0:T(4,128)}, f32[4,128]{1,0:T(4,128)}, f32[4,128]{1,0:T(4,128)}, /*index=5*/f32[4,128]{1,0:T(4,128)}) custom-call(bf16[512,384]{1,0:T(8,128)(2,1)S(1)} %reshape.42.arrived, s32[1,512]{1,0:T(1,128)S(1)} %copy-done.2, ...), custom_call_target="tpu_custom_call" | custom-call | flops 167772160 | bytes 1976320 | tf_op jit(solution)/shard_map/pallas_call | solution.py:173
  89.2 8.8 %all_to_all.20.parts = bf16[4,256,128]{2,1,0:T(8,128)(2,1)S(1)} all-to-all(bf16[4,256,128]{2,1,0:T(8,128)(2,1)S(1)} %get-tuple-element.38), channel_id=1, replica_groups=mesh['space'=128,'feat'=4] {'feat'}, dimensions={0} | all-to-all | bytes 524288 | tf_op jit(solution)/shard_map/all_to_all | solution.py:200
  98.0 0.7 shard_map.151
  (19 shorter events, 0.0 us)
Async XLA Ops:
  2.5 18.6 %copy-start.8 = (bf16[512,128]{1,0:T(8,128)(2,1)S(1)}, bf16[512,128]{1,0:T(8,128)(2,1)}, u32[]{:S(2)}) copy-start(bf16[512,128]{1,0:T(8,128)(2,1)} %get-tuple-element.25) | copy-start | bytes 393220
  2.5 31.3 %all-to-all-start = ((bf16[128,4,128]{2,1,0:T(4,128)(2,1)}), bf16[128,4,128]{2,1,0:T(4,128)(2,1)S(1)}, u32[]{:S(2)}, u32[]{:S(2)}) async-start(bf16[128,4,128]{2,1,0:T(4,128)(2,1)} %bitcast.13), calls=%async_computation | async-start | bytes 262144 | tf_op jit(solution)/shard_map/all_to_all | solution.py:204
  34.6 11.9 %copy-start = (bf16[512,128]{1,0:T(8,128)(2,1)S(1)}, bf16[512,128]{1,0:T(8,128)(2,1)}, u32[]{:S(2)}) copy-start(bf16[512,128]{1,0:T(8,128)(2,1)} %w_send.3) | copy-start | bytes 393220
  34.6 11.9 %copy-start.1 = (bf16[512,128]{1,0:T(8,128)(2,1)S(1)}, bf16[512,128]{1,0:T(8,128)(2,1)}, u32[]{:S(2)}) copy-start(bf16[512,128]{1,0:T(8,128)(2,1)} %w_recv.3) | copy-start | bytes 393220
  34.6 11.9 %copy-start.3 = (bf16[512,512]{1,0:T(8,128)(2,1)S(1)}, bf16[512,512]{1,0:T(8,128)(2,1)}, u32[]{:S(2)}) copy-start(bf16[512,512]{1,0:T(8,128)(2,1)} %edge_feat.1) | copy-start | bytes 1572868
  34.6 11.9 %copy-start.4 = (bf16[512,128]{1,0:T(8,128)(2,1)S(1)}, bf16[512,128]{1,0:T(8,128)(2,1)}, u32[]{:S(2)}) copy-start(bf16[512,128]{1,0:T(8,128)(2,1)} %w_out.1) | copy-start | bytes 393220
  34.7 11.9 %copy-start.5 = (bf16[512,128]{1,0:T(8,128)(2,1)S(1)}, bf16[512,128]{1,0:T(8,128)(2,1)}, u32[]{:S(2)}) copy-start(bf16[512,128]{1,0:T(8,128)(2,1)} %w_edge.3) | copy-start | bytes 393220
  34.7 11.9 %copy-start.7 = (s32[512]{0:T(512)S(1)}, s32[512]{0:T(512)}, u32[]{:S(2)}) copy-start(s32[512]{0:T(512)} %param.17) | copy-start | bytes 6148
  34.7 11.8 %all-to-all-start.1 = ((bf16[4,512,128]{2,1,0:T(8,128)(2,1)}), bf16[4,512,128]{2,1,0:T(8,128)(2,1)S(1)}, u32[]{:S(2)}, u32[]{:S(2)}) async-start(bf16[4,512,128]{2,1,0:T(8,128)(2,1)} %shard_map.146), calls=%async_computation.1 | async-start | bytes 1048576 | tf_op jit(solution)/shard_map/all_to_all | solution.py:200
  46.5 0.7 copy-start.6
  49.6 6.2 %collective-permute-start = (f32[1024,128]{1,0:T(8,128)S(1)}, f32[1024,128]{1,0:T(8,128)S(1)}, u32[]{:S(2)}, u32[]{:S(2)}) collective-permute-start(f32[1024,128]{1,0:T(8,128)S(1)} %get-tuple-element.28), channel_id=1, source_target_pairs={{0,4},{4,0},{8,12},{12,8},{16,20},{20,16},{24,28},{28,24},{32,36},... | collective-permute-start | bytes 1572872 | tf_op jit(solution)/shard_map/ppermute | solution.py:239
  56.7 30.4 %all-to-all-start.2 = ((bf16[128,4,384]{2,1,0:T(4,128)(2,1)}), bf16[128,4,384]{2,1,0:T(4,128)(2,1)S(1)}, u32[]{:S(2)}, u32[]{:S(2)}) async-start(bf16[128,4,384]{2,1,0:T(4,128)(2,1)} %reshape.41), calls=%async_computation.2 | async-start | bytes 786432 | tf_op jit(solution)/shard_map/all_to_all | solution.py:204
  69.6 17.6 %collective-permute-start.1 = (bf16[512,128]{1,0:T(8,128)(2,1)S(1)}, bf16[512,128]{1,0:T(8,128)(2,1)S(1)}, u32[]{:S(2)}, u32[]{:S(2)}) collective-permute-start(bf16[512,128]{1,0:T(8,128)(2,1)S(1)} %get-tuple-element.35), channel_id=1, source_target_pairs={{0,1},{1,2},{2,3},{3,0},{4,5},{5,6},{6,7},{7,4},{8,9},{9,10},{10,1... | collective-permute-start | bytes 393224 | tf_op jit(solution)/shard_map/ppermute | solution.py:254
  71.8 15.4 %collective-permute-start.2 = (bf16[512,128]{1,0:T(8,128)(2,1)S(1)}, bf16[512,128]{1,0:T(8,128)(2,1)S(1)}, u32[]{:S(2)}, u32[]{:S(2)}) collective-permute-start(bf16[512,128]{1,0:T(8,128)(2,1)S(1)} %get-tuple-element.36), channel_id=1, source_target_pairs={{0,2},{1,3},{2,0},{3,1},{4,6},{5,7},{6,4},{7,5},{8,10},{9,11},{10,... | collective-permute-start | bytes 393224 | tf_op jit(solution)/shard_map/ppermute | solution.py:254
  75.5 11.7 %collective-permute-start.3 = (bf16[512,128]{1,0:T(8,128)(2,1)S(1)}, bf16[512,128]{1,0:T(8,128)(2,1)S(1)}, u32[]{:S(2)}, u32[]{:S(2)}) collective-permute-start(bf16[512,128]{1,0:T(8,128)(2,1)S(1)} %get-tuple-element.37), channel_id=1, source_target_pairs={{0,3},{1,0},{2,1},{3,2},{4,7},{5,4},{6,5},{7,6},{8,11},{9,8},{10,9... | collective-permute-start | bytes 393224 | tf_op jit(solution)/shard_map/ppermute | solution.py:254
  87.2 0.7 copy-start.2

commit v3 on v2

v3 whole, which is shorter than its diff:
```python
import jax
import jax.numpy as jnp
from jax import lax
from jax.experimental import pallas as pl
from jax.experimental.pallas import tpu as pltpu
from jax.sharding import PartitionSpec as P

F32 = jnp.float32
BF16 = jnp.bfloat16
LANES = 128


def mm(a, b):
    return jnp.dot(a, b, preferred_element_type=F32)


def mm_nt(a, b):
    return lax.dot_general(a, b, (((1,), (1,)), ((), ())), preferred_element_type=F32)


def mm_tn(a, b):
    return lax.dot_general(a, b, (((0,), (0,)), ((), ())), preferred_element_type=F32)


def hot(mask):
    return jnp.where(mask, 1.0, 0.0).astype(BF16)


def hot_by_column(row, rows):
    shape = (rows, row.shape[1])
    return hot(lax.broadcasted_iota(jnp.int32, shape, 0) == row)


def hot_by_row(row, columns):
    count = row.shape[1]
    column = jnp.broadcast_to(row, (LANES, count)).T
    lane = lax.broadcasted_iota(jnp.int32, (count, LANES), 1)
    parts = [hot(column == lane + start) for start in range(0, columns, LANES)]
    return jnp.concatenate(parts, axis=1)


def fetch(sems, *pairs):
    copies = [pltpu.make_async_copy(src, dst, sems.at[i]) for i, (src, dst) in enumerate(pairs)]
    for copy in copies:
        copy.start()
    return copies


def join(ref, start, size):
    return jnp.concatenate([ref[q, start : start + size, :] for q in range(ref.shape[0])], axis=1)


def split_high_low(x):
    high = x.astype(BF16)
    return high, (x - high.astype(F32)).astype(BF16)


def first_kernel(node, rows, picked, node_here, rows_here, sems):
    copies = fetch(sems, (rows, rows_here), (node, node_here))
    copies[0].wait()
    pick = hot_by_row(rows_here[...], node.shape[0])
    copies[1].wait()
    picked[...] = mm(pick, node_here[...]).astype(BF16)


def spread_kernel(slot_rows, node, agg, spread):
    slots, count = slot_rows.shape[0], node.shape[0]
    for q in range(spread.shape[0]):
        spread[q, 0:slots, :] = slot_rows[...]
        spread[q, slots : slots + count, :] = node[...]
        spread[q, slots + count :, :] = agg[...]


def hidden_kernel(
    shared, edge_feat, w_send, w_recv, w_edge, w_out, receivers, slots, rows, spread
):
    edges, width = edge_feat.shape
    quarter = w_send.shape[1]
    slot_count = edges
    count = (shared.shape[1] - slot_count) // 2
    receive = hot_by_row(receivers[...], count)
    receiver_rows = mm(receive, join(shared, slot_count, count)).astype(BF16)
    message_grad = mm(receive, join(shared, slot_count + count, count)).astype(BF16)
    slot_hot = hot_by_row(slots[...], slot_count)
    sender_rows = mm(slot_hot, join(shared, 0, slot_count)).astype(BF16)
    rows[:, 0:width] = sender_rows
    rows[:, width : 2 * width] = receiver_rows
    rows[:, 2 * width : 3 * width] = message_grad
    act_grad = mm(message_grad, w_out[...])
    pre_act = (
        mm(sender_rows, w_send[...])
        + mm(receiver_rows, w_recv[...])
        + mm(edge_feat[...], w_edge[...])
    )
    gate = jax.nn.sigmoid(pre_act)
    rows[:, 3 * width :] = (pre_act * gate).astype(BF16)
    grad = (act_grad * gate * (1.0 + pre_act * (1.0 - gate))).astype(BF16)
    for q in range(spread.shape[0]):
        spread[q, 0:edges, :] = grad
        block = slice(q * quarter, (q + 1) * quarter)
        for i, weight in enumerate((w_send, w_recv, w_edge)):
            start = edges + i * quarter
            spread[q, start : start + quarter, :] = weight[block, :]


def weight_kernel(core, rows, edge_feat, spread, kept, given):
    edges, size = edge_feat.shape
    sender_rows, receiver_rows, message_grad = (
        rows[:, i * size : (i + 1) * size] for i in range(3)
    )
    grad = spread[0, 0:edges, :]
    mine = core[0] == 0
    for i, (low, high, high_right) in enumerate(
        (
            (sender_rows, edge_feat[...], grad),
            (receiver_rows, message_grad, rows[:, 3 * size :]),
        )
    ):
        low_sum = mm_tn(low, grad)
        high_sum = mm_tn(high, high_right)
        kept[i * size : (i + 1) * size, :] = jnp.where(mine, low_sum, high_sum)
        given[i * size : (i + 1) * size, :] = jnp.where(mine, high_sum, low_sum)


def payload_kernel(hidden, slots, kept, taken, payload):
    size = kept.shape[0] // 2
    quarter = kept.shape[1]
    edges = slots.shape[1]
    w_send = join(hidden, edges, quarter)
    sums = mm(hot_by_column(slots[...], payload.shape[0]), join(hidden, 0, edges))
    high, low = split_high_low(sums)
    payload[:, 0:quarter] = (kept[0:size, :] + taken[0:size, :]).astype(BF16)
    payload[:, quarter : 2 * quarter] = (kept[size:, :] + taken[size:, :]).astype(BF16)
    payload[:, 2 * quarter :] = (mm_nt(high, w_send) + mm_nt(low, w_send)).astype(BF16)


def edge_kernel(hidden, receivers, rows, edge_grad, recv_part, owner_hot):
    edges, quarter = edge_grad.shape
    full = join(hidden, 0, edges)
    edge_grad[...] = mm_nt(full, join(hidden, edges + 2 * quarter, quarter))
    sums = mm(hot_by_column(receivers[...], recv_part.shape[0]), full)
    high, low = split_high_low(sums)
    w_recv = join(hidden, edges + quarter, quarter)
    recv_part[...] = mm_nt(high, w_recv) + mm_nt(low, w_recv)
    owner_hot[...] = hot_by_column(rows[...], owner_hot.shape[0])


def last_kernel(
    arrived, owner_hot, recv_part, node_grad, grad_send, grad_recv, grad_edge, grad_out
):
    quarter = node_grad.shape[1]
    back = mm(owner_hot[...], arrived[:, 2 * quarter : 3 * quarter])
    node_grad[...] = recv_part[...] + back
    shape = (8, arrived.shape[0])
    place = lax.broadcasted_iota(jnp.int32, shape, 1) % 8
    pick = hot(place == lax.broadcasted_iota(jnp.int32, shape, 0))
    sums = mm(pick, arrived[:, 0 : 2 * quarter])
    grad_send[...] = sums[0:4, 0:quarter]
    grad_recv[...] = sums[0:4, quarter:]
    grad_edge[...] = sums[4:8, 0:quarter]
    grad_out[...] = sums[4:8, quarter:]


ANY = pl.BlockSpec(memory_space=pl.ANY)
VMEM = pl.BlockSpec(memory_space=pltpu.VMEM)
SMEM = pl.BlockSpec(memory_space=pltpu.SMEM)


def call(kernel, outs, *operands, places=None, scratch=(), flops=0, limit=24 * 1024 * 1024):
    moved = sum(x.size * x.dtype.itemsize for x in operands)
    moved += sum(x.size * x.dtype.itemsize for x in outs)
    return pl.pallas_call(
        kernel,
        out_shape=list(outs),
        in_specs=list(places or [VMEM] * len(operands)),
        out_specs=[VMEM] * len(outs),
        scratch_shapes=list(scratch),
        compiler_params=pltpu.CompilerParams(vmem_limit_bytes=limit),
        cost_estimate=pl.CostEstimate(flops=flops, bytes_accessed=moved, transcendentals=0),
    )(*operands)


def local(
    node, edge_feat, agg_grad, w_send, w_recv, w_edge, w_out, receivers, edge_slot, send_rows
):
    spaces = lax.axis_size("space")
    feats = lax.axis_size("feat")
    slot_count = send_rows.shape[1]
    capacity = slot_count // spaces
    node_count, quarter = node.shape
    edges, width = edge_feat.shape
    sds = jax.ShapeDtypeStruct
    receivers = receivers.reshape(1, edges)
    slots = edge_slot.reshape(1, edges)
    core = (lax.axis_index("space") % 2).reshape(1)

    def over_feat(x):
        return lax.all_to_all(x, "feat", split_axis=0, concat_axis=0, tiled=True)

    def over_space(x):
        lanes = x.shape[1]
        moved = lax.all_to_all(
            x.reshape(spaces, capacity, lanes), "space", split_axis=0, concat_axis=0, tiled=True
        )
        return moved.reshape(slot_count, lanes)

    (picked,) = call(
        first_kernel,
        (sds((slot_count, quarter), BF16),),
        node, send_rows,
        places=[ANY] * 2,
        scratch=[
            pltpu.VMEM(node.shape, BF16),
            pltpu.VMEM(send_rows.shape, jnp.int32),
            pltpu.SemaphoreType.DMA((2,)),
        ],
        flops=2 * slot_count * node_count * quarter,
        limit=60 * 1024 * 1024,
    )
    (spread,) = call(
        spread_kernel,
        (sds((feats, slot_count + 2 * node_count, quarter), BF16),),
        over_space(picked), node, agg_grad,
    )
    shared = over_feat(spread)
    rows, spread = call(
        hidden_kernel,
        (
            sds((edges, 3 * width + quarter), BF16),
            sds((feats, edges + 3 * quarter, quarter), BF16),
        ),
        shared, edge_feat, w_send, w_recv, w_edge, w_out, receivers, slots,
        flops=2 * edges * width * (2 * node_count + slot_count + 4 * quarter),
    )
    hidden = over_feat(spread)
    kept, given = call(
        weight_kernel,
        (sds((2 * width, quarter), F32), sds((2 * width, quarter), F32)),
        core, rows, edge_feat, spread,
        places=[SMEM] + [VMEM] * 3,
        flops=8 * edges * width * quarter,
    )
    taken = lax.ppermute(given, "space", [(i, i ^ 1) for i in range(spaces)])
    (payload,) = call(
        payload_kernel,
        (sds((slot_count, 3 * quarter), BF16),),
        hidden, slots, kept, taken,
        flops=2 * slot_count * width * (edges + 2 * quarter),
    )
    returned = over_space(payload)
    edge_grad, recv_part, owner_hot = call(
        edge_kernel,
        (
            sds((edges, quarter), F32),
            sds((node_count, quarter), F32),
            sds((node_count, slot_count), BF16),
        ),
        hidden, receivers, send_rows,
        flops=2 * edges * width * (node_count + 2 * quarter),
    )
    small = sds((width // spaces, quarter), F32)
    node_grad, grad_send, grad_recv, grad_edge, grad_out = call(
        last_kernel,
        (sds((node_count, quarter), F32), small, small, small, small),
        returned, owner_hot, recv_part,
        flops=2 * node_count * slot_count * quarter,
    )
    return (node_grad, edge_grad, grad_send, grad_recv, grad_edge, grad_out)


def solution(mesh):
    placed = (
        P("space", "feat"),
        P("space", None),
        P("space", "feat"),
        P(None, "feat"),
        P(None, "feat"),
        P(None, "feat"),
        P(None, "feat"),
        P("space"),
        P("space"),
        P("space", None),
    )
    return jax.shard_map(
        local,
        mesh=mesh,
        in_specs=placed,
        out_specs=(P("space", "feat"),) * 6,
        check_vma=False,
    )
```

time: 99.2 us -> 102 us (1.028)
  starting transfers between devices: 48.3 us -> 15.2 us
  blocking collectives: 20.6 us -> 49.3 us
  waiting for transfers between devices: 19.2 us -> 22.3 us
  local copies, waits for them, and re-layouts: 2.26 us -> 4.51 us
  Pallas kernels: 7.49 us -> 9.38 us
    all_to_all x0 -> x1, blocking collectives: none -> 31.2 us  [over_space(): lax.all_to_all(x.reshape(spaces, capacity, lanes), 'space', split_axis=0,...]
    all_to_all x2 -> x1, starting transfers between devices: 31.1 us -> 7.91 us  [over_space(): lax.all_to_all(x.reshape(spaces, capacity, lanes), 'space', split_axis=0,...]
    all_gather x1 -> x0, blocking collectives: 11.8 us -> none  [local(): shared = lax.all_gather(own, 'feat', axis=0, tiled=False)]
    all_to_all x1, blocking collectives: 8.78 us -> 18.2 us  [over_feat(): return lax.all_to_all(x, 'feat', split_axis=0, concat_axis=0, tiled=True)]
    ppermute x3 -> x0, starting transfers between devices: 8.41 us -> none  [local(): lax.ppermute(x, 'feat', [(i, (i + step) % feats) for i in range(feats)])]
    all_to_all x2 -> x1, waiting for transfers between devices: 10 us -> 17 us  [over_space(): lax.all_to_all(x.reshape(spaces, capacity, lanes), 'space', split_axis=0,...]
    all_to_all x1, waiting for transfers between devices: 7.67 us -> 3.79 us  [over_feat(): return lax.all_to_all(x, 'feat', split_axis=0, concat_axis=0, tiled=True)]
    unnamed x18 -> x24, local copies, waits for them, and re-layouts: 1.32 us -> 3.56 us
  transfers between devices with their start and end apart: 7 -> 3, of which waited for: 4 -> 3; matrix products, arithmetic and copies ran while one was open for 0% -> 0% of each run, Pallas kernels for 0% -> 3%
where the time goes in v3:
time: 102 us; the launch traced here: 101 us
  blocking collectives  49.3 us (48%)
  waiting for transfers between devices  22.3 us (22%)
  starting transfers between devices  15.2 us (15%)
  Pallas kernels  9.38 us (9%)
  local copies, waits for them, and re-layouts  4.51 us (4%)
    all_to_all x1, blocking collectives, over_space(): lax.all_to_all(x.reshape(spaces, capacity, lanes), 'space', split_axis=0,...  31.2 us
    all_to_all x1, blocking collectives, over_feat(): return lax.all_to_all(x, 'feat', split_axis=0, concat_axis=0, tiled=True)  18.2 us
    all_to_all x1, waiting for transfers between devices, over_space(): lax.all_to_all(x.reshape(spaces, capacity, lanes), 'space', split_axis=0,...  17 us
    pallas_call x7, Pallas kernels, call(): pl.pallas_call(kernel, out_shape=list(outs), in_specs=list(places or [VME...  9.38 us
    all_to_all x1, starting transfers between devices, over_space(): lax.all_to_all(x.reshape(spaces, capacity, lanes), 'space', split_axis=0,...  7.91 us
    all_to_all x1, waiting for transfers between devices, over_feat(): return lax.all_to_all(x, 'feat', split_axis=0, concat_axis=0, tiled=True)  3.79 us
    ppermute x1, starting transfers between devices, local(): taken = lax.ppermute(given, 'space', [(i, i ^ 1) for i in range(spaces)])  3.73 us
    unnamed x24, local copies, waits for them, and re-layouts  3.56 us
  transfers between devices with their start and end apart: 3, of which 3 were waited for; matrix products, arithmetic and copies ran while one was open for 0% of the time, Pallas kernels for 3%

profile of v3, /device:TPU:1, one launch (start us, length us, event | category | flops | bytes accessed | tf_op | source)
XLA Modules:
  0.0 101.4 jit_solution(17553695405978789390)
XLA Ops:
  0.6 1.8 %shard_map.145 = bf16[512,128]{1,0:T(8,128)(2,1)} custom-call(bf16[256,128]{1,0:T(8,128)(2,1)} %node.3, s32[1,512]{1,0:T(1,128)} %rows.3), custom_call_target="tpu_custom_call" | custom-call | flops 33554432 | bytes 198656 | tf_op jit(solution)/shard_map/pallas_call | solution.py:172
  2.4 31.2 %all_to_all.20 = bf16[128,4,128]{2,1,0:T(4,128)(2,1)S(1)} all-to-all(bf16[128,4,128]{2,1,0:T(4,128)(2,1)} %bitcast.10), channel_id=1, replica_groups=mesh['space'=128,'feat'=4] {'space'}, dimensions={0} | all-to-all | bytes 262144 | tf_op jit(solution)/shard_map/all_to_all | solution.py:202
  33.6 0.8 copy-done.3
  34.4 0.8 copy-done.4
  35.2 0.0 copy-start.9
  35.3 0.0 copy-start.10
  35.3 0.0 copy-start.11
  35.3 0.1 shard_map.146
  35.4 18.2 %all_to_all.21.shared = bf16[4,1024,128]{2,1,0:T(8,128)(2,1)S(1)} all-to-all(bf16[4,1024,128]{2,1,0:T(8,128)(2,1)S(1)} %shard_map.146), channel_id=1, replica_groups=mesh['space'=128,'feat'=4] {'feat'}, dimensions={0} | all-to-all | bytes 2097152 | tf_op jit(solution)/shard_map/all_to_all | solution.py:198
  53.6 2.5 %shard_map.147 = (bf16[512,1664]{1,0:T(8,128)(2,1)S(1)}, bf16[4,896,128]{2,1,0:T(8,128)(2,1)}) custom-call(bf16[4,1024,128]{2,1,0:T(8,128)(2,1)S(1)} %all_to_all.21.shared, bf16[512,512]{1,0:T(8,128)(2,1)S(1)} %copy-done, bf16[512,128]{1,0:T(8,128)(2,1)S(1)} %copy-done.7, bf16[512,128]{1,0:T(8,128)(2,1)S(1)} %copy-done.8, bf16[512,128]{1,0:T(8,128)(2,1)S(1)} %copy-done.9, ...), custom_call_target="tpu_custom_call" | custom-call | flops 805306368 | bytes 4722688 | tf_op jit(solution)/shard_map/pallas_call | solution.py:172
  56.1 3.5 %all-to-all-start.2 = ((bf16[4,896,128]{2,1,0:T(8,128)(2,1)}), bf16[4,896,128]{2,1,0:T(8,128)(2,1)S(1)}, u32[]{:S(2)}, u32[]{:S(2)}) async-start(bf16[4,896,128]{2,1,0:T(8,128)(2,1)} %get-tuple-element.18.spread), calls=%async_computation.2 | async-start | bytes 1835008 | tf_op jit(solution)/shard_map/all_to_all | solution.py:198
  59.7 2.0 %shard_map.148 = (f32[1024,128]{1,0:T(8,128)S(1)}, f32[1024,128]{1,0:T(8,128)S(1)}) custom-call(s32[1]{0:T(128)} %bitcast.4.core, bf16[512,1664]{1,0:T(8,128)(2,1)S(1)} %get-tuple-element.19.rows, bf16[512,512]{1,0:T(8,128)(2,1)S(1)} %copy-done, bf16[4,896,128]{2,1,0:T(8,128)(2,1)} %get-tuple-element.18.spread), custom_call_target="tpu_custom_call" | custom-call | flops 268435456 | bytes 4194308 | tf_op jit(solution)/shard_map/pallas_call | solution.py:172
  61.6 0.8 copy-done.1
  62.4 3.7 %collective-permute-start = (f32[1024,128]{1,0:T(8,128)S(1)}, f32[1024,128]{1,0:T(8,128)S(1)}, u32[]{:S(2)}, u32[]{:S(2)}) collective-permute-start(f32[1024,128]{1,0:T(8,128)S(1)} %get-tuple-element.21), channel_id=1, source_target_pairs={{0,4},{4,0},{8,12},{12,8},{16,20},{20,16},{24,28},{28,24},{32,36},... | collective-permute-start | bytes 1572872 | tf_op jit(solution)/shard_map/ppermute | solution.py:243
  66.2 1.5 %collective-permute-done.taken = f32[1024,128]{1,0:T(8,128)S(1)} collective-permute-done((f32[1024,128]{1,0:T(8,128)S(1)}, f32[1024,128]{1,0:T(8,128)S(1)}, u32[]{:S(2)}, u32[]{:S(2)}) %collective-permute-start) | collective-permute-done | bytes 524320 | tf_op jit(solution)/shard_map/ppermute | solution.py:243
  67.7 3.8 %all-to-all-done.2.hidden = bf16[4,896,128]{2,1,0:T(8,128)(2,1)S(1)} async-done(((bf16[4,896,128]{2,1,0:T(8,128)(2,1)}), bf16[4,896,128]{2,1,0:T(8,128)(2,1)S(1)}, u32[]{:S(2)}, u32[]{:S(2)}) %all-to-all-start.2) | async-done | bytes 917536 | tf_op jit(solution)/shard_map/all_to_all | solution.py:198
  71.5 1.0 %copy-done.2 = f32[1024,128]{1,0:T(8,128)S(1)} copy-done((f32[1024,128]{1,0:T(8,128)S(1)}, f32[1024,128]{1,0:T(8,128)}, u32[]{:S(2)}) %copy-start.2) | copy-done | bytes 524312
  72.5 1.1 %shard_map.149 = bf16[512,384]{1,0:T(8,128)(2,1)S(1)} custom-call(bf16[4,896,128]{2,1,0:T(8,128)(2,1)S(1)} %all-to-all-done.2.hidden, s32[1,512]{1,0:T(1,128)S(1)} %bitcast.7, f32[1024,128]{1,0:T(8,128)S(1)} %copy-done.2, f32[1024,128]{1,0:T(8,128)S(1)} %collective-permute-done.taken), custom_call_target="tpu_custom_call" | custom-call | flops 402653184 | bytes 2361344 | tf_op jit(solution)/shard_map/pallas_call | solution.py:172
  73.7 0.9 reshape.38
  74.5 7.9 %all-to-all-start.3 = ((bf16[128,4,384]{2,1,0:T(4,128)(2,1)}), bf16[128,4,384]{2,1,0:T(4,128)(2,1)S(1)}, u32[]{:S(2)}, u32[]{:S(2)}) async-start(bf16[128,4,384]{2,1,0:T(4,128)(2,1)} %reshape.38), calls=%async_computation.3 | async-start | bytes 786432 | tf_op jit(solution)/shard_map/all_to_all | solution.py:202
  82.5 1.0 shard_map.150
  83.5 17.0 %all-to-all-done.3 = bf16[128,4,384]{2,1,0:T(4,128)(2,1)S(1)} async-done(((bf16[128,4,384]{2,1,0:T(4,128)(2,1)}), bf16[128,4,384]{2,1,0:T(4,128)(2,1)S(1)}, u32[]{:S(2)}, u32[]{:S(2)}) %all-to-all-start.3) | async-done | bytes 393248 | tf_op jit(solution)/shard_map/all_to_all | solution.py:202
  100.5 0.1 reshape.39.arrived
  100.6 0.9 shard_map.151
  (17 shorter events, 0.0 us)
Async XLA Ops:
  33.6 0.8 copy-start.3
  34.4 0.8 copy-start.4
  35.2 18.4 %copy-start = (bf16[512,512]{1,0:T(8,128)(2,1)S(1)}, bf16[512,512]{1,0:T(8,128)(2,1)}, u32[]{:S(2)}) copy-start(bf16[512,512]{1,0:T(8,128)(2,1)} %edge_feat.3) | copy-start | bytes 1572868
  35.2 18.4 %copy-start.6 = (s32[512]{0:T(512)S(1)}, s32[512]{0:T(512)}, u32[]{:S(2)}) copy-start(s32[512]{0:T(512)} %param.18) | copy-start | bytes 6148
  35.2 18.4 %copy-start.7 = (bf16[512,128]{1,0:T(8,128)(2,1)S(1)}, bf16[512,128]{1,0:T(8,128)(2,1)}, u32[]{:S(2)}) copy-start(bf16[512,128]{1,0:T(8,128)(2,1)} %w_send.1) | copy-start | bytes 393220
  35.2 18.4 %copy-start.8 = (bf16[512,128]{1,0:T(8,128)(2,1)S(1)}, bf16[512,128]{1,0:T(8,128)(2,1)}, u32[]{:S(2)}) copy-start(bf16[512,128]{1,0:T(8,128)(2,1)} %w_recv.1) | copy-start | bytes 393220
  35.2 18.4 %copy-start.9 = (bf16[512,128]{1,0:T(8,128)(2,1)S(1)}, bf16[512,128]{1,0:T(8,128)(2,1)}, u32[]{:S(2)}) copy-start(bf16[512,128]{1,0:T(8,128)(2,1)} %w_edge.1) | copy-start | bytes 393220
  35.3 18.4 %copy-start.10 = (bf16[512,128]{1,0:T(8,128)(2,1)S(1)}, bf16[512,128]{1,0:T(8,128)(2,1)}, u32[]{:S(2)}) copy-start(bf16[512,128]{1,0:T(8,128)(2,1)} %w_out.1) | copy-start | bytes 393220
  35.3 18.4 %copy-start.11 = (s32[512]{0:T(512)S(1)}, s32[512]{0:T(512)}, u32[]{:S(2)}) copy-start(s32[512]{0:T(512)} %param.17) | copy-start | bytes 6148
  56.1 15.4 %all-to-all-start.2 = ((bf16[4,896,128]{2,1,0:T(8,128)(2,1)}), bf16[4,896,128]{2,1,0:T(8,128)(2,1)S(1)}, u32[]{:S(2)}, u32[]{:S(2)}) async-start(bf16[4,896,128]{2,1,0:T(8,128)(2,1)} %get-tuple-element.18.spread), calls=%async_computation.2 | async-start | bytes 1835008 | tf_op jit(solution)/shard_map/all_to_all | solution.py:198
  61.6 0.8 copy-start.1
  62.4 5.3 %collective-permute-start = (f32[1024,128]{1,0:T(8,128)S(1)}, f32[1024,128]{1,0:T(8,128)S(1)}, u32[]{:S(2)}, u32[]{:S(2)}) collective-permute-start(f32[1024,128]{1,0:T(8,128)S(1)} %get-tuple-element.21), channel_id=1, source_target_pairs={{0,4},{4,0},{8,12},{12,8},{16,20},{20,16},{24,28},{28,24},{32,36},... | collective-permute-start | bytes 1572872 | tf_op jit(solution)/shard_map/ppermute | solution.py:243
  71.5 1.0 %copy-start.2 = (f32[1024,128]{1,0:T(8,128)S(1)}, f32[1024,128]{1,0:T(8,128)}, u32[]{:S(2)}) copy-start(f32[1024,128]{1,0:T(8,128)} %copy-done.1) | copy-start | bytes 1572868
  72.5 9.9 %copy-start.5 = (s32[1,512]{1,0:T(1,128)S(1)}, s32[1,512]{1,0:T(1,128)}, u32[]{:S(2)}) copy-start(s32[1,512]{1,0:T(1,128)} %rows.3) | copy-start | bytes 6148
  74.5 25.9 %all-to-all-start.3 = ((bf16[128,4,384]{2,1,0:T(4,128)(2,1)}), bf16[128,4,384]{2,1,0:T(4,128)(2,1)S(1)}, u32[]{:S(2)}, u32[]{:S(2)}) async-start(bf16[128,4,384]{2,1,0:T(4,128)(2,1)} %reshape.38), calls=%async_computation.3 | async-start | bytes 786432 | tf_op jit(solution)/shard_map/all_to_all | solution.py:202

commit v4 on v3

--- a/solution.py
+++ b/solution.py
@@ -8,6 +8,7 @@
 F32 = jnp.float32
 BF16 = jnp.bfloat16
 LANES = 128
+CAPACITY = 4
 
 
 def mm(a, b):
@@ -36,7 +37,7 @@
     column = jnp.broadcast_to(row, (LANES, count)).T
     lane = lax.broadcasted_iota(jnp.int32, (count, LANES), 1)
     parts = [hot(column == lane + start) for start in range(0, columns, LANES)]
-    return jnp.concatenate(parts, axis=1)
+    return jnp.concatenate(parts, axis=1)[:, 0:columns]
 
 
 def fetch(sems, *pairs):
@@ -53,6 +54,17 @@
 def split_high_low(x):
     high = x.astype(BF16)
     return high, (x - high.astype(F32)).astype(BF16)
+
+
+def pick_sum(hots, x):
+    lanes = x.shape[1]
+    both = mm(hots, jnp.concatenate(split_high_low(x), axis=1))
+    return both[:, 0:lanes] + both[:, lanes:]
+
+
+def high_low(product, a, x):
+    high, low = split_high_low(x)
+    return product(a, high) + product(a, low)
 
 
 def first_kernel(node, rows, picked, node_here, rows_here, sems):
@@ -63,37 +75,53 @@
     picked[...] = mm(pick, node_here[...]).astype(BF16)
 
 
-def spread_kernel(slot_rows, node, agg, spread):
-    slots, count = slot_rows.shape[0], node.shape[0]
-    for q in range(spread.shape[0]):
-        spread[q, 0:slots, :] = slot_rows[...]
-        spread[q, slots : slots + count, :] = node[...]
-        spread[q, slots + count :, :] = agg[...]
+def early_kernel(region, node, agg, receivers, slots, send_rows, own, indices):
+    count = node.shape[0]
+    own[0:count, :] = node[...]
+    own[count:, :] = agg[...]
+    slot = slots[...]
+    first = region[0] * CAPACITY
+    lane = lax.broadcasted_iota(jnp.int32, send_rows.shape, 1)
+    own_row = jnp.full(slot.shape, -1, jnp.int32)
+    for k in range(CAPACITY):
+        row = jnp.sum(jnp.where(lane == first + k, send_rows[...], 0), axis=1, keepdims=True)
+        own_row = jnp.where(slot == first + k, row, own_row)
+    other = jnp.where(slot >= first + CAPACITY, slot - CAPACITY, slot)
+    other = jnp.where(own_row >= 0, -1, other)
+    for i, values in enumerate((receivers[...], slot, other, own_row, send_rows[...])):
+        indices[i : i + 1, :] = values
+
+
+def pack_kernel(region, slot_rows, own, packed):
+    start = own.shape[0]
+    rest = packed.shape[0] - start
+    rows = slot_rows[...].astype(F32)
+    place = lax.broadcasted_iota(jnp.int32, (rest, rows.shape[1]), 0)
+    kept = jnp.where(place < region[0] * CAPACITY, rows[0:rest, :], rows[CAPACITY:, :])
+    packed[0:start, :] = own[...]
+    packed[start:, :] = kept.astype(BF16)
 
 
 def hidden_kernel(
-    shared, edge_feat, w_send, w_recv, w_edge, w_out, receivers, slots, rows, spread
+    shared, edge_feat, w_send, w_recv, w_edge, w_out, indices, activation, spread
 ):
-    edges, width = edge_feat.shape
-    quarter = w_send.shape[1]
-    slot_count = edges
+    edges, quarter = activation.shape
+    slot_count = edges - CAPACITY
     count = (shared.shape[1] - slot_count) // 2
-    receive = hot_by_row(receivers[...], count)
-    receiver_rows = mm(receive, join(shared, slot_count, count)).astype(BF16)
-    message_grad = mm(receive, join(shared, slot_count + count, count)).astype(BF16)
-    slot_hot = hot_by_row(slots[...], slot_count)
-    sender_rows = mm(slot_hot, join(shared, 0, slot_count)).astype(BF16)
-    rows[:, 0:width] = sender_rows
-    rows[:, width : 2 * width] = receiver_rows
-    rows[:, 2 * width : 3 * width] = message_grad
-    act_grad = mm(message_grad, w_out[...])
+    at_node = mm(join(shared, 0, count), jnp.concatenate([w_recv[...], w_send[...]], axis=1))
+    at_agg = mm(join(shared, count, count), w_out[...])
+    at_slot = mm(join(shared, 2 * count, slot_count), w_send[...])
+    receive = hot_by_row(indices[0:1, :], count)
+    at_edge = pick_sum(receive, jnp.concatenate([at_node[:, 0:quarter], at_agg], axis=1))
+    act_grad = at_edge[:, quarter:]
     pre_act = (
-        mm(sender_rows, w_send[...])
-        + mm(receiver_rows, w_recv[...])
+        pick_sum(hot_by_row(indices[2:3, :], slot_count), at_slot)
+        + pick_sum(hot_by_row(indices[3:4, :], count), at_node[:, quarter:])
+        + at_edge[:, 0:quarter]
         + mm(edge_feat[...], w_edge[...])
     )
     gate = jax.nn.sigmoid(pre_act)
-    rows[:, 3 * width :] = (pre_act * gate).astype(BF16)
+    activation[...] = (pre_act * gate).astype(BF16)
     grad = (act_grad * gate * (1.0 + pre_act * (1.0 - gate))).astype(BF16)
     for q in range(spread.shape[0]):
         spread[q, 0:edges, :] = grad
@@ -103,46 +131,58 @@
             spread[q, start : start + quarter, :] = weight[block, :]
 
 
-def weight_kernel(core, rows, edge_feat, spread, kept, given):
+def weight_kernel(core, shared, edge_feat, indices, activation, spread, kept, given):
     edges, size = edge_feat.shape
-    sender_rows, receiver_rows, message_grad = (
-        rows[:, i * size : (i + 1) * size] for i in range(3)
-    )
+    quarter = activation.shape[1]
+    slot_count = edges - CAPACITY
+    count = (shared.shape[1] - slot_count) // 2
     grad = spread[0, 0:edges, :]
+    receive = hot_by_column(indices[0:1, :], count)
+    by_slot = mm(hot_by_column(indices[2:3, :], slot_count), grad)
+    by_own = mm(hot_by_column(indices[3:4, :], count), grad)
+    by_node = mm(receive, grad)
+    by_agg = mm(receive, activation[...])
+    node_grads = high_low(
+        mm_tn, join(shared, 0, count), jnp.concatenate([by_own, by_node], axis=1)
+    )
+    grads = (
+        high_low(mm_tn, join(shared, 2 * count, slot_count), by_slot) + node_grads[:, 0:quarter],
+        node_grads[:, quarter:],
+        mm_tn(edge_feat[...], grad),
+        high_low(mm_tn, join(shared, count, count), by_agg),
+    )
     mine = core[0] == 0
-    for i, (low, high, high_right) in enumerate(
-        (
-            (sender_rows, edge_feat[...], grad),
-            (receiver_rows, message_grad, rows[:, 3 * size :]),
-        )
-    ):
-        low_sum = mm_tn(low, grad)
-        high_sum = mm_tn(high, high_right)
-        kept[i * size : (i + 1) * size, :] = jnp.where(mine, low_sum, high_sum)
-        given[i * size : (i + 1) * size, :] = jnp.where(mine, high_sum, low_sum)
-
-
-def payload_kernel(hidden, slots, kept, taken, payload):
+    for i in range(2):
+        kept[i * size : (i + 1) * size, :] = jnp.where(mine, grads[i], grads[i + 2])
+        given[i * size : (i + 1) * size, :] = jnp.where(mine, grads[i + 2], grads[i])
+
+
+def pair_kernel(kept, taken, sums):
     size = kept.shape[0] // 2
     quarter = kept.shape[1]
-    edges = slots.shape[1]
+    for i in range(2):
+        part = (kept[i * size : (i + 1) * size, :] + taken[i * size : (i + 1) * size, :]).astype(BF16)
+        sums[:, :, i * quarter : (i + 1) * quarter] = part.reshape(*sums.shape[0:2], quarter)
+
+
+def payload_kernel(hidden, indices, sums, payload):
+    spaces, capacity, lanes = payload.shape
+    quarter = hidden.shape[2]
+    edges = indices.shape[1]
+    payload[:, :, 0 : lanes - quarter] = sums[...]
     w_send = join(hidden, edges, quarter)
-    sums = mm(hot_by_column(slots[...], payload.shape[0]), join(hidden, 0, edges))
-    high, low = split_high_low(sums)
-    payload[:, 0:quarter] = (kept[0:size, :] + taken[0:size, :]).astype(BF16)
-    payload[:, quarter : 2 * quarter] = (kept[size:, :] + taken[size:, :]).astype(BF16)
-    payload[:, 2 * quarter :] = (mm_nt(high, w_send) + mm_nt(low, w_send)).astype(BF16)
-
-
-def edge_kernel(hidden, receivers, rows, edge_grad, recv_part, owner_hot):
+    terms = mm_nt(join(hidden, 0, edges), w_send)
+    part = pick_sum(hot_by_column(indices[1:2, :], spaces * capacity), terms).astype(BF16)
+    payload[:, :, lanes - quarter :] = part.reshape(spaces, capacity, quarter)
+
+
+def edge_kernel(hidden, indices, edge_grad, recv_part, owner_hot):
     edges, quarter = edge_grad.shape
     full = join(hidden, 0, edges)
     edge_grad[...] = mm_nt(full, join(hidden, edges + 2 * quarter, quarter))
-    sums = mm(hot_by_column(receivers[...], recv_part.shape[0]), full)
-    high, low = split_high_low(sums)
-    w_recv = join(hidden, edges + quarter, quarter)
-    recv_part[...] = mm_nt(high, w_recv) + mm_nt(low, w_recv)
-    owner_hot[...] = hot_by_column(rows[...], owner_hot.shape[0])
+    terms = mm_nt(full, join(hidden, edges + quarter, quarter))
+    recv_part[...] = pick_sum(hot_by_column(indices[0:1, :], recv_part.shape[0]), terms)
+    owner_hot[...] = hot_by_column(indices[4:5, :], owner_hot.shape[0])
 
 
 def last_kernel(
@@ -192,17 +232,15 @@
     sds = jax.ShapeDtypeStruct
     receivers = receivers.reshape(1, edges)
     slots = edge_slot.reshape(1, edges)
-    core = (lax.axis_index("space") % 2).reshape(1)
+    region = lax.axis_index("space").reshape(1)
+    core = region % 2
 
     def over_feat(x):
         return lax.all_to_all(x, "feat", split_axis=0, concat_axis=0, tiled=True)
 
     def over_space(x):
-        lanes = x.shape[1]
-        moved = lax.all_to_all(
-            x.reshape(spaces, capacity, lanes), "space", split_axis=0, concat_axis=0, tiled=True
-        )
-        return moved.reshape(slot_count, lanes)
+        moved = lax.all_to_all(x, "space", split_axis=0, concat_axis=0, tiled=True)
+        return moved.reshape(slot_count, x.shape[2])
 
     (picked,) = call(
         first_kernel,
@@ -217,34 +255,42 @@
         flops=2 * slot_count * node_count * quarter,
         limit=60 * 1024 * 1024,
     )
-    (spread,) = call(
-        spread_kernel,
-        (sds((feats, slot_count + 2 * node_count, quarter), BF16),),
-        over_space(picked), node, agg_grad,
-    )
-    shared = over_feat(spread)
-    rows, spread = call(
+    own, indices = call(
+        early_kernel,
+        (sds((2 * node_count, quarter), BF16), sds((8, edges), jnp.int32)),
+        region, node, agg_grad, receivers, slots, send_rows,
+        places=[SMEM] + [VMEM] * 5,
+    )
+    (packed,) = call(
+        pack_kernel,
+        (sds((2 * node_count + slot_count - capacity, quarter), BF16),),
+        region, over_space(picked.reshape(spaces, capacity, quarter)), own,
+        places=[SMEM] + [VMEM] * 2,
+    )
+    shared = lax.all_gather(packed, "feat", axis=0, tiled=False)
+    activation, spread = call(
         hidden_kernel,
         (
-            sds((edges, 3 * width + quarter), BF16),
+            sds((edges, quarter), BF16),
             sds((feats, edges + 3 * quarter, quarter), BF16),
         ),
-        shared, edge_feat, w_send, w_recv, w_edge, w_out, receivers, slots,
+        shared, edge_feat, w_send, w_recv, w_edge, w_out, indices,
         flops=2 * edges * width * (2 * node_count + slot_count + 4 * quarter),
     )
     hidden = over_feat(spread)
     kept, given = call(
         weight_kernel,
         (sds((2 * width, quarter), F32), sds((2 * width, quarter), F32)),
-        core, rows, edge_feat, spread,
-        places=[SMEM] + [VMEM] * 3,
+        core, shared, edge_feat, indices, activation, spread,
+        places=[SMEM] + [VMEM] * 5,
         flops=8 * edges * width * quarter,
     )
     taken = lax.ppermute(given, "space", [(i, i ^ 1) for i in range(spaces)])
+    (sums,) = call(pair_kernel, (sds((spaces, capacity, 2 * quarter), BF16),), kept, taken)
     (payload,) = call(
         payload_kernel,
-        (sds((slot_count, 3 * quarter), BF16),),
-        hidden, slots, kept, taken,
+        (sds((spaces, capacity, 3 * quarter), BF16),),
+        hidden, indices, sums,
         flops=2 * slot_count * width * (edges + 2 * quarter),
     )
     returned = over_space(payload)
@@ -255,7 +301,7 @@
             sds((node_count, quarter), F32),
             sds((node_count, slot_count), BF16),
         ),
-        hidden, receivers, send_rows,
+        hidden, indices,
         flops=2 * edges * width * (node_count + 2 * quarter),
     )
     small = sds((width // spaces, quarter), F32)

time: 102 us -> 93.4 us (0.916)
  blocking collectives: 49.3 us -> 13.3 us
  starting transfers between devices: 15.2 us -> 36.9 us
  waiting for transfers between devices: 22.3 us -> 31.1 us
  local copies, waits for them, and re-layouts: 4.51 us -> 0.81 us
    all_to_all x2 -> x0, blocking collectives: 49.3 us -> none  [the longest x1 31.2 us: over_space(): lax.all_to_all(x.reshape(spaces, capacity, lanes), 'space', split_axis=0,...]
    all_to_all x1 -> x2, starting transfers between devices: 7.91 us -> 28.2 us  [over_space(): moved = lax.all_to_all(x, 'space', split_axis=0, concat_axis=0, tiled=True)]
    all_gather x0 -> x1, blocking collectives: none -> 13.3 us  [local(): shared = lax.all_gather(packed, 'feat', axis=0, tiled=False)]
    all_to_all x1 -> x2, waiting for transfers between devices: 17 us -> 28.7 us  [over_space(): moved = lax.all_to_all(x, 'space', split_axis=0, concat_axis=0, tiled=True)]
    all_to_all x1, waiting for transfers between devices: 3.79 us -> 0.84 us  [over_feat(): return lax.all_to_all(x, 'feat', split_axis=0, concat_axis=0, tiled=True)]
    unnamed x24 -> x20, local copies, waits for them, and re-layouts: 3.56 us -> 0.71 us
    ppermute x1, starting transfers between devices: 3.73 us -> 5.16 us  [local(): taken = lax.ppermute(given, 'space', [(i, i ^ 1) for i in range(spaces)])]
    pallas_call x7 -> x9, Pallas kernels: 9.38 us -> 10 us  [call(): pl.pallas_call(kernel, out_shape=list(outs), in_specs=list(places or [VME...]
  transfers between devices with their start and end apart: 3 -> 4, of which waited for: 3 -> 4; matrix products, arithmetic and copies ran while one was open for 0% -> 0% of each run, Pallas kernels for 3% -> 4%
where the time goes in v4:
time: 93.4 us; the launch traced here: 92.9 us
  starting transfers between devices  36.9 us (40%)
  waiting for transfers between devices  31.1 us (33%)
  blocking collectives  13.3 us (14%)
  Pallas kernels  10 us (11%)
    all_to_all x2, waiting for transfers between devices, over_space(): moved = lax.all_to_all(x, 'space', split_axis=0, concat_axis=0, tiled=True)  28.7 us
    all_to_all x2, starting transfers between devices, over_space(): moved = lax.all_to_all(x, 'space', split_axis=0, concat_axis=0, tiled=True)  28.2 us
    all_gather x1, blocking collectives, local(): shared = lax.all_gather(packed, 'feat', axis=0, tiled=False)  13.3 us
    pallas_call x9, Pallas kernels, call(): pl.pallas_call(kernel, out_shape=list(outs), in_specs=list(places or [VME...  10 us
    ppermute x1, starting transfers between devices, local(): taken = lax.ppermute(given, 'space', [(i, i ^ 1) for i in range(spaces)])  5.16 us
    all_to_all x1, starting transfers between devices, over_feat(): return lax.all_to_all(x, 'feat', split_axis=0, concat_axis=0, tiled=True)  3.5 us
  transfers between devices with their start and end apart: 4, of which 4 were waited for; matrix products, arithmetic and copies ran while one was open for 0% of the time, Pallas kernels for 4%

profile of v4, /device:TPU:1, one launch (start us, length us, event | category | flops | bytes accessed | tf_op | source)
XLA Modules:
  0.0 92.9 jit_solution(8654606953969141913)
XLA Ops:
  0.6 1.8 %shard_map.145 = bf16[512,128]{1,0:T(8,128)(2,1)} custom-call(bf16[256,128]{1,0:T(8,128)(2,1)} %node.3, s32[1,512]{1,0:T(1,128)} %send_rows.1), custom_call_target="tpu_custom_call" | custom-call | flops 33554432 | bytes 198656 | tf_op jit(solution)/shard_map/pallas_call | solution.py:212
  2.4 0.0 copy-start.1
  2.4 18.6 %all-to-all-start = ((bf16[128,4,128]{2,1,0:T(4,128)(2,1)}), bf16[128,4,128]{2,1,0:T(4,128)(2,1)S(1)}, u32[]{:S(2)}, u32[]{:S(2)}) async-start(bf16[128,4,128]{2,1,0:T(4,128)(2,1)} %bitcast.10), calls=%async_computation | async-start | bytes 262144 | tf_op jit(solution)/shard_map/all_to_all | solution.py:242
  21.0 0.0 copy-start.5
  21.0 0.6 copy-done.5
  21.7 0.0 copy-done.4
  21.7 0.0 copy-done.3
  21.7 0.1 shard_map.146
  21.8 11.9 %all-to-all-done = bf16[128,4,128]{2,1,0:T(4,128)(2,1)S(1)} async-done(((bf16[128,4,128]{2,1,0:T(4,128)(2,1)}), bf16[128,4,128]{2,1,0:T(4,128)(2,1)S(1)}, u32[]{:S(2)}, u32[]{:S(2)}) %all-to-all-start) | async-done | bytes 131104 | tf_op jit(solution)/shard_map/all_to_all | solution.py:242
  33.7 0.1 shard_map.147
  33.8 13.3 %all-gather.1.shared = bf16[4,1020,128]{2,1,0:T(8,128)(2,1)S(1)} all-gather(bf16[1,1020,128]{2,1,0:T(8,128)(2,1)S(1)} %bitcast.6), channel_id=2, replica_groups=mesh['space'=128,'feat'=4] {'feat'}, dimensions={0}, use_global_device_ids=true | all-gather | bytes 1305600 | tf_op jit(solution)/shard_map/all_gather | solution.py:270
  47.2 2.0 %shard_map.148 = (bf16[512,128]{1,0:T(8,128)(2,1)S(1)}, bf16[4,896,128]{2,1,0:T(8,128)(2,1)}) custom-call(bf16[4,1020,128]{2,1,0:T(8,128)(2,1)S(1)} %all-gather.1.shared, bf16[512,512]{1,0:T(8,128)(2,1)S(1)} %copy-done, bf16[512,128]{1,0:T(8,128)(2,1)S(1)} %copy-done.6, bf16[512,128]{1,0:T(8,128)(2,1)S(1)} %copy-done.7, bf16[512,128]{1,0:T(8,128)(2,1)S(1)} %copy-done.8, ...), custom_call_target="tpu_custom_call" | custom-call | flops 805306368 | bytes 3158016 | tf_op jit(solution)/shard_map/pallas_call | solution.py:212
  49.2 3.5 %all-to-all-start.1 = ((bf16[4,896,128]{2,1,0:T(8,128)(2,1)}), bf16[4,896,128]{2,1,0:T(8,128)(2,1)S(1)}, u32[]{:S(2)}, u32[]{:S(2)}) async-start(bf16[4,896,128]{2,1,0:T(8,128)(2,1)} %get-tuple-element.22.spread), calls=%async_computation.1 | async-start | bytes 1835008 | tf_op jit(solution)/shard_map/all_to_all | solution.py:239
  52.7 2.5 %shard_map.149 = (f32[1024,128]{1,0:T(8,128)S(1)}, f32[1024,128]{1,0:T(8,128)S(1)}) custom-call(s32[1]{0:T(128)S(6)} %select_n.7.core, bf16[4,1020,128]{2,1,0:T(8,128)(2,1)S(1)} %all-gather.1.shared, bf16[512,512]{1,0:T(8,128)(2,1)S(1)} %copy-done, s32[8,512]{1,0:T(8,128)S(1)} %get-tuple-element.21.indices, ...), custom_call_target="tpu_custom_call" | custom-call | flops 268435456 | bytes 3682308 | tf_op jit(solution)/shard_map/pallas_call | solution.py:212
  55.1 5.2 %collective-permute-start = (f32[1024,128]{1,0:T(8,128)S(1)}, f32[1024,128]{1,0:T(8,128)S(1)}, u32[]{:S(2)}, u32[]{:S(2)}) collective-permute-start(f32[1024,128]{1,0:T(8,128)S(1)} %get-tuple-element.25), channel_id=1, source_target_pairs={{0,4},{4,0},{8,12},{12,8},{16,20},{20,16},{24,28},{28,24},{32,36},... | collective-permute-start | bytes 1572872 | tf_op jit(solution)/shard_map/ppermute | solution.py:288
  60.3 1.5 %collective-permute-done.taken = f32[1024,128]{1,0:T(8,128)S(1)} collective-permute-done((f32[1024,128]{1,0:T(8,128)S(1)}, f32[1024,128]{1,0:T(8,128)S(1)}, u32[]{:S(2)}, u32[]{:S(2)}) %collective-permute-start) | collective-permute-done | bytes 524320 | tf_op jit(solution)/shard_map/ppermute | solution.py:288
  61.8 0.1 shard_map.150.sums
  61.9 0.8 all-to-all-done.1.hidden
  62.7 1.5 %shard_map.151 = bf16[128,4,384]{2,1,0:T(4,128)(2,1)} custom-call(bf16[4,896,128]{2,1,0:T(8,128)(2,1)S(1)} %all-to-all-done.1.hidden, s32[8,512]{1,0:T(8,128)S(1)} %get-tuple-element.21.indices, bf16[128,4,256]{2,1,0:T(4,128)(2,1)S(1)} %shard_map.150.sums), custom_call_target="tpu_custom_call" | custom-call | flops 402653184 | bytes 1589248 | tf_op jit(solution)/shard_map/pallas_call | solution.py:212
  64.2 9.7 %all-to-all-start.2 = ((bf16[128,4,384]{2,1,0:T(4,128)(2,1)}), bf16[128,4,384]{2,1,0:T(4,128)(2,1)S(1)}, u32[]{:S(2)}, u32[]{:S(2)}) async-start(bf16[128,4,384]{2,1,0:T(4,128)(2,1)} %shard_map.151), calls=%async_computation.2 | async-start | bytes 786432 | tf_op jit(solution)/shard_map/all_to_all | solution.py:242
  73.9 1.2 %shard_map.152 = (f32[512,128]{1,0:T(8,128)}, f32[256,128]{1,0:T(8,128)S(1)}, bf16[256,512]{1,0:T(8,128)(2,1)S(1)}) custom-call(bf16[4,896,128]{2,1,0:T(8,128)(2,1)S(1)} %all-to-all-done.1.hidden, s32[8,512]{1,0:T(8,128)S(1)} %get-tuple-element.21.indices), custom_call_target="tpu_custom_call" | custom-call | flops 268435456 | bytes 1589248 | tf_op jit(solution)/shard_map/pallas_call | solution.py:212
  75.1 16.8 %all-to-all-done.2 = bf16[128,4,384]{2,1,0:T(4,128)(2,1)S(1)} async-done(((bf16[128,4,384]{2,1,0:T(4,128)(2,1)}), bf16[128,4,384]{2,1,0:T(4,128)(2,1)S(1)}, u32[]{:S(2)}, u32[]{:S(2)}) %all-to-all-start.2) | async-done | bytes 393248 | tf_op jit(solution)/shard_map/all_to_all | solution.py:242
  91.9 0.1 reshape.37.arrived
  92.0 0.9 shard_map.153
  (15 shorter events, 0.0 us)
Async XLA Ops:
  2.4 18.6 %copy-start.1 = (bf16[256,128]{1,0:T(8,128)(2,1)S(1)}, bf16[256,128]{1,0:T(8,128)(2,1)}, u32[]{:S(2)}) copy-start(bf16[256,128]{1,0:T(8,128)(2,1)} %node.3) | copy-start | bytes 196612
  2.4 18.6 %copy-start.2 = (bf16[256,128]{1,0:T(8,128)(2,1)S(1)}, bf16[256,128]{1,0:T(8,128)(2,1)}, u32[]{:S(2)}) copy-start(bf16[256,128]{1,0:T(8,128)(2,1)} %agg.1) | copy-start | bytes 196612
  2.4 31.3 %all-to-all-start = ((bf16[128,4,128]{2,1,0:T(4,128)(2,1)}), bf16[128,4,128]{2,1,0:T(4,128)(2,1)S(1)}, u32[]{:S(2)}, u32[]{:S(2)}) async-start(bf16[128,4,128]{2,1,0:T(4,128)(2,1)} %bitcast.10), calls=%async_computation | async-start | bytes 262144 | tf_op jit(solution)/shard_map/all_to_all | solution.py:242
  21.0 0.7 copy-start.5
  21.0 0.7 copy-start.4
  21.0 0.7 copy-start.3
  33.8 13.4 %copy-start = (bf16[512,512]{1,0:T(8,128)(2,1)S(1)}, bf16[512,512]{1,0:T(8,128)(2,1)}, u32[]{:S(2)}) copy-start(bf16[512,512]{1,0:T(8,128)(2,1)} %edge_feat.3) | copy-start | bytes 1572868
  33.8 13.4 %copy-start.6 = (bf16[512,128]{1,0:T(8,128)(2,1)S(1)}, bf16[512,128]{1,0:T(8,128)(2,1)}, u32[]{:S(2)}) copy-start(bf16[512,128]{1,0:T(8,128)(2,1)} %w_send.1) | copy-start | bytes 393220
  33.8 13.3 %copy-start.7 = (bf16[512,128]{1,0:T(8,128)(2,1)S(1)}, bf16[512,128]{1,0:T(8,128)(2,1)}, u32[]{:S(2)}) copy-start(bf16[512,128]{1,0:T(8,128)(2,1)} %w_recv.1) | copy-start | bytes 393220
  33.8 13.3 %copy-start.8 = (bf16[512,128]{1,0:T(8,128)(2,1)S(1)}, bf16[512,128]{1,0:T(8,128)(2,1)}, u32[]{:S(2)}) copy-start(bf16[512,128]{1,0:T(8,128)(2,1)} %w_edge.1) | copy-start | bytes 393220
  33.8 13.3 %copy-start.9 = (bf16[512,128]{1,0:T(8,128)(2,1)S(1)}, bf16[512,128]{1,0:T(8,128)(2,1)}, u32[]{:S(2)}) copy-start(bf16[512,128]{1,0:T(8,128)(2,1)} %w_out.1) | copy-start | bytes 393220
  49.2 13.6 %all-to-all-start.1 = ((bf16[4,896,128]{2,1,0:T(8,128)(2,1)}), bf16[4,896,128]{2,1,0:T(8,128)(2,1)S(1)}, u32[]{:S(2)}, u32[]{:S(2)}) async-start(bf16[4,896,128]{2,1,0:T(8,128)(2,1)} %get-tuple-element.22.spread), calls=%async_computation.1 | async-start | bytes 1835008 | tf_op jit(solution)/shard_map/all_to_all | solution.py:239
  55.1 6.7 %collective-permute-start = (f32[1024,128]{1,0:T(8,128)S(1)}, f32[1024,128]{1,0:T(8,128)S(1)}, u32[]{:S(2)}, u32[]{:S(2)}) collective-permute-start(f32[1024,128]{1,0:T(8,128)S(1)} %get-tuple-element.25), channel_id=1, source_target_pairs={{0,4},{4,0},{8,12},{12,8},{16,20},{20,16},{24,28},{28,24},{32,36},... | collective-permute-start | bytes 1572872 | tf_op jit(solution)/shard_map/ppermute | solution.py:288
  64.2 27.7 %all-to-all-start.2 = ((bf16[128,4,384]{2,1,0:T(4,128)(2,1)}), bf16[128,4,384]{2,1,0:T(4,128)(2,1)S(1)}, u32[]{:S(2)}, u32[]{:S(2)}) async-start(bf16[128,4,384]{2,1,0:T(4,128)(2,1)} %shard_map.151), calls=%async_computation.2 | async-start | bytes 786432 | tf_op jit(solution)/shard_map/all_to_all | solution.py:242

commit v5 on v4

--- a/solution.py
+++ b/solution.py
@@ -176,21 +176,19 @@
     payload[:, :, lanes - quarter :] = part.reshape(spaces, capacity, quarter)
 
 
-def edge_kernel(hidden, indices, edge_grad, recv_part, owner_hot):
+def last_kernel(
+    arrived, hidden, indices,
+    edge_grad, node_grad, grad_send, grad_recv, grad_edge, grad_out, edge_here, sem,
+):
     edges, quarter = edge_grad.shape
     full = join(hidden, 0, edges)
-    edge_grad[...] = mm_nt(full, join(hidden, edges + 2 * quarter, quarter))
+    edge_here[...] = mm_nt(full, join(hidden, edges + 2 * quarter, quarter))
+    (copy,) = fetch(sem, (edge_here, edge_grad))
     terms = mm_nt(full, join(hidden, edges + quarter, quarter))
-    recv_part[...] = pick_sum(hot_by_column(indices[0:1, :], recv_part.shape[0]), terms)
-    owner_hot[...] = hot_by_column(indices[4:5, :], owner_hot.shape[0])
-
-
-def last_kernel(
-    arrived, owner_hot, recv_part, node_grad, grad_send, grad_recv, grad_edge, grad_out
-):
-    quarter = node_grad.shape[1]
-    back = mm(owner_hot[...], arrived[:, 2 * quarter : 3 * quarter])
-    node_grad[...] = recv_part[...] + back
+    count = node_grad.shape[0]
+    node_grad[...] = pick_sum(hot_by_column(indices[0:1, :], count), terms) + mm(
+        hot_by_column(indices[4:5, :], count), arrived[:, 2 * quarter : 3 * quarter]
+    )
     shape = (8, arrived.shape[0])
     place = lax.broadcasted_iota(jnp.int32, shape, 1) % 8
     pick = hot(place == lax.broadcasted_iota(jnp.int32, shape, 0))
@@ -199,6 +197,7 @@
     grad_recv[...] = sums[0:4, quarter:]
     grad_edge[...] = sums[4:8, 0:quarter]
     grad_out[...] = sums[4:8, quarter:]
+    copy.wait()
 
 
 ANY = pl.BlockSpec(memory_space=pl.ANY)
@@ -206,14 +205,14 @@
 SMEM = pl.BlockSpec(memory_space=pltpu.SMEM)
 
 
-def call(kernel, outs, *operands, places=None, scratch=(), flops=0, limit=24 * 1024 * 1024):
+def call(kernel, outs, *operands, places=None, out_places=None, scratch=(), flops=0, limit=24 * 1024 * 1024):
     moved = sum(x.size * x.dtype.itemsize for x in operands)
     moved += sum(x.size * x.dtype.itemsize for x in outs)
     return pl.pallas_call(
         kernel,
         out_shape=list(outs),
         in_specs=list(places or [VMEM] * len(operands)),
-        out_specs=[VMEM] * len(outs),
+        out_specs=list(out_places or [VMEM] * len(outs)),
         scratch_shapes=list(scratch),
         compiler_params=pltpu.CompilerParams(vmem_limit_bytes=limit),
         cost_estimate=pl.CostEstimate(flops=flops, bytes_accessed=moved, transcendentals=0),
@@ -294,22 +293,18 @@
         flops=2 * slot_count * width * (edges + 2 * quarter),
     )
     returned = over_space(payload)
-    edge_grad, recv_part, owner_hot = call(
-        edge_kernel,
+    small = sds((width // spaces, quarter), F32)
+    edge_grad, node_grad, grad_send, grad_recv, grad_edge, grad_out = call(
+        last_kernel,
         (
             sds((edges, quarter), F32),
             sds((node_count, quarter), F32),
-            sds((node_count, slot_count), BF16),
+            small, small, small, small,
         ),
-        hidden, indices,
-        flops=2 * edges * width * (node_count + 2 * quarter),
-    )
-    small = sds((width // spaces, quarter), F32)
-    node_grad, grad_send, grad_recv, grad_edge, grad_out = call(
-        last_kernel,
-        (sds((node_count, quarter), F32), small, small, small, small),
-        returned, owner_hot, recv_part,
-        flops=2 * node_count * slot_count * quarter,
+        returned, hidden, indices,
+        out_places=[ANY] + [VMEM] * 5,
+        scratch=[pltpu.VMEM((edges, quarter), F32), pltpu.SemaphoreType.DMA((1,))],
+        flops=2 * edges * (2 * width * quarter + 3 * node_count * quarter),
     )
     return (node_grad, edge_grad, grad_send, grad_recv, grad_edge, grad_out)
 

time: 93.4 us -> 92.9 us (level)
  blocking collectives: 13.3 us -> 40.4 us
  waiting for transfers between devices: 31.1 us -> 14.3 us
  starting transfers between devices: 36.9 us -> 27.2 us
  Pallas kernels: 10 us -> 9.02 us
    all_to_all x0 -> x1, blocking collectives: none -> 27.1 us  [over_space(): moved = lax.all_to_all(x, 'space', split_axis=0, concat_axis=0, tiled=True)]
    all_to_all x2 -> x1, waiting for transfers between devices: 28.7 us -> 11.9 us  [over_space(): moved = lax.all_to_all(x, 'space', split_axis=0, concat_axis=0, tiled=True)]
    all_to_all x2 -> x1, starting transfers between devices: 28.2 us -> 18.6 us  [over_space(): moved = lax.all_to_all(x, 'space', split_axis=0, concat_axis=0, tiled=True)]
    pallas_call x9 -> x8, Pallas kernels: 10 us -> 9.02 us  [call(): pl.pallas_call(kernel, out_shape=list(outs), in_specs=list(places or [VME...]
  transfers between devices with their start and end apart: 4 -> 3, of which waited for: 4 -> 3; matrix products, arithmetic and copies ran while one was open for 0% -> 0% of each run, Pallas kernels for 4% -> 3%
where the time goes in v5:
time: 92.9 us; the launch traced here: 92.5 us
  blocking collectives  40.4 us (43%)
  starting transfers between devices  27.2 us (29%)
  waiting for transfers between devices  14.3 us (15%)
  Pallas kernels  9.02 us (10%)
    all_to_all x1, blocking collectives, over_space(): moved = lax.all_to_all(x, 'space', split_axis=0, concat_axis=0, tiled=True)  27.1 us
    all_to_all x1, starting transfers between devices, over_space(): moved = lax.all_to_all(x, 'space', split_axis=0, concat_axis=0, tiled=True)  18.6 us
    all_gather x1, blocking collectives, local(): shared = lax.all_gather(packed, 'feat', axis=0, tiled=False)  13.3 us
    all_to_all x1, waiting for transfers between devices, over_space(): moved = lax.all_to_all(x, 'space', split_axis=0, concat_axis=0, tiled=True)  11.9 us
    pallas_call x8, Pallas kernels, call(): pl.pallas_call(kernel, out_shape=list(outs), in_specs=list(places or [VME...  9.02 us
    ppermute x1, starting transfers between devices, local(): taken = lax.ppermute(given, 'space', [(i, i ^ 1) for i in range(spaces)])  5.18 us
    all_to_all x1, starting transfers between devices, over_feat(): return lax.all_to_all(x, 'feat', split_axis=0, concat_axis=0, tiled=True)  3.5 us
  transfers between devices with their start and end apart: 3, of which 3 were waited for; matrix products, arithmetic and copies ran while one was open for 0% of the time, Pallas kernels for 3%

profile of v5, /device:TPU:1, one launch (start us, length us, event | category | flops | bytes accessed | tf_op | source)
XLA Modules:
  0.0 92.5 jit_solution(15009882085738652466)
XLA Ops:
  0.6 1.8 %shard_map.145 = bf16[512,128]{1,0:T(8,128)(2,1)} custom-call(bf16[256,128]{1,0:T(8,128)(2,1)} %node.3, s32[1,512]{1,0:T(1,128)} %send_rows.1), custom_call_target="tpu_custom_call" | custom-call | flops 33554432 | bytes 198656 | tf_op jit(solution)/shard_map/pallas_call | solution.py:211
  2.4 0.0 copy-start.1
  2.4 18.6 %all-to-all-start = ((bf16[128,4,128]{2,1,0:T(4,128)(2,1)}), bf16[128,4,128]{2,1,0:T(4,128)(2,1)S(1)}, u32[]{:S(2)}, u32[]{:S(2)}) async-start(bf16[128,4,128]{2,1,0:T(4,128)(2,1)} %bitcast.10), calls=%async_computation | async-start | bytes 262144 | tf_op jit(solution)/shard_map/all_to_all | solution.py:241
  21.0 0.0 copy-start.5
  21.0 0.0 copy-start.4
  21.0 0.6 copy-done.5
  21.7 0.0 copy-done.4
  21.7 0.0 copy-done.3
  21.7 0.1 shard_map.146
  21.8 11.9 %all-to-all-done = bf16[128,4,128]{2,1,0:T(4,128)(2,1)S(1)} async-done(((bf16[128,4,128]{2,1,0:T(4,128)(2,1)}), bf16[128,4,128]{2,1,0:T(4,128)(2,1)S(1)}, u32[]{:S(2)}, u32[]{:S(2)}) %all-to-all-start) | async-done | bytes 131104 | tf_op jit(solution)/shard_map/all_to_all | solution.py:241
  33.7 0.1 shard_map.147
  33.8 0.0 copy-start.7
  33.8 13.3 %all-gather.1.shared = bf16[4,1020,128]{2,1,0:T(8,128)(2,1)S(1)} all-gather(bf16[1,1020,128]{2,1,0:T(8,128)(2,1)S(1)} %bitcast.6), channel_id=2, replica_groups=mesh['space'=128,'feat'=4] {'feat'}, dimensions={0}, use_global_device_ids=true | all-gather | bytes 1305600 | tf_op jit(solution)/shard_map/all_gather | solution.py:269
  47.2 2.0 %shard_map.148 = (bf16[512,128]{1,0:T(8,128)(2,1)S(1)}, bf16[4,896,128]{2,1,0:T(8,128)(2,1)}) custom-call(bf16[4,1020,128]{2,1,0:T(8,128)(2,1)S(1)} %all-gather.1.shared, bf16[512,512]{1,0:T(8,128)(2,1)S(1)} %copy-done, bf16[512,128]{1,0:T(8,128)(2,1)S(1)} %copy-done.6, bf16[512,128]{1,0:T(8,128)(2,1)S(1)} %copy-done.7, bf16[512,128]{1,0:T(8,128)(2,1)S(1)} %copy-done.8, ...), custom_call_target="tpu_custom_call" | custom-call | flops 805306368 | bytes 3158016 | tf_op jit(solution)/shard_map/pallas_call | solution.py:211
  49.2 3.5 %all-to-all-start.1 = ((bf16[4,896,128]{2,1,0:T(8,128)(2,1)}), bf16[4,896,128]{2,1,0:T(8,128)(2,1)S(1)}, u32[]{:S(2)}, u32[]{:S(2)}) async-start(bf16[4,896,128]{2,1,0:T(8,128)(2,1)} %get-tuple-element.20.spread), calls=%async_computation.1 | async-start | bytes 1835008 | tf_op jit(solution)/shard_map/all_to_all | solution.py:238
  52.7 2.4 %shard_map.149 = (f32[1024,128]{1,0:T(8,128)S(1)}, f32[1024,128]{1,0:T(8,128)S(1)}) custom-call(s32[1]{0:T(128)S(6)} %select_n.7.core, bf16[4,1020,128]{2,1,0:T(8,128)(2,1)S(1)} %all-gather.1.shared, bf16[512,512]{1,0:T(8,128)(2,1)S(1)} %copy-done, s32[8,512]{1,0:T(8,128)S(1)} %get-tuple-element.19.indices, ...), custom_call_target="tpu_custom_call" | custom-call | flops 268435456 | bytes 3682308 | tf_op jit(solution)/shard_map/pallas_call | solution.py:211
  55.1 5.2 %collective-permute-start = (f32[1024,128]{1,0:T(8,128)S(1)}, f32[1024,128]{1,0:T(8,128)S(1)}, u32[]{:S(2)}, u32[]{:S(2)}) collective-permute-start(f32[1024,128]{1,0:T(8,128)S(1)} %get-tuple-element.23), channel_id=1, source_target_pairs={{0,4},{4,0},{8,12},{12,8},{16,20},{20,16},{24,28},{28,24},{32,36},... | collective-permute-start | bytes 1572872 | tf_op jit(solution)/shard_map/ppermute | solution.py:287
  60.3 1.5 %collective-permute-done.taken = f32[1024,128]{1,0:T(8,128)S(1)} collective-permute-done((f32[1024,128]{1,0:T(8,128)S(1)}, f32[1024,128]{1,0:T(8,128)S(1)}, u32[]{:S(2)}, u32[]{:S(2)}) %collective-permute-start) | collective-permute-done | bytes 524320 | tf_op jit(solution)/shard_map/ppermute | solution.py:287
  61.8 0.1 shard_map.150.sums
  61.9 0.8 all-to-all-done.1.hidden
  62.7 0.7 shard_map.151
  63.5 27.1 %all_to_all.15 = bf16[128,4,384]{2,1,0:T(4,128)(2,1)S(1)} all-to-all(bf16[128,4,384]{2,1,0:T(4,128)(2,1)S(1)} %shard_map.151), channel_id=1, replica_groups=mesh['space'=128,'feat'=4] {'space'}, dimensions={0} | all-to-all | bytes 786432 | tf_op jit(solution)/shard_map/all_to_all | solution.py:241
  90.6 0.1 reshape.37.arrived
  90.7 1.8 %shard_map.152 = (f32[512,128]{1,0:T(8,128)}, f32[256,128]{1,0:T(8,128)}, f32[4,128]{1,0:T(4,128)}, f32[4,128]{1,0:T(4,128)}, f32[4,128]{1,0:T(4,128)}, /*index=5*/f32[4,128]{1,0:T(4,128)}) custom-call(bf16[512,384]{1,0:T(8,128)(2,1)S(1)} %reshape.37.arrived, bf16[4,896,128]{2,1,0:T(8,128)(2,1)S(1)} %all-to-all-done.1.hidden, ...), custom_call_target="tpu_custom_call" | custom-call | flops 234881024 | bytes 1728512 | tf_op jit(solution)/shard_map/pallas_call | solution.py:211
  (13 shorter events, 0.0 us)
Async XLA Ops:
  2.4 18.6 %copy-start.1 = (bf16[256,128]{1,0:T(8,128)(2,1)S(1)}, bf16[256,128]{1,0:T(8,128)(2,1)}, u32[]{:S(2)}) copy-start(bf16[256,128]{1,0:T(8,128)(2,1)} %node.3) | copy-start | bytes 196612
  2.4 18.6 %copy-start.2 = (bf16[256,128]{1,0:T(8,128)(2,1)S(1)}, bf16[256,128]{1,0:T(8,128)(2,1)}, u32[]{:S(2)}) copy-start(bf16[256,128]{1,0:T(8,128)(2,1)} %agg.1) | copy-start | bytes 196612
  2.4 31.3 %all-to-all-start = ((bf16[128,4,128]{2,1,0:T(4,128)(2,1)}), bf16[128,4,128]{2,1,0:T(4,128)(2,1)S(1)}, u32[]{:S(2)}, u32[]{:S(2)}) async-start(bf16[128,4,128]{2,1,0:T(4,128)(2,1)} %bitcast.10), calls=%async_computation | async-start | bytes 262144 | tf_op jit(solution)/shard_map/all_to_all | solution.py:241
  21.0 0.7 copy-start.5
  21.0 0.7 copy-start.4
  21.0 0.7 copy-start.3
  33.8 13.4 %copy-start = (bf16[512,512]{1,0:T(8,128)(2,1)S(1)}, bf16[512,512]{1,0:T(8,128)(2,1)}, u32[]{:S(2)}) copy-start(bf16[512,512]{1,0:T(8,128)(2,1)} %edge_feat.3) | copy-start | bytes 1572868
  33.8 13.4 %copy-start.6 = (bf16[512,128]{1,0:T(8,128)(2,1)S(1)}, bf16[512,128]{1,0:T(8,128)(2,1)}, u32[]{:S(2)}) copy-start(bf16[512,128]{1,0:T(8,128)(2,1)} %w_send.1) | copy-start | bytes 393220
  33.8 13.3 %copy-start.7 = (bf16[512,128]{1,0:T(8,128)(2,1)S(1)}, bf16[512,128]{1,0:T(8,128)(2,1)}, u32[]{:S(2)}) copy-start(bf16[512,128]{1,0:T(8,128)(2,1)} %w_recv.1) | copy-start | bytes 393220
  33.8 13.3 %copy-start.8 = (bf16[512,128]{1,0:T(8,128)(2,1)S(1)}, bf16[512,128]{1,0:T(8,128)(2,1)}, u32[]{:S(2)}) copy-start(bf16[512,128]{1,0:T(8,128)(2,1)} %w_edge.1) | copy-start | bytes 393220
  33.8 13.3 %copy-start.9 = (bf16[512,128]{1,0:T(8,128)(2,1)S(1)}, bf16[512,128]{1,0:T(8,128)(2,1)}, u32[]{:S(2)}) copy-start(bf16[512,128]{1,0:T(8,128)(2,1)} %w_out.1) | copy-start | bytes 393220
  49.2 13.6 %all-to-all-start.1 = ((bf16[4,896,128]{2,1,0:T(8,128)(2,1)}), bf16[4,896,128]{2,1,0:T(8,128)(2,1)S(1)}, u32[]{:S(2)}, u32[]{:S(2)}) async-start(bf16[4,896,128]{2,1,0:T(8,128)(2,1)} %get-tuple-element.20.spread), calls=%async_computation.1 | async-start | bytes 1835008 | tf_op jit(solution)/shard_map/all_to_all | solution.py:238
  55.1 6.7 %collective-permute-start = (f32[1024,128]{1,0:T(8,128)S(1)}, f32[1024,128]{1,0:T(8,128)S(1)}, u32[]{:S(2)}, u32[]{:S(2)}) collective-permute-start(f32[1024,128]{1,0:T(8,128)S(1)} %get-tuple-element.23), channel_id=1, source_target_pairs={{0,4},{4,0},{8,12},{12,8},{16,20},{20,16},{24,28},{28,24},{32,36},... | collective-permute-start | bytes 1572872 | tf_op jit(solution)/shard_map/ppermute | solution.py:287

commit v6 on v5

--- a/solution.py
+++ b/solution.py
@@ -1,3 +1,5 @@
+import functools
+
 import jax
 import jax.numpy as jnp
 from jax import lax
@@ -9,6 +11,7 @@
 BF16 = jnp.bfloat16
 LANES = 128
 CAPACITY = 4
+Z_STRIDE = 16
 
 
 def mm(a, b):
@@ -67,12 +70,22 @@
     return product(a, high) + product(a, low)
 
 
-def first_kernel(node, rows, picked, node_here, rows_here, sems):
+def first_kernel(node, rows, picked, node_here, rows_here, picked_here, sems, out_sems):
     copies = fetch(sems, (rows, rows_here), (node, node_here))
     copies[0].wait()
-    pick = hot_by_row(rows_here[...], node.shape[0])
+    picks = hot_by_row(rows_here[...], node.shape[0])
     copies[1].wait()
-    picked[...] = mm(pick, node_here[...]).astype(BF16)
+    size = picked.shape[0] // 2
+    parts = []
+    for i in range(2):
+        part = pl.ds(i * size, size)
+        picked_here[part, :] = mm(picks[i * size : (i + 1) * size], node_here[...]).astype(BF16)
+        parts.append(
+            pltpu.make_async_copy(picked_here.at[part, :], picked.at[part, :], out_sems.at[i])
+        )
+        parts[-1].start()
+    for part in parts:
+        part.wait()
 
 
 def early_kernel(region, node, agg, receivers, slots, send_rows, own, indices):
@@ -103,9 +116,23 @@
 
 
 def hidden_kernel(
-    shared, edge_feat, w_send, w_recv, w_edge, w_out, indices, activation, spread
+    shared, edge_feat, w_send, w_recv, w_edge, w_out, indices,
+    activation, spread, hidden, sems, hidden_sems,
 ):
     edges, quarter = activation.shape
+    feats = spread.shape[0]
+    weights = (w_send, w_recv, w_edge)
+    blocks = fetch(
+        sems,
+        *(
+            (
+                weight.at[q * quarter : (q + 1) * quarter, :],
+                spread.at[q, edges + i * quarter : edges + (i + 1) * quarter, :],
+            )
+            for q in range(feats)
+            for i, weight in enumerate(weights)
+        ),
+    )
     slot_count = edges - CAPACITY
     count = (shared.shape[1] - slot_count) // 2
     at_node = mm(join(shared, 0, count), jnp.concatenate([w_recv[...], w_send[...]], axis=1))
@@ -122,82 +149,104 @@
     )
     gate = jax.nn.sigmoid(pre_act)
     activation[...] = (pre_act * gate).astype(BF16)
-    grad = (act_grad * gate * (1.0 + pre_act * (1.0 - gate))).astype(BF16)
-    for q in range(spread.shape[0]):
-        spread[q, 0:edges, :] = grad
-        block = slice(q * quarter, (q + 1) * quarter)
-        for i, weight in enumerate((w_send, w_recv, w_edge)):
-            start = edges + i * quarter
-            spread[q, start : start + quarter, :] = weight[block, :]
-
-
-def weight_kernel(core, shared, edge_feat, indices, activation, spread, kept, given):
-    edges, size = edge_feat.shape
-    quarter = activation.shape[1]
+    hidden[...] = (act_grad * gate * (1.0 + pre_act * (1.0 - gate))).astype(BF16)
+    rows = fetch(
+        hidden_sems, *((hidden, spread.at[q, 0:edges, :]) for q in range(feats))
+    )
+    for copy in (*rows, *blocks):
+        copy.wait()
+
+
+def sender_grads(shared, indices, hidden, out):
+    edges = hidden.shape[0]
     slot_count = edges - CAPACITY
+    size = out.shape[0] // 2
+    quarter = out.shape[1]
     count = (shared.shape[1] - slot_count) // 2
-    grad = spread[0, 0:edges, :]
-    receive = hot_by_column(indices[0:1, :], count)
+    grad = hidden[...]
     by_slot = mm(hot_by_column(indices[2:3, :], slot_count), grad)
     by_own = mm(hot_by_column(indices[3:4, :], count), grad)
-    by_node = mm(receive, grad)
-    by_agg = mm(receive, activation[...])
+    by_node = mm(hot_by_column(indices[0:1, :], count), grad)
     node_grads = high_low(
         mm_tn, join(shared, 0, count), jnp.concatenate([by_own, by_node], axis=1)
     )
-    grads = (
-        high_low(mm_tn, join(shared, 2 * count, slot_count), by_slot) + node_grads[:, 0:quarter],
-        node_grads[:, quarter:],
-        mm_tn(edge_feat[...], grad),
-        high_low(mm_tn, join(shared, count, count), by_agg),
-    )
-    mine = core[0] == 0
-    for i in range(2):
-        kept[i * size : (i + 1) * size, :] = jnp.where(mine, grads[i], grads[i + 2])
-        given[i * size : (i + 1) * size, :] = jnp.where(mine, grads[i + 2], grads[i])
-
-
-def pair_kernel(kept, taken, sums):
-    size = kept.shape[0] // 2
-    quarter = kept.shape[1]
-    for i in range(2):
-        part = (kept[i * size : (i + 1) * size, :] + taken[i * size : (i + 1) * size, :]).astype(BF16)
-        sums[:, :, i * quarter : (i + 1) * quarter] = part.reshape(*sums.shape[0:2], quarter)
-
-
-def payload_kernel(hidden, indices, sums, payload):
-    spaces, capacity, lanes = payload.shape
-    quarter = hidden.shape[2]
+    out[0:size, :] = (
+        high_low(mm_tn, join(shared, 2 * count, slot_count), by_slot) + node_grads[:, 0:quarter]
+    )
+    out[size:, :] = node_grads[:, quarter:]
+
+
+def edge_grads(shared, indices, hidden, edge_feat, activation, out):
+    edges = hidden.shape[0]
+    size = out.shape[0] // 2
+    count = (shared.shape[1] - edges + CAPACITY) // 2
+    out[0:size, :] = mm_tn(edge_feat[...], hidden[...])
+    by_agg = mm(hot_by_column(indices[0:1, :], count), activation[...])
+    out[size:, :] = high_low(mm_tn, join(shared, count, count), by_agg)
+
+
+def weight_kernel(other, core, shared, edge_feat, indices, activation, hidden, out):
+    first = (core[0] + other) % 2 == 0
+    pl.when(first)(lambda: sender_grads(shared, indices, hidden, out))
+    pl.when(jnp.logical_not(first))(
+        lambda: edge_grads(shared, indices, hidden, edge_feat, activation, out)
+    )
+
+
+def pair_kernel(side, kept, taken, mine, given):
+    size = mine.shape[0]
+    first, second = (
+        kept[i * size : (i + 1) * size, :] + taken[i * size : (i + 1) * size, :] for i in range(2)
+    )
+    even = side[0] == 0
+    mine[...] = jnp.where(even, first, second)
+    given[...] = jnp.where(even, second, first).astype(BF16)
+
+
+def slot_kernel(hidden, indices, terms):
+    spaces, capacity, quarter = terms.shape
     edges = indices.shape[1]
-    payload[:, :, 0 : lanes - quarter] = sums[...]
     w_send = join(hidden, edges, quarter)
-    terms = mm_nt(join(hidden, 0, edges), w_send)
-    part = pick_sum(hot_by_column(indices[1:2, :], spaces * capacity), terms).astype(BF16)
-    payload[:, :, lanes - quarter :] = part.reshape(spaces, capacity, quarter)
+    by_edge = mm_nt(join(hidden, 0, edges), w_send)
+    sums = pick_sum(hot_by_column(indices[1:2, :], spaces * capacity), by_edge)
+    terms[...] = sums.astype(BF16).reshape(terms.shape)
+
+
+def payload_kernel(mine, taken, terms, payload):
+    quarter = mine.shape[1]
+    total = (mine[...] + taken[...].astype(F32)).astype(BF16)
+    payload[:, :, 0:quarter] = total.reshape(terms.shape)
+    payload[:, :, quarter:] = terms[...]
 
 
 def last_kernel(
     arrived, hidden, indices,
-    edge_grad, node_grad, grad_send, grad_recv, grad_edge, grad_out, edge_here, sem,
+    edge_grad, node_grad, grad_send, grad_recv, grad_edge, grad_out,
+    edge_here, node_here, grads_here, sems,
 ):
     edges, quarter = edge_grad.shape
     full = join(hidden, 0, edges)
     edge_here[...] = mm_nt(full, join(hidden, edges + 2 * quarter, quarter))
-    (copy,) = fetch(sem, (edge_here, edge_grad))
+    copies = fetch(sems, (edge_here, edge_grad))
+    shape = (16, arrived.shape[0])
+    place = lax.broadcasted_iota(jnp.int32, shape, 1)
+    source = place // CAPACITY
+    core = source % 2
+    side = jnp.where(core == 0, source // 2, source // Z_STRIDE) % 2
+    row = (2 * core + side) * CAPACITY + place % CAPACITY
+    sums = mm(hot(row == lax.broadcasted_iota(jnp.int32, shape, 0)), arrived[:, 0:quarter])
+    outs = (grad_send, grad_recv, grad_edge, grad_out)
+    for i, out in enumerate(outs):
+        grads_here[i] = sums[i * CAPACITY : (i + 1) * CAPACITY, :]
+        copies += fetch(sems.at[1 + i : 2 + i], (grads_here.at[i], out))
     terms = mm_nt(full, join(hidden, edges + quarter, quarter))
     count = node_grad.shape[0]
-    node_grad[...] = pick_sum(hot_by_column(indices[0:1, :], count), terms) + mm(
-        hot_by_column(indices[4:5, :], count), arrived[:, 2 * quarter : 3 * quarter]
-    )
-    shape = (8, arrived.shape[0])
-    place = lax.broadcasted_iota(jnp.int32, shape, 1) % 8
-    pick = hot(place == lax.broadcasted_iota(jnp.int32, shape, 0))
-    sums = mm(pick, arrived[:, 0 : 2 * quarter])
-    grad_send[...] = sums[0:4, 0:quarter]
-    grad_recv[...] = sums[0:4, quarter:]
-    grad_edge[...] = sums[4:8, 0:quarter]
-    grad_out[...] = sums[4:8, quarter:]
-    copy.wait()
+    node_here[...] = pick_sum(hot_by_column(indices[0:1, :], count), terms) + mm(
+        hot_by_column(indices[4:5, :], count), arrived[:, quarter:]
+    )
+    copies += fetch(sems.at[5:6], (node_here, node_grad))
+    for copy in copies:
+        copy.wait()
 
 
 ANY = pl.BlockSpec(memory_space=pl.ANY)
@@ -249,8 +298,11 @@
         scratch=[
             pltpu.VMEM(node.shape, BF16),
             pltpu.VMEM(send_rows.shape, jnp.int32),
+            pltpu.VMEM((slot_count, quarter), BF16),
+            pltpu.SemaphoreType.DMA((2,)),
             pltpu.SemaphoreType.DMA((2,)),
         ],
+        out_places=[ANY],
         flops=2 * slot_count * node_count * quarter,
         limit=60 * 1024 * 1024,
     )
@@ -267,30 +319,48 @@
         places=[SMEM] + [VMEM] * 2,
     )
     shared = lax.all_gather(packed, "feat", axis=0, tiled=False)
-    activation, spread = call(
+    activation, spread, own_hidden = call(
         hidden_kernel,
         (
             sds((edges, quarter), BF16),
             sds((feats, edges + 3 * quarter, quarter), BF16),
+            sds((edges, quarter), BF16),
         ),
         shared, edge_feat, w_send, w_recv, w_edge, w_out, indices,
+        out_places=[VMEM, ANY, VMEM],
+        scratch=[pltpu.SemaphoreType.DMA((3 * feats,)), pltpu.SemaphoreType.DMA((feats,))],
         flops=2 * edges * width * (2 * node_count + slot_count + 4 * quarter),
     )
     hidden = over_feat(spread)
-    kept, given = call(
-        weight_kernel,
-        (sds((2 * width, quarter), F32), sds((2 * width, quarter), F32)),
-        core, shared, edge_feat, indices, activation, spread,
-        places=[SMEM] + [VMEM] * 5,
-        flops=8 * edges * width * quarter,
+    given, kept = (
+        call(
+            functools.partial(weight_kernel, other),
+            (sds((2 * width, quarter), F32),),
+            core, shared, edge_feat, indices, activation, own_hidden,
+            places=[SMEM] + [VMEM] * 5,
+            flops=4 * edges * width * quarter,
+        )[0]
+        for other in (1, 0)
     )
     taken = lax.ppermute(given, "space", [(i, i ^ 1) for i in range(spaces)])
-    (sums,) = call(pair_kernel, (sds((spaces, capacity, 2 * quarter), BF16),), kept, taken)
+    side = jnp.where(core == 0, region // 2, region // Z_STRIDE) % 2
+    mine, given = call(
+        pair_kernel,
+        (sds((width, quarter), F32), sds((width, quarter), BF16)),
+        side, kept, taken,
+        places=[SMEM] + [VMEM] * 2,
+    )
+    taken = lax.ppermute(
+        given, "space", [(i, i ^ (Z_STRIDE if i % 2 else 2)) for i in range(spaces)]
+    )
+    (terms,) = call(
+        slot_kernel,
+        (sds((spaces, capacity, quarter), BF16),),
+        hidden, indices,
+        flops=2 * edges * quarter * (width + 2 * slot_count),
+    )
     (payload,) = call(
-        payload_kernel,
-        (sds((spaces, capacity, 3 * quarter), BF16),),
-        hidden, indices, sums,
-        flops=2 * slot_count * width * (edges + 2 * quarter),
+        payload_kernel, (sds((spaces, capacity, 2 * quarter), BF16),), mine, taken, terms
     )
     returned = over_space(payload)
     small = sds((width // spaces, quarter), F32)
@@ -302,8 +372,13 @@
             small, small, small, small,
         ),
         returned, hidden, indices,
-        out_places=[ANY] + [VMEM] * 5,
-        scratch=[pltpu.VMEM((edges, quarter), F32), pltpu.SemaphoreType.DMA((1,))],
+        out_places=[ANY] * 6,
+        scratch=[
+            pltpu.VMEM((edges, quarter), F32),
+            pltpu.VMEM((node_count, quarter), F32),
+            pltpu.VMEM((4, *small.shape), F32),
+            pltpu.SemaphoreType.DMA((6,)),
+        ],
         flops=2 * edges * (2 * width * quarter + 3 * node_count * quarter),
     )
     return (node_grad, edge_grad, grad_send, grad_recv, grad_edge, grad_out)

time: 92.9 us -> 89.9 us (0.968)
  blocking collectives: 40.4 us -> 35.2 us
  starting transfers between devices: 27.2 us -> 29.2 us
  waiting for transfers between devices: 14.3 us -> 15.7 us
  Pallas kernels: 9.02 us -> 7.78 us
    all_to_all x1, blocking collectives: 27.1 us -> 21.9 us  [over_space(): moved = lax.all_to_all(x, 'space', split_axis=0, concat_axis=0, tiled=True)]
    ppermute x0 -> x1, waiting for transfers between devices: none -> 2.55 us  [local(): lax.ppermute(given, 'space', [(i, i ^ (Z_STRIDE if i % 2 else 2)) for i i...]
    ppermute x0 -> x1, starting transfers between devices: none -> 2.3 us  [local(): lax.ppermute(given, 'space', [(i, i ^ (Z_STRIDE if i % 2 else 2)) for i i...]
    pallas_call x8 -> x10, Pallas kernels: 9.02 us -> 7.78 us  [call(): pl.pallas_call(kernel, out_shape=list(outs), in_specs=list(places or [VME...]
  transfers between devices with their start and end apart: 3 -> 4, of which waited for: 3 -> 4; matrix products, arithmetic and copies ran while one was open for 0% -> 0% of each run, Pallas kernels for 3% -> 3%
where the time goes in v6:
time: 89.9 us; the launch traced here: 89.5 us
  blocking collectives  35.2 us (39%)
  starting transfers between devices  29.2 us (32%)
  waiting for transfers between devices  15.7 us (17%)
  Pallas kernels  7.78 us (9%)
    all_to_all x1, blocking collectives, over_space(): moved = lax.all_to_all(x, 'space', split_axis=0, concat_axis=0, tiled=True)  21.9 us
    all_to_all x1, starting transfers between devices, over_space(): moved = lax.all_to_all(x, 'space', split_axis=0, concat_axis=0, tiled=True)  18.6 us
    all_gather x1, blocking collectives, local(): shared = lax.all_gather(packed, 'feat', axis=0, tiled=False)  13.3 us
    all_to_all x1, waiting for transfers between devices, over_space(): moved = lax.all_to_all(x, 'space', split_axis=0, concat_axis=0, tiled=True)  11.9 us
    pallas_call x10, Pallas kernels, call(): pl.pallas_call(kernel, out_shape=list(outs), in_specs=list(places or [VME...  7.78 us
    ppermute x1, starting transfers between devices, local(): taken = lax.ppermute(given, 'space', [(i, i ^ 1) for i in range(spaces)])  4.8 us
    all_to_all x1, starting transfers between devices, over_feat(): return lax.all_to_all(x, 'feat', split_axis=0, concat_axis=0, tiled=True)  3.52 us
    ppermute x1, waiting for transfers between devices, local(): lax.ppermute(given, 'space', [(i, i ^ (Z_STRIDE if i % 2 else 2)) for i i...  2.55 us
  transfers between devices with their start and end apart: 4, of which 4 were waited for; matrix products, arithmetic and copies ran while one was open for 0% of the time, Pallas kernels for 3%

profile of v6, /device:TPU:1, one launch (start us, length us, event | category | flops | bytes accessed | tf_op | source)
XLA Modules:
  0.0 89.5 jit_solution(8219156283604240725)
XLA Ops:
  0.6 1.8 %shard_map.145 = bf16[512,128]{1,0:T(8,128)(2,1)} custom-call(bf16[256,128]{1,0:T(8,128)(2,1)} %node.3, s32[1,512]{1,0:T(1,128)} %send_rows.1), custom_call_target="tpu_custom_call" | custom-call | flops 33554432 | bytes 198656 | tf_op jit(solution)/shard_map/pallas_call | solution.py:260
  2.4 18.6 %all-to-all-start = ((bf16[128,4,128]{2,1,0:T(4,128)(2,1)}), bf16[128,4,128]{2,1,0:T(4,128)(2,1)S(1)}, u32[]{:S(2)}, u32[]{:S(2)}) async-start(bf16[128,4,128]{2,1,0:T(4,128)(2,1)} %bitcast.10), calls=%async_computation | async-start | bytes 262144 | tf_op jit(solution)/shard_map/all_to_all | solution.py:290
  21.0 0.6 copy-done.5
  21.7 0.0 copy-done.4
  21.7 0.0 copy-done.3
  21.7 0.1 shard_map.146
  21.8 11.9 %all-to-all-done = bf16[128,4,128]{2,1,0:T(4,128)(2,1)S(1)} async-done(((bf16[128,4,128]{2,1,0:T(4,128)(2,1)}), bf16[128,4,128]{2,1,0:T(4,128)(2,1)S(1)}, u32[]{:S(2)}, u32[]{:S(2)}) %all-to-all-start) | async-done | bytes 131104 | tf_op jit(solution)/shard_map/all_to_all | solution.py:290
  33.7 0.1 shard_map.147
  33.8 13.3 %all-gather.1.shared = bf16[4,1020,128]{2,1,0:T(8,128)(2,1)S(1)} all-gather(bf16[1,1020,128]{2,1,0:T(8,128)(2,1)S(1)} %bitcast.6), channel_id=2, replica_groups=mesh['space'=128,'feat'=4] {'feat'}, dimensions={0}, use_global_device_ids=true | all-gather | bytes 1305600 | tf_op jit(solution)/shard_map/all_gather | solution.py:321
  47.2 2.0 %shard_map.148 = (bf16[512,128]{1,0:T(8,128)(2,1)S(1)}, bf16[4,896,128]{2,1,0:T(8,128)(2,1)}, bf16[512,128]{1,0:T(8,128)(2,1)S(1)}) custom-call(bf16[4,1020,128]{2,1,0:T(8,128)(2,1)S(1)} %all-gather.1.shared, bf16[512,512]{1,0:T(8,128)(2,1)S(1)} %copy-done, bf16[512,128]{1,0:T(8,128)(2,1)S(1)} %copy-done.6, bf16[512,128]{1,0:T(8,128)(2,1)S(1)} %copy-done.7, ...), custom_call_target="tpu_custom_call" | custom-call | flops 805306368 | bytes 3289088 | tf_op jit(solution)/shard_map/pallas_call | solution.py:260
  49.2 3.5 %all-to-all-start.1 = ((bf16[4,896,128]{2,1,0:T(8,128)(2,1)}), bf16[4,896,128]{2,1,0:T(8,128)(2,1)S(1)}, u32[]{:S(2)}, u32[]{:S(2)}) async-start(bf16[4,896,128]{2,1,0:T(8,128)(2,1)} %get-tuple-element.25), calls=%async_computation.1 | async-start | bytes 1835008 | tf_op jit(solution)/shard_map/all_to_all | solution.py:287
  52.7 1.0 %shard_map.150 = f32[1024,128]{1,0:T(8,128)S(1)} custom-call(s32[1]{0:T(128)S(6)} %select_n.22.core, bf16[4,1020,128]{2,1,0:T(8,128)(2,1)S(1)} %all-gather.1.shared, bf16[512,512]{1,0:T(8,128)(2,1)S(1)} %copy-done, s32[8,512]{1,0:T(8,128)S(1)} %get-tuple-element.20.indices, bf16[512,128]{1,0:T(8,128)(2,1)S(1)} %get-tuple-element.21.activation, ...), custom_call_target="tpu_custom_call" | custom-call | flops 134217728 | bytes 2371588 | tf_op jit(solution)/shard_map/pallas_call | solution.py:260
  53.7 4.8 %collective-permute-start = (f32[1024,128]{1,0:T(8,128)S(1)}, f32[1024,128]{1,0:T(8,128)S(1)}, u32[]{:S(2)}, u32[]{:S(2)}) collective-permute-start(f32[1024,128]{1,0:T(8,128)S(1)} %shard_map.150), channel_id=1, source_target_pairs={{0,4},{4,0},{8,12},{12,8},{16,20},{20,16},{24,28},{28,24},{32,36},... | collective-permute-start | bytes 1572872 | tf_op jit(solution)/shard_map/ppermute | solution.py:345
  58.6 0.6 shard_map.149.kept
  59.2 0.9 collective-permute-done.taken
  60.0 0.1 shard_map.151
  60.1 2.3 %collective-permute-start.1 = (bf16[512,128]{1,0:T(8,128)(2,1)S(1)}, bf16[512,128]{1,0:T(8,128)(2,1)S(1)}, u32[]{:S(2)}, u32[]{:S(2)}) collective-permute-start(bf16[512,128]{1,0:T(8,128)(2,1)S(1)} %get-tuple-element.24), channel_id=1, source_target_pairs={{0,8},{4,68},{8,0},{12,76},{16,24},{20,84},{24,16},{28,92},{32,40}... | collective-permute-start | bytes 393224 | tf_op jit(solution)/shard_map/ppermute | solution.py:353
  62.4 0.4 all-to-all-done.1.hidden
  62.8 0.7 shard_map.152.terms
  63.5 2.6 %collective-permute-done.1.taken = bf16[512,128]{1,0:T(8,128)(2,1)S(1)} collective-permute-done((bf16[512,128]{1,0:T(8,128)(2,1)S(1)}, bf16[512,128]{1,0:T(8,128)(2,1)S(1)}, u32[]{:S(2)}, u32[]{:S(2)}) %collective-permute-start.1) | collective-permute-done | bytes 131104 | tf_op jit(solution)/shard_map/ppermute | solution.py:353
  66.1 0.1 shard_map.153
  66.2 21.9 %all_to_all.15 = bf16[128,4,256]{2,1,0:T(4,128)(2,1)S(1)} all-to-all(bf16[128,4,256]{2,1,0:T(4,128)(2,1)S(1)} %shard_map.153), channel_id=1, replica_groups=mesh['space'=128,'feat'=4] {'space'}, dimensions={0} | all-to-all | bytes 524288 | tf_op jit(solution)/shard_map/all_to_all | solution.py:290
  88.1 0.1 reshape.45.arrived
  88.1 1.4 %shard_map.154 = (f32[512,128]{1,0:T(8,128)}, f32[256,128]{1,0:T(8,128)}, f32[4,128]{1,0:T(4,128)}, f32[4,128]{1,0:T(4,128)}, f32[4,128]{1,0:T(4,128)}, /*index=5*/f32[4,128]{1,0:T(4,128)}) custom-call(bf16[512,256]{1,0:T(8,128)(2,1)S(1)} %reshape.45.arrived, bf16[4,896,128]{2,1,0:T(8,128)(2,1)S(1)} %all-to-all-done.1.hidden, ...), custom_call_target="tpu_custom_call" | custom-call | flops 234881024 | bytes 1597440 | tf_op jit(solution)/shard_map/pallas_call | solution.py:260
  (17 shorter events, 0.1 us)
Async XLA Ops:
  2.4 18.6 %copy-start.1 = (bf16[256,128]{1,0:T(8,128)(2,1)S(1)}, bf16[256,128]{1,0:T(8,128)(2,1)}, u32[]{:S(2)}) copy-start(bf16[256,128]{1,0:T(8,128)(2,1)} %node.3) | copy-start | bytes 196612
  2.4 18.6 %copy-start.2 = (bf16[256,128]{1,0:T(8,128)(2,1)S(1)}, bf16[256,128]{1,0:T(8,128)(2,1)}, u32[]{:S(2)}) copy-start(bf16[256,128]{1,0:T(8,128)(2,1)} %agg.1) | copy-start | bytes 196612
  2.4 31.3 %all-to-all-start = ((bf16[128,4,128]{2,1,0:T(4,128)(2,1)}), bf16[128,4,128]{2,1,0:T(4,128)(2,1)S(1)}, u32[]{:S(2)}, u32[]{:S(2)}) async-start(bf16[128,4,128]{2,1,0:T(4,128)(2,1)} %bitcast.10), calls=%async_computation | async-start | bytes 262144 | tf_op jit(solution)/shard_map/all_to_all | solution.py:290
  21.0 0.7 copy-start.5
  21.0 0.7 copy-start.4
  21.0 0.7 copy-start.3
  33.8 13.4 %copy-start = (bf16[512,512]{1,0:T(8,128)(2,1)S(1)}, bf16[512,512]{1,0:T(8,128)(2,1)}, u32[]{:S(2)}) copy-start(bf16[512,512]{1,0:T(8,128)(2,1)} %edge_feat.5) | copy-start | bytes 1572868
  33.8 13.4 %copy-start.6 = (bf16[512,128]{1,0:T(8,128)(2,1)S(1)}, bf16[512,128]{1,0:T(8,128)(2,1)}, u32[]{:S(2)}) copy-start(bf16[512,128]{1,0:T(8,128)(2,1)} %w_send.1) | copy-start | bytes 393220
  33.8 13.3 %copy-start.7 = (bf16[512,128]{1,0:T(8,128)(2,1)S(1)}, bf16[512,128]{1,0:T(8,128)(2,1)}, u32[]{:S(2)}) copy-start(bf16[512,128]{1,0:T(8,128)(2,1)} %w_recv.1) | copy-start | bytes 393220
  33.8 13.3 %copy-start.8 = (bf16[512,128]{1,0:T(8,128)(2,1)S(1)}, bf16[512,128]{1,0:T(8,128)(2,1)}, u32[]{:S(2)}) copy-start(bf16[512,128]{1,0:T(8,128)(2,1)} %w_edge.1) | copy-start | bytes 393220
  33.8 13.3 %copy-start.9 = (bf16[512,128]{1,0:T(8,128)(2,1)S(1)}, bf16[512,128]{1,0:T(8,128)(2,1)}, u32[]{:S(2)}) copy-start(bf16[512,128]{1,0:T(8,128)(2,1)} %w_out.1) | copy-start | bytes 393220
  49.2 13.6 %all-to-all-start.1 = ((bf16[4,896,128]{2,1,0:T(8,128)(2,1)}), bf16[4,896,128]{2,1,0:T(8,128)(2,1)S(1)}, u32[]{:S(2)}, u32[]{:S(2)}) async-start(bf16[4,896,128]{2,1,0:T(8,128)(2,1)} %get-tuple-element.25), calls=%async_computation.1 | async-start | bytes 1835008 | tf_op jit(solution)/shard_map/all_to_all | solution.py:287
  53.7 6.3 %collective-permute-start = (f32[1024,128]{1,0:T(8,128)S(1)}, f32[1024,128]{1,0:T(8,128)S(1)}, u32[]{:S(2)}, u32[]{:S(2)}) collective-permute-start(f32[1024,128]{1,0:T(8,128)S(1)} %shard_map.150), channel_id=1, source_target_pairs={{0,4},{4,0},{8,12},{12,8},{16,20},{20,16},{24,28},{28,24},{32,36},... | collective-permute-start | bytes 1572872 | tf_op jit(solution)/shard_map/ppermute | solution.py:345
  60.1 6.0 %collective-permute-start.1 = (bf16[512,128]{1,0:T(8,128)(2,1)S(1)}, bf16[512,128]{1,0:T(8,128)(2,1)S(1)}, u32[]{:S(2)}, u32[]{:S(2)}) collective-permute-start(bf16[512,128]{1,0:T(8,128)(2,1)S(1)} %get-tuple-element.24), channel_id=1, source_target_pairs={{0,8},{4,68},{8,0},{12,76},{16,24},{20,84},{24,16},{28,92},{32,40}... | collective-permute-start | bytes 393224 | tf_op jit(solution)/shard_map/ppermute | solution.py:353

commit v7 on v6

--- a/solution.py
+++ b/solution.py
@@ -203,13 +203,18 @@
     given[...] = jnp.where(even, second, first).astype(BF16)
 
 
-def slot_kernel(hidden, indices, terms):
+def slot_kernel(hidden, indices, terms, edge_grad, recv_part, edge_here, sem):
     spaces, capacity, quarter = terms.shape
     edges = indices.shape[1]
-    w_send = join(hidden, edges, quarter)
-    by_edge = mm_nt(join(hidden, 0, edges), w_send)
+    full = join(hidden, 0, edges)
+    edge_here[...] = mm_nt(full, join(hidden, edges + 2 * quarter, quarter))
+    (copy,) = fetch(sem, (edge_here, edge_grad))
+    by_edge = mm_nt(full, join(hidden, edges, quarter))
     sums = pick_sum(hot_by_column(indices[1:2, :], spaces * capacity), by_edge)
     terms[...] = sums.astype(BF16).reshape(terms.shape)
+    by_edge = mm_nt(full, join(hidden, edges + quarter, quarter))
+    recv_part[...] = pick_sum(hot_by_column(indices[0:1, :], recv_part.shape[0]), by_edge)
+    copy.wait()
 
 
 def payload_kernel(mine, taken, terms, payload):
@@ -220,14 +225,13 @@
 
 
 def last_kernel(
-    arrived, hidden, indices,
-    edge_grad, node_grad, grad_send, grad_recv, grad_edge, grad_out,
-    edge_here, node_here, grads_here, sems,
+    arrived, indices, recv_part,
+    node_grad, grad_send, grad_recv, grad_edge, grad_out, node_here, grads_here, sems,
 ):
-    edges, quarter = edge_grad.shape
-    full = join(hidden, 0, edges)
-    edge_here[...] = mm_nt(full, join(hidden, edges + 2 * quarter, quarter))
-    copies = fetch(sems, (edge_here, edge_grad))
+    count, quarter = node_grad.shape
+    back = mm(hot_by_column(indices[4:5, :], count), arrived[:, quarter:])
+    node_here[...] = recv_part[...] + back
+    copies = fetch(sems.at[4:5], (node_here, node_grad))
     shape = (16, arrived.shape[0])
     place = lax.broadcasted_iota(jnp.int32, shape, 1)
     source = place // CAPACITY
@@ -238,13 +242,7 @@
     outs = (grad_send, grad_recv, grad_edge, grad_out)
     for i, out in enumerate(outs):
         grads_here[i] = sums[i * CAPACITY : (i + 1) * CAPACITY, :]
-        copies += fetch(sems.at[1 + i : 2 + i], (grads_here.at[i], out))
-    terms = mm_nt(full, join(hidden, edges + quarter, quarter))
-    count = node_grad.shape[0]
-    node_here[...] = pick_sum(hot_by_column(indices[0:1, :], count), terms) + mm(
-        hot_by_column(indices[4:5, :], count), arrived[:, quarter:]
-    )
-    copies += fetch(sems.at[5:6], (node_here, node_grad))
+        copies += fetch(sems.at[i : i + 1], (grads_here.at[i], out))
     for copy in copies:
         copy.wait()
 
@@ -353,33 +351,34 @@
     taken = lax.ppermute(
         given, "space", [(i, i ^ (Z_STRIDE if i % 2 else 2)) for i in range(spaces)]
     )
-    (terms,) = call(
+    terms, edge_grad, recv_part = call(
         slot_kernel,
-        (sds((spaces, capacity, quarter), BF16),),
+        (
+            sds((spaces, capacity, quarter), BF16),
+            sds((edges, quarter), F32),
+            sds((node_count, quarter), F32),
+        ),
         hidden, indices,
-        flops=2 * edges * quarter * (width + 2 * slot_count),
+        out_places=[VMEM, ANY, VMEM],
+        scratch=[pltpu.VMEM((edges, quarter), F32), pltpu.SemaphoreType.DMA((1,))],
+        flops=2 * edges * quarter * (3 * width + 2 * slot_count + 2 * node_count),
     )
     (payload,) = call(
         payload_kernel, (sds((spaces, capacity, 2 * quarter), BF16),), mine, taken, terms
     )
     returned = over_space(payload)
     small = sds((width // spaces, quarter), F32)
-    edge_grad, node_grad, grad_send, grad_recv, grad_edge, grad_out = call(
+    node_grad, grad_send, grad_recv, grad_edge, grad_out = call(
         last_kernel,
-        (
-            sds((edges, quarter), F32),
-            sds((node_count, quarter), F32),
-            small, small, small, small,
-        ),
-        returned, hidden, indices,
-        out_places=[ANY] * 6,
+        (sds((node_count, quarter), F32), small, small, small, small),
+        returned, indices, recv_part,
+        out_places=[ANY] * 5,
         scratch=[
-            pltpu.VMEM((edges, quarter), F32),
             pltpu.VMEM((node_count, quarter), F32),
             pltpu.VMEM((4, *small.shape), F32),
-            pltpu.SemaphoreType.DMA((6,)),
+            pltpu.SemaphoreType.DMA((5,)),
         ],
-        flops=2 * edges * (2 * width * quarter + 3 * node_count * quarter),
+        flops=2 * slot_count * quarter * (node_count + 16),
     )
     return (node_grad, edge_grad, grad_send, grad_recv, grad_edge, grad_out)
 

time: 89.9 us -> 90.3 us (level)
  transfers between devices with their start and end apart: 4 -> 4, of which waited for: 4 -> 4; matrix products, arithmetic and copies ran while one was open for 0% -> 0% of each run, Pallas kernels for 3% -> 4%
where the time goes in v7:
time: 90.3 us; the launch traced here: 89.9 us
  blocking collectives  36 us (40%)
  starting transfers between devices  29.2 us (32%)
  waiting for transfers between devices  14.9 us (17%)
  Pallas kernels  8.14 us (9%)
    all_to_all x1, blocking collectives, over_space(): moved = lax.all_to_all(x, 'space', split_axis=0, concat_axis=0, tiled=True)  22.7 us
    all_to_all x1, starting transfers between devices, over_space(): moved = lax.all_to_all(x, 'space', split_axis=0, concat_axis=0, tiled=True)  18.6 us
    all_gather x1, blocking collectives, local(): shared = lax.all_gather(packed, 'feat', axis=0, tiled=False)  13.3 us
    all_to_all x1, waiting for transfers between devices, over_space(): moved = lax.all_to_all(x, 'space', split_axis=0, concat_axis=0, tiled=True)  11.9 us
    pallas_call x10, Pallas kernels, call(): pl.pallas_call(kernel, out_shape=list(outs), in_specs=list(places or [VME...  8.14 us
    ppermute x1, starting transfers between devices, local(): taken = lax.ppermute(given, 'space', [(i, i ^ 1) for i in range(spaces)])  4.8 us
    all_to_all x1, starting transfers between devices, over_feat(): return lax.all_to_all(x, 'feat', split_axis=0, concat_axis=0, tiled=True)  3.52 us
    ppermute x1, starting transfers between devices, local(): lax.ppermute(given, 'space', [(i, i ^ (Z_STRIDE if i % 2 else 2)) for i i...  2.3 us
  transfers between devices with their start and end apart: 4, of which 4 were waited for; matrix products, arithmetic and copies ran while one was open for 0% of the time, Pallas kernels for 4%

profile of v7, /device:TPU:1, one launch (start us, length us, event | category | flops | bytes accessed | tf_op | source)
XLA Modules:
  0.0 89.9 jit_solution(1298479840401038148)
XLA Ops:
  0.6 1.8 %shard_map.145 = bf16[512,128]{1,0:T(8,128)(2,1)} custom-call(bf16[256,128]{1,0:T(8,128)(2,1)} %node.3, s32[1,512]{1,0:T(1,128)} %send_rows.1), custom_call_target="tpu_custom_call" | custom-call | flops 33554432 | bytes 198656 | tf_op jit(solution)/shard_map/pallas_call | solution.py:258
  2.4 18.6 %all-to-all-start = ((bf16[128,4,128]{2,1,0:T(4,128)(2,1)}), bf16[128,4,128]{2,1,0:T(4,128)(2,1)S(1)}, u32[]{:S(2)}, u32[]{:S(2)}) async-start(bf16[128,4,128]{2,1,0:T(4,128)(2,1)} %bitcast.10), calls=%async_computation | async-start | bytes 262144 | tf_op jit(solution)/shard_map/all_to_all | solution.py:288
  21.0 0.6 copy-done.5
  21.7 0.0 copy-done.4
  21.7 0.0 copy-done.3
  21.7 0.1 shard_map.146
  21.8 11.9 %all-to-all-done = bf16[128,4,128]{2,1,0:T(4,128)(2,1)S(1)} async-done(((bf16[128,4,128]{2,1,0:T(4,128)(2,1)}), bf16[128,4,128]{2,1,0:T(4,128)(2,1)S(1)}, u32[]{:S(2)}, u32[]{:S(2)}) %all-to-all-start) | async-done | bytes 131104 | tf_op jit(solution)/shard_map/all_to_all | solution.py:288
  33.7 0.1 shard_map.147
  33.8 13.3 %all-gather.1.shared = bf16[4,1020,128]{2,1,0:T(8,128)(2,1)S(1)} all-gather(bf16[1,1020,128]{2,1,0:T(8,128)(2,1)S(1)} %bitcast.6), channel_id=2, replica_groups=mesh['space'=128,'feat'=4] {'feat'}, dimensions={0}, use_global_device_ids=true | all-gather | bytes 1305600 | tf_op jit(solution)/shard_map/all_gather | solution.py:319
  47.2 2.0 %shard_map.148 = (bf16[512,128]{1,0:T(8,128)(2,1)S(1)}, bf16[4,896,128]{2,1,0:T(8,128)(2,1)}, bf16[512,128]{1,0:T(8,128)(2,1)S(1)}) custom-call(bf16[4,1020,128]{2,1,0:T(8,128)(2,1)S(1)} %all-gather.1.shared, bf16[512,512]{1,0:T(8,128)(2,1)S(1)} %copy-done, bf16[512,128]{1,0:T(8,128)(2,1)S(1)} %copy-done.6, bf16[512,128]{1,0:T(8,128)(2,1)S(1)} %copy-done.7, ...), custom_call_target="tpu_custom_call" | custom-call | flops 805306368 | bytes 3289088 | tf_op jit(solution)/shard_map/pallas_call | solution.py:258
  49.2 3.5 %all-to-all-start.1 = ((bf16[4,896,128]{2,1,0:T(8,128)(2,1)}), bf16[4,896,128]{2,1,0:T(8,128)(2,1)S(1)}, u32[]{:S(2)}, u32[]{:S(2)}) async-start(bf16[4,896,128]{2,1,0:T(8,128)(2,1)} %get-tuple-element.27), calls=%async_computation.1 | async-start | bytes 1835008 | tf_op jit(solution)/shard_map/all_to_all | solution.py:285
  52.7 1.0 %shard_map.150 = f32[1024,128]{1,0:T(8,128)S(1)} custom-call(s32[1]{0:T(128)S(6)} %select_n.22.core, bf16[4,1020,128]{2,1,0:T(8,128)(2,1)S(1)} %all-gather.1.shared, bf16[512,512]{1,0:T(8,128)(2,1)S(1)} %copy-done, s32[8,512]{1,0:T(8,128)S(1)} %get-tuple-element.22.indices, bf16[512,128]{1,0:T(8,128)(2,1)S(1)} %get-tuple-element.23.activation, ...), custom_call_target="tpu_custom_call" | custom-call | flops 134217728 | bytes 2371588 | tf_op jit(solution)/shard_map/pallas_call | solution.py:258
  53.7 4.8 %collective-permute-start = (f32[1024,128]{1,0:T(8,128)S(1)}, f32[1024,128]{1,0:T(8,128)S(1)}, u32[]{:S(2)}, u32[]{:S(2)}) collective-permute-start(f32[1024,128]{1,0:T(8,128)S(1)} %shard_map.150), channel_id=1, source_target_pairs={{0,4},{4,0},{8,12},{12,8},{16,20},{20,16},{24,28},{28,24},{32,36},... | collective-permute-start | bytes 1572872 | tf_op jit(solution)/shard_map/ppermute | solution.py:343
  58.6 0.6 shard_map.149.kept
  59.2 0.8 collective-permute-done.taken
  60.0 0.1 shard_map.151
  60.1 2.3 %collective-permute-start.1 = (bf16[512,128]{1,0:T(8,128)(2,1)S(1)}, bf16[512,128]{1,0:T(8,128)(2,1)S(1)}, u32[]{:S(2)}, u32[]{:S(2)}) collective-permute-start(bf16[512,128]{1,0:T(8,128)(2,1)S(1)} %get-tuple-element.26), channel_id=1, source_target_pairs={{0,8},{4,68},{8,0},{12,76},{16,24},{20,84},{24,16},{28,92},{32,40}... | collective-permute-start | bytes 393224 | tf_op jit(solution)/shard_map/ppermute | solution.py:351
  62.4 0.4 all-to-all-done.1.hidden
  62.8 1.5 %shard_map.152 = (bf16[128,4,128]{2,1,0:T(4,128)(2,1)S(1)}, f32[512,128]{1,0:T(8,128)}, f32[256,128]{1,0:T(8,128)S(1)}) custom-call(bf16[4,896,128]{2,1,0:T(8,128)(2,1)S(1)} %all-to-all-done.1.hidden, s32[8,512]{1,0:T(8,128)S(1)} %get-tuple-element.22.indices), custom_call_target="tpu_custom_call" | custom-call | flops 402653184 | bytes 1458176 | tf_op jit(solution)/shard_map/pallas_call | solution.py:258
  64.4 1.8 %collective-permute-done.1.taken = bf16[512,128]{1,0:T(8,128)(2,1)S(1)} collective-permute-done((bf16[512,128]{1,0:T(8,128)(2,1)S(1)}, bf16[512,128]{1,0:T(8,128)(2,1)S(1)}, u32[]{:S(2)}, u32[]{:S(2)}) %collective-permute-start.1) | collective-permute-done | bytes 131104 | tf_op jit(solution)/shard_map/ppermute | solution.py:351
  66.1 0.1 shard_map.153
  66.2 22.7 %all_to_all.15 = bf16[128,4,256]{2,1,0:T(4,128)(2,1)S(1)} all-to-all(bf16[128,4,256]{2,1,0:T(4,128)(2,1)S(1)} %shard_map.153), channel_id=1, replica_groups=mesh['space'=128,'feat'=4] {'space'}, dimensions={0} | all-to-all | bytes 524288 | tf_op jit(solution)/shard_map/all_to_all | solution.py:288
  88.9 0.1 reshape.45.arrived
  88.9 0.9 %shard_map.154 = (f32[256,128]{1,0:T(8,128)}, f32[4,128]{1,0:T(4,128)}, f32[4,128]{1,0:T(4,128)}, f32[4,128]{1,0:T(4,128)}, f32[4,128]{1,0:T(4,128)}) custom-call(bf16[512,256]{1,0:T(8,128)(2,1)S(1)} %reshape.45.arrived, s32[8,512]{1,0:T(8,128)S(1)} %get-tuple-element.22.indices, f32[256,128]{1,0:T(8,128)S(1)} %get-tuple-element.29.recv_part), custom_call_target="tpu_custom_call" | custom-call | flops 35651584 | bytes 548864 | tf_op jit(solution)/shard_map/pallas_call | solution.py:258
  (17 shorter events, 0.1 us)
Async XLA Ops:
  2.4 18.6 %copy-start.1 = (bf16[256,128]{1,0:T(8,128)(2,1)S(1)}, bf16[256,128]{1,0:T(8,128)(2,1)}, u32[]{:S(2)}) copy-start(bf16[256,128]{1,0:T(8,128)(2,1)} %node.3) | copy-start | bytes 196612
  2.4 18.6 %copy-start.2 = (bf16[256,128]{1,0:T(8,128)(2,1)S(1)}, bf16[256,128]{1,0:T(8,128)(2,1)}, u32[]{:S(2)}) copy-start(bf16[256,128]{1,0:T(8,128)(2,1)} %agg.1) | copy-start | bytes 196612
  2.4 31.3 %all-to-all-start = ((bf16[128,4,128]{2,1,0:T(4,128)(2,1)}), bf16[128,4,128]{2,1,0:T(4,128)(2,1)S(1)}, u32[]{:S(2)}, u32[]{:S(2)}) async-start(bf16[128,4,128]{2,1,0:T(4,128)(2,1)} %bitcast.10), calls=%async_computation | async-start | bytes 262144 | tf_op jit(solution)/shard_map/all_to_all | solution.py:288
  21.0 0.7 copy-start.5
  21.0 0.7 copy-start.4
  21.0 0.7 copy-start.3
  33.8 13.4 %copy-start = (bf16[512,512]{1,0:T(8,128)(2,1)S(1)}, bf16[512,512]{1,0:T(8,128)(2,1)}, u32[]{:S(2)}) copy-start(bf16[512,512]{1,0:T(8,128)(2,1)} %edge_feat.5) | copy-start | bytes 1572868
  33.8 13.4 %copy-start.6 = (bf16[512,128]{1,0:T(8,128)(2,1)S(1)}, bf16[512,128]{1,0:T(8,128)(2,1)}, u32[]{:S(2)}) copy-start(bf16[512,128]{1,0:T(8,128)(2,1)} %w_send.1) | copy-start | bytes 393220
  33.8 13.3 %copy-start.7 = (bf16[512,128]{1,0:T(8,128)(2,1)S(1)}, bf16[512,128]{1,0:T(8,128)(2,1)}, u32[]{:S(2)}) copy-start(bf16[512,128]{1,0:T(8,128)(2,1)} %w_recv.1) | copy-start | bytes 393220
  33.8 13.3 %copy-start.8 = (bf16[512,128]{1,0:T(8,128)(2,1)S(1)}, bf16[512,128]{1,0:T(8,128)(2,1)}, u32[]{:S(2)}) copy-start(bf16[512,128]{1,0:T(8,128)(2,1)} %w_edge.1) | copy-start | bytes 393220
  33.8 13.3 %copy-start.9 = (bf16[512,128]{1,0:T(8,128)(2,1)S(1)}, bf16[512,128]{1,0:T(8,128)(2,1)}, u32[]{:S(2)}) copy-start(bf16[512,128]{1,0:T(8,128)(2,1)} %w_out.1) | copy-start | bytes 393220
  49.2 13.6 %all-to-all-start.1 = ((bf16[4,896,128]{2,1,0:T(8,128)(2,1)}), bf16[4,896,128]{2,1,0:T(8,128)(2,1)S(1)}, u32[]{:S(2)}, u32[]{:S(2)}) async-start(bf16[4,896,128]{2,1,0:T(8,128)(2,1)} %get-tuple-element.27), calls=%async_computation.1 | async-start | bytes 1835008 | tf_op jit(solution)/shard_map/all_to_all | solution.py:285
  53.7 6.3 %collective-permute-start = (f32[1024,128]{1,0:T(8,128)S(1)}, f32[1024,128]{1,0:T(8,128)S(1)}, u32[]{:S(2)}, u32[]{:S(2)}) collective-permute-start(f32[1024,128]{1,0:T(8,128)S(1)} %shard_map.150), channel_id=1, source_target_pairs={{0,4},{4,0},{8,12},{12,8},{16,20},{20,16},{24,28},{28,24},{32,36},... | collective-permute-start | bytes 1572872 | tf_op jit(solution)/shard_map/ppermute | solution.py:343
  60.1 6.0 %collective-permute-start.1 = (bf16[512,128]{1,0:T(8,128)(2,1)S(1)}, bf16[512,128]{1,0:T(8,128)(2,1)S(1)}, u32[]{:S(2)}, u32[]{:S(2)}) collective-permute-start(bf16[512,128]{1,0:T(8,128)(2,1)S(1)} %get-tuple-element.26), channel_id=1, source_target_pairs={{0,8},{4,68},{8,0},{12,76},{16,24},{20,84},{24,16},{28,92},{32,40}... | collective-permute-start | bytes 393224 | tf_op jit(solution)/shard_map/ppermute | solution.py:351

commit v8 on v6

--- a/solution.py
+++ b/solution.py
@@ -138,21 +138,26 @@
     at_node = mm(join(shared, 0, count), jnp.concatenate([w_recv[...], w_send[...]], axis=1))
     at_agg = mm(join(shared, count, count), w_out[...])
     at_slot = mm(join(shared, 2 * count, slot_count), w_send[...])
-    receive = hot_by_row(indices[0:1, :], count)
-    at_edge = pick_sum(receive, jnp.concatenate([at_node[:, 0:quarter], at_agg], axis=1))
-    act_grad = at_edge[:, quarter:]
-    pre_act = (
-        pick_sum(hot_by_row(indices[2:3, :], slot_count), at_slot)
-        + pick_sum(hot_by_row(indices[3:4, :], count), at_node[:, quarter:])
-        + at_edge[:, 0:quarter]
-        + mm(edge_feat[...], w_edge[...])
-    )
-    gate = jax.nn.sigmoid(pre_act)
-    activation[...] = (pre_act * gate).astype(BF16)
-    hidden[...] = (act_grad * gate * (1.0 + pre_act * (1.0 - gate))).astype(BF16)
-    rows = fetch(
-        hidden_sems, *((hidden, spread.at[q, 0:edges, :]) for q in range(feats))
-    )
+    at_row = jnp.concatenate([at_node[:, 0:quarter], at_agg], axis=1)
+    size = edges // 2
+    rows = []
+    for half in range(2):
+        part = slice(half * size, (half + 1) * size)
+        at_edge = pick_sum(hot_by_row(indices[0:1, part], count), at_row)
+        act_grad = at_edge[:, quarter:]
+        pre_act = (
+            pick_sum(hot_by_row(indices[2:3, part], slot_count), at_slot)
+            + pick_sum(hot_by_row(indices[3:4, part], count), at_node[:, quarter:])
+            + at_edge[:, 0:quarter]
+            + mm(edge_feat[part, :], w_edge[...])
+        )
+        gate = jax.nn.sigmoid(pre_act)
+        hidden[part, :] = (act_grad * gate * (1.0 + pre_act * (1.0 - gate))).astype(BF16)
+        rows += fetch(
+            hidden_sems.at[half * feats : (half + 1) * feats],
+            *((hidden.at[part, :], spread.at[q, part, :]) for q in range(feats)),
+        )
+        activation[part, :] = (pre_act * gate).astype(BF16)
     for copy in (*rows, *blocks):
         copy.wait()
 
@@ -328,7 +333,7 @@
         ),
         shared, edge_feat, w_send, w_recv, w_edge, w_out, indices,
         out_places=[VMEM, ANY, VMEM],
-        scratch=[pltpu.SemaphoreType.DMA((3 * feats,)), pltpu.SemaphoreType.DMA((feats,))],
+        scratch=[pltpu.SemaphoreType.DMA((3 * feats,)), pltpu.SemaphoreType.DMA((2 * feats,))],
         flops=2 * edges * width * (2 * node_count + slot_count + 4 * quarter),
     )
     hidden = over_feat(spread)

time: 89.9 us -> 90 us (level)
  no operation moved by 1% of the time
where the time goes in v8:
time: 90 us; the launch traced here: 89.5 us
  blocking collectives  35.2 us (39%)
  starting transfers between devices  29.2 us (32%)
  waiting for transfers between devices  15.7 us (17%)
  Pallas kernels  7.81 us (9%)
    all_to_all x1, blocking collectives, over_space(): moved = lax.all_to_all(x, 'space', split_axis=0, concat_axis=0, tiled=True)  21.9 us
    all_to_all x1, starting transfers between devices, over_space(): moved = lax.all_to_all(x, 'space', split_axis=0, concat_axis=0, tiled=True)  18.6 us
    all_gather x1, blocking collectives, local(): shared = lax.all_gather(packed, 'feat', axis=0, tiled=False)  13.3 us
    all_to_all x1, waiting for transfers between devices, over_space(): moved = lax.all_to_all(x, 'space', split_axis=0, concat_axis=0, tiled=True)  11.9 us
    pallas_call x10, Pallas kernels, call(): pl.pallas_call(kernel, out_shape=list(outs), in_specs=list(places or [VME...  7.81 us
    ppermute x1, starting transfers between devices, local(): taken = lax.ppermute(given, 'space', [(i, i ^ 1) for i in range(spaces)])  4.79 us
    all_to_all x1, starting transfers between devices, over_feat(): return lax.all_to_all(x, 'feat', split_axis=0, concat_axis=0, tiled=True)  3.52 us
    ppermute x1, waiting for transfers between devices, local(): lax.ppermute(given, 'space', [(i, i ^ (Z_STRIDE if i % 2 else 2)) for i i...  2.55 us
  transfers between devices with their start and end apart: 4, of which 4 were waited for; matrix products, arithmetic and copies ran while one was open for 0% of the time, Pallas kernels for 3%

profile of v8, /device:TPU:1, one launch (start us, length us, event | category | flops | bytes accessed | tf_op | source)
XLA Modules:
  0.0 89.5 jit_solution(13835560131759946751)
XLA Ops:
  0.6 1.8 %shard_map.145 = bf16[512,128]{1,0:T(8,128)(2,1)} custom-call(bf16[256,128]{1,0:T(8,128)(2,1)} %node.3, s32[1,512]{1,0:T(1,128)} %send_rows.1), custom_call_target="tpu_custom_call" | custom-call | flops 33554432 | bytes 198656 | tf_op jit(solution)/shard_map/pallas_call | solution.py:265
  2.4 18.6 %all-to-all-start = ((bf16[128,4,128]{2,1,0:T(4,128)(2,1)}), bf16[128,4,128]{2,1,0:T(4,128)(2,1)S(1)}, u32[]{:S(2)}, u32[]{:S(2)}) async-start(bf16[128,4,128]{2,1,0:T(4,128)(2,1)} %bitcast.10), calls=%async_computation | async-start | bytes 262144 | tf_op jit(solution)/shard_map/all_to_all | solution.py:295
  21.0 0.6 copy-done.5
  21.7 0.0 copy-done.4
  21.7 0.0 copy-done.3
  21.7 0.1 shard_map.146
  21.8 11.9 %all-to-all-done = bf16[128,4,128]{2,1,0:T(4,128)(2,1)S(1)} async-done(((bf16[128,4,128]{2,1,0:T(4,128)(2,1)}), bf16[128,4,128]{2,1,0:T(4,128)(2,1)S(1)}, u32[]{:S(2)}, u32[]{:S(2)}) %all-to-all-start) | async-done | bytes 131104 | tf_op jit(solution)/shard_map/all_to_all | solution.py:295
  33.7 0.1 shard_map.147
  33.8 13.3 %all-gather.1.shared = bf16[4,1020,128]{2,1,0:T(8,128)(2,1)S(1)} all-gather(bf16[1,1020,128]{2,1,0:T(8,128)(2,1)S(1)} %bitcast.6), channel_id=2, replica_groups=mesh['space'=128,'feat'=4] {'feat'}, dimensions={0}, use_global_device_ids=true | all-gather | bytes 1305600 | tf_op jit(solution)/shard_map/all_gather | solution.py:326
  47.2 2.0 %shard_map.148 = (bf16[512,128]{1,0:T(8,128)(2,1)S(1)}, bf16[4,896,128]{2,1,0:T(8,128)(2,1)}, bf16[512,128]{1,0:T(8,128)(2,1)S(1)}) custom-call(bf16[4,1020,128]{2,1,0:T(8,128)(2,1)S(1)} %all-gather.1.shared, bf16[512,512]{1,0:T(8,128)(2,1)S(1)} %copy-done, bf16[512,128]{1,0:T(8,128)(2,1)S(1)} %copy-done.6, bf16[512,128]{1,0:T(8,128)(2,1)S(1)} %copy-done.7, ...), custom_call_target="tpu_custom_call" | custom-call | flops 805306368 | bytes 3289088 | tf_op jit(solution)/shard_map/pallas_call | solution.py:265
  49.2 3.5 %all-to-all-start.1 = ((bf16[4,896,128]{2,1,0:T(8,128)(2,1)}), bf16[4,896,128]{2,1,0:T(8,128)(2,1)S(1)}, u32[]{:S(2)}, u32[]{:S(2)}) async-start(bf16[4,896,128]{2,1,0:T(8,128)(2,1)} %get-tuple-element.25), calls=%async_computation.1 | async-start | bytes 1835008 | tf_op jit(solution)/shard_map/all_to_all | solution.py:292
  52.7 1.0 %shard_map.150 = f32[1024,128]{1,0:T(8,128)S(1)} custom-call(s32[1]{0:T(128)S(6)} %select_n.22.core, bf16[4,1020,128]{2,1,0:T(8,128)(2,1)S(1)} %all-gather.1.shared, bf16[512,512]{1,0:T(8,128)(2,1)S(1)} %copy-done, s32[8,512]{1,0:T(8,128)S(1)} %get-tuple-element.20.indices, bf16[512,128]{1,0:T(8,128)(2,1)S(1)} %get-tuple-element.21.activation, ...), custom_call_target="tpu_custom_call" | custom-call | flops 134217728 | bytes 2371588 | tf_op jit(solution)/shard_map/pallas_call | solution.py:265
  53.7 4.8 %collective-permute-start = (f32[1024,128]{1,0:T(8,128)S(1)}, f32[1024,128]{1,0:T(8,128)S(1)}, u32[]{:S(2)}, u32[]{:S(2)}) collective-permute-start(f32[1024,128]{1,0:T(8,128)S(1)} %shard_map.150), channel_id=1, source_target_pairs={{0,4},{4,0},{8,12},{12,8},{16,20},{20,16},{24,28},{28,24},{32,36},... | collective-permute-start | bytes 1572872 | tf_op jit(solution)/shard_map/ppermute | solution.py:350
  58.6 0.6 shard_map.149.kept
  59.2 0.9 collective-permute-done.taken
  60.0 0.1 shard_map.151
  60.1 2.3 %collective-permute-start.1 = (bf16[512,128]{1,0:T(8,128)(2,1)S(1)}, bf16[512,128]{1,0:T(8,128)(2,1)S(1)}, u32[]{:S(2)}, u32[]{:S(2)}) collective-permute-start(bf16[512,128]{1,0:T(8,128)(2,1)S(1)} %get-tuple-element.24), channel_id=1, source_target_pairs={{0,8},{4,68},{8,0},{12,76},{16,24},{20,84},{24,16},{28,92},{32,40}... | collective-permute-start | bytes 393224 | tf_op jit(solution)/shard_map/ppermute | solution.py:358
  62.4 0.4 all-to-all-done.1.hidden
  62.8 0.7 shard_map.152.terms
  63.6 2.6 %collective-permute-done.1.taken = bf16[512,128]{1,0:T(8,128)(2,1)S(1)} collective-permute-done((bf16[512,128]{1,0:T(8,128)(2,1)S(1)}, bf16[512,128]{1,0:T(8,128)(2,1)S(1)}, u32[]{:S(2)}, u32[]{:S(2)}) %collective-permute-start.1) | collective-permute-done | bytes 131104 | tf_op jit(solution)/shard_map/ppermute | solution.py:358
  66.1 0.1 shard_map.153
  66.2 21.9 %all_to_all.15 = bf16[128,4,256]{2,1,0:T(4,128)(2,1)S(1)} all-to-all(bf16[128,4,256]{2,1,0:T(4,128)(2,1)S(1)} %shard_map.153), channel_id=1, replica_groups=mesh['space'=128,'feat'=4] {'space'}, dimensions={0} | all-to-all | bytes 524288 | tf_op jit(solution)/shard_map/all_to_all | solution.py:295
  88.1 0.1 reshape.45.arrived
  88.2 1.4 %shard_map.154 = (f32[512,128]{1,0:T(8,128)}, f32[256,128]{1,0:T(8,128)}, f32[4,128]{1,0:T(4,128)}, f32[4,128]{1,0:T(4,128)}, f32[4,128]{1,0:T(4,128)}, /*index=5*/f32[4,128]{1,0:T(4,128)}) custom-call(bf16[512,256]{1,0:T(8,128)(2,1)S(1)} %reshape.45.arrived, bf16[4,896,128]{2,1,0:T(8,128)(2,1)S(1)} %all-to-all-done.1.hidden, ...), custom_call_target="tpu_custom_call" | custom-call | flops 234881024 | bytes 1597440 | tf_op jit(solution)/shard_map/pallas_call | solution.py:265
  (17 shorter events, 0.1 us)
Async XLA Ops:
  2.4 18.6 %copy-start.1 = (bf16[256,128]{1,0:T(8,128)(2,1)S(1)}, bf16[256,128]{1,0:T(8,128)(2,1)}, u32[]{:S(2)}) copy-start(bf16[256,128]{1,0:T(8,128)(2,1)} %node.3) | copy-start | bytes 196612
  2.4 18.6 %copy-start.2 = (bf16[256,128]{1,0:T(8,128)(2,1)S(1)}, bf16[256,128]{1,0:T(8,128)(2,1)}, u32[]{:S(2)}) copy-start(bf16[256,128]{1,0:T(8,128)(2,1)} %agg.1) | copy-start | bytes 196612
  2.4 31.3 %all-to-all-start = ((bf16[128,4,128]{2,1,0:T(4,128)(2,1)}), bf16[128,4,128]{2,1,0:T(4,128)(2,1)S(1)}, u32[]{:S(2)}, u32[]{:S(2)}) async-start(bf16[128,4,128]{2,1,0:T(4,128)(2,1)} %bitcast.10), calls=%async_computation | async-start | bytes 262144 | tf_op jit(solution)/shard_map/all_to_all | solution.py:295
  21.0 0.7 copy-start.5
  21.0 0.7 copy-start.4
  21.0 0.7 copy-start.3
  33.8 13.4 %copy-start = (bf16[512,512]{1,0:T(8,128)(2,1)S(1)}, bf16[512,512]{1,0:T(8,128)(2,1)}, u32[]{:S(2)}) copy-start(bf16[512,512]{1,0:T(8,128)(2,1)} %edge_feat.5) | copy-start | bytes 1572868
  33.8 13.4 %copy-start.6 = (bf16[512,128]{1,0:T(8,128)(2,1)S(1)}, bf16[512,128]{1,0:T(8,128)(2,1)}, u32[]{:S(2)}) copy-start(bf16[512,128]{1,0:T(8,128)(2,1)} %w_send.1) | copy-start | bytes 393220
  33.8 13.3 %copy-start.7 = (bf16[512,128]{1,0:T(8,128)(2,1)S(1)}, bf16[512,128]{1,0:T(8,128)(2,1)}, u32[]{:S(2)}) copy-start(bf16[512,128]{1,0:T(8,128)(2,1)} %w_recv.1) | copy-start | bytes 393220
  33.8 13.3 %copy-start.8 = (bf16[512,128]{1,0:T(8,128)(2,1)S(1)}, bf16[512,128]{1,0:T(8,128)(2,1)}, u32[]{:S(2)}) copy-start(bf16[512,128]{1,0:T(8,128)(2,1)} %w_edge.1) | copy-start | bytes 393220
  33.8 13.3 %copy-start.9 = (bf16[512,128]{1,0:T(8,128)(2,1)S(1)}, bf16[512,128]{1,0:T(8,128)(2,1)}, u32[]{:S(2)}) copy-start(bf16[512,128]{1,0:T(8,128)(2,1)} %w_out.1) | copy-start | bytes 393220
  49.2 13.6 %all-to-all-start.1 = ((bf16[4,896,128]{2,1,0:T(8,128)(2,1)}), bf16[4,896,128]{2,1,0:T(8,128)(2,1)S(1)}, u32[]{:S(2)}, u32[]{:S(2)}) async-start(bf16[4,896,128]{2,1,0:T(8,128)(2,1)} %get-tuple-element.25), calls=%async_computation.1 | async-start | bytes 1835008 | tf_op jit(solution)/shard_map/all_to_all | solution.py:292
  53.7 6.3 %collective-permute-start = (f32[1024,128]{1,0:T(8,128)S(1)}, f32[1024,128]{1,0:T(8,128)S(1)}, u32[]{:S(2)}, u32[]{:S(2)}) collective-permute-start(f32[1024,128]{1,0:T(8,128)S(1)} %shard_map.150), channel_id=1, source_target_pairs={{0,4},{4,0},{8,12},{12,8},{16,20},{20,16},{24,28},{28,24},{32,36},... | collective-permute-start | bytes 1572872 | tf_op jit(solution)/shard_map/ppermute | solution.py:350
  60.1 6.0 %collective-permute-start.1 = (bf16[512,128]{1,0:T(8,128)(2,1)S(1)}, bf16[512,128]{1,0:T(8,128)(2,1)S(1)}, u32[]{:S(2)}, u32[]{:S(2)}) collective-permute-start(bf16[512,128]{1,0:T(8,128)(2,1)S(1)} %get-tuple-element.24), channel_id=1, source_target_pairs={{0,8},{4,68},{8,0},{12,76},{16,24},{20,84},{24,16},{28,92},{32,40}... | collective-permute-start | bytes 393224 | tf_op jit(solution)/shard_map/ppermute | solution.py:358

commit v9 on v7

--- a/solution.py
+++ b/solution.py
@@ -203,18 +203,16 @@
     given[...] = jnp.where(even, second, first).astype(BF16)
 
 
-def slot_kernel(hidden, indices, terms, edge_grad, recv_part, edge_here, sem):
+def slot_kernel(hidden, indices, terms, edge_grad, recv_part):
     spaces, capacity, quarter = terms.shape
     edges = indices.shape[1]
     full = join(hidden, 0, edges)
-    edge_here[...] = mm_nt(full, join(hidden, edges + 2 * quarter, quarter))
-    (copy,) = fetch(sem, (edge_here, edge_grad))
+    edge_grad[...] = mm_nt(full, join(hidden, edges + 2 * quarter, quarter))
     by_edge = mm_nt(full, join(hidden, edges, quarter))
     sums = pick_sum(hot_by_column(indices[1:2, :], spaces * capacity), by_edge)
     terms[...] = sums.astype(BF16).reshape(terms.shape)
     by_edge = mm_nt(full, join(hidden, edges + quarter, quarter))
     recv_part[...] = pick_sum(hot_by_column(indices[0:1, :], recv_part.shape[0]), by_edge)
-    copy.wait()
 
 
 def payload_kernel(mine, taken, terms, payload):
@@ -225,13 +223,14 @@
 
 
 def last_kernel(
-    arrived, indices, recv_part,
-    node_grad, grad_send, grad_recv, grad_edge, grad_out, node_here, grads_here, sems,
+    arrived, indices, recv_part, edge_here,
+    edge_grad, node_grad, grad_send, grad_recv, grad_edge, grad_out, node_here, grads_here, sems,
 ):
     count, quarter = node_grad.shape
+    copies = fetch(sems.at[5:6], (edge_here, edge_grad))
     back = mm(hot_by_column(indices[4:5, :], count), arrived[:, quarter:])
     node_here[...] = recv_part[...] + back
-    copies = fetch(sems.at[4:5], (node_here, node_grad))
+    copies += fetch(sems.at[4:5], (node_here, node_grad))
     shape = (16, arrived.shape[0])
     place = lax.broadcasted_iota(jnp.int32, shape, 1)
     source = place // CAPACITY
@@ -351,7 +350,7 @@
     taken = lax.ppermute(
         given, "space", [(i, i ^ (Z_STRIDE if i % 2 else 2)) for i in range(spaces)]
     )
-    terms, edge_grad, recv_part = call(
+    terms, edge_part, recv_part = call(
         slot_kernel,
         (
             sds((spaces, capacity, quarter), BF16),
@@ -359,8 +358,6 @@
             sds((node_count, quarter), F32),
         ),
         hidden, indices,
-        out_places=[VMEM, ANY, VMEM],
-        scratch=[pltpu.VMEM((edges, quarter), F32), pltpu.SemaphoreType.DMA((1,))],
         flops=2 * edges * quarter * (3 * width + 2 * slot_count + 2 * node_count),
     )
     (payload,) = call(
@@ -368,15 +365,19 @@
     )
     returned = over_space(payload)
     small = sds((width // spaces, quarter), F32)
-    node_grad, grad_send, grad_recv, grad_edge, grad_out = call(
+    edge_grad, node_grad, grad_send, grad_recv, grad_edge, grad_out = call(
         last_kernel,
-        (sds((node_count, quarter), F32), small, small, small, small),
-        returned, indices, recv_part,
-        out_places=[ANY] * 5,
+        (
+            sds((edges, quarter), F32),
+            sds((node_count, quarter), F32),
+            small, small, small, small,
+        ),
+        returned, indices, recv_part, edge_part,
+        out_places=[ANY] * 6,
         scratch=[
             pltpu.VMEM((node_count, quarter), F32),
             pltpu.VMEM((4, *small.shape), F32),
-            pltpu.SemaphoreType.DMA((5,)),
+            pltpu.SemaphoreType.DMA((6,)),
         ],
         flops=2 * slot_count * quarter * (node_count + 16),
     )

time: 90.3 us -> 89.7 us (level)
  transfers between devices with their start and end apart: 4 -> 4, of which waited for: 4 -> 4; matrix products, arithmetic and copies ran while one was open for 0% -> 0% of each run, Pallas kernels for 4% -> 3%
where the time goes in v9:
time: 89.7 us; the launch traced here: 89.3 us
  blocking collectives  35.4 us (39%)
  starting transfers between devices  29.2 us (33%)
  waiting for transfers between devices  15.5 us (17%)
  Pallas kernels  7.57 us (8%)
    all_to_all x1, blocking collectives, over_space(): moved = lax.all_to_all(x, 'space', split_axis=0, concat_axis=0, tiled=True)  22.1 us
    all_to_all x1, starting transfers between devices, over_space(): moved = lax.all_to_all(x, 'space', split_axis=0, concat_axis=0, tiled=True)  18.6 us
    all_gather x1, blocking collectives, local(): shared = lax.all_gather(packed, 'feat', axis=0, tiled=False)  13.3 us
    all_to_all x1, waiting for transfers between devices, over_space(): moved = lax.all_to_all(x, 'space', split_axis=0, concat_axis=0, tiled=True)  11.9 us
    pallas_call x10, Pallas kernels, call(): pl.pallas_call(kernel, out_shape=list(outs), in_specs=list(places or [VME...  7.57 us
    ppermute x1, starting transfers between devices, local(): taken = lax.ppermute(given, 'space', [(i, i ^ 1) for i in range(spaces)])  4.8 us
    all_to_all x1, starting transfers between devices, over_feat(): return lax.all_to_all(x, 'feat', split_axis=0, concat_axis=0, tiled=True)  3.52 us
    ppermute x1, waiting for transfers between devices, local(): lax.ppermute(given, 'space', [(i, i ^ (Z_STRIDE if i % 2 else 2)) for i i...  2.33 us
  transfers between devices with their start and end apart: 4, of which 4 were waited for; matrix products, arithmetic and copies ran while one was open for 0% of the time, Pallas kernels for 3%

profile of v9, /device:TPU:1, one launch (start us, length us, event | category | flops | bytes accessed | tf_op | source)
XLA Modules:
  0.0 89.3 jit_solution(16936532746688253097)
XLA Ops:
  0.6 1.8 %shard_map.145 = bf16[512,128]{1,0:T(8,128)(2,1)} custom-call(bf16[256,128]{1,0:T(8,128)(2,1)} %node.3, s32[1,512]{1,0:T(1,128)} %send_rows.1), custom_call_target="tpu_custom_call" | custom-call | flops 33554432 | bytes 198656 | tf_op jit(solution)/shard_map/pallas_call | solution.py:257
  2.4 18.6 %all-to-all-start = ((bf16[128,4,128]{2,1,0:T(4,128)(2,1)}), bf16[128,4,128]{2,1,0:T(4,128)(2,1)S(1)}, u32[]{:S(2)}, u32[]{:S(2)}) async-start(bf16[128,4,128]{2,1,0:T(4,128)(2,1)} %bitcast.10), calls=%async_computation | async-start | bytes 262144 | tf_op jit(solution)/shard_map/all_to_all | solution.py:287
  21.0 0.6 copy-done.5
  21.7 0.0 copy-done.4
  21.7 0.0 copy-done.3
  21.7 0.1 shard_map.146
  21.8 11.9 %all-to-all-done = bf16[128,4,128]{2,1,0:T(4,128)(2,1)S(1)} async-done(((bf16[128,4,128]{2,1,0:T(4,128)(2,1)}), bf16[128,4,128]{2,1,0:T(4,128)(2,1)S(1)}, u32[]{:S(2)}, u32[]{:S(2)}) %all-to-all-start) | async-done | bytes 131104 | tf_op jit(solution)/shard_map/all_to_all | solution.py:287
  33.7 0.1 shard_map.147
  33.8 13.3 %all-gather.1.shared = bf16[4,1020,128]{2,1,0:T(8,128)(2,1)S(1)} all-gather(bf16[1,1020,128]{2,1,0:T(8,128)(2,1)S(1)} %bitcast.6), channel_id=2, replica_groups=mesh['space'=128,'feat'=4] {'feat'}, dimensions={0}, use_global_device_ids=true | all-gather | bytes 1305600 | tf_op jit(solution)/shard_map/all_gather | solution.py:318
  47.2 2.0 %shard_map.148 = (bf16[512,128]{1,0:T(8,128)(2,1)S(1)}, bf16[4,896,128]{2,1,0:T(8,128)(2,1)}, bf16[512,128]{1,0:T(8,128)(2,1)S(1)}) custom-call(bf16[4,1020,128]{2,1,0:T(8,128)(2,1)S(1)} %all-gather.1.shared, bf16[512,512]{1,0:T(8,128)(2,1)S(1)} %copy-done, bf16[512,128]{1,0:T(8,128)(2,1)S(1)} %copy-done.6, bf16[512,128]{1,0:T(8,128)(2,1)S(1)} %copy-done.7, ...), custom_call_target="tpu_custom_call" | custom-call | flops 805306368 | bytes 3289088 | tf_op jit(solution)/shard_map/pallas_call | solution.py:257
  49.2 3.5 %all-to-all-start.1 = ((bf16[4,896,128]{2,1,0:T(8,128)(2,1)}), bf16[4,896,128]{2,1,0:T(8,128)(2,1)S(1)}, u32[]{:S(2)}, u32[]{:S(2)}) async-start(bf16[4,896,128]{2,1,0:T(8,128)(2,1)} %get-tuple-element.28), calls=%async_computation.1 | async-start | bytes 1835008 | tf_op jit(solution)/shard_map/all_to_all | solution.py:284
  52.7 1.0 %shard_map.150 = f32[1024,128]{1,0:T(8,128)S(1)} custom-call(s32[1]{0:T(128)S(6)} %select_n.22.core, bf16[4,1020,128]{2,1,0:T(8,128)(2,1)S(1)} %all-gather.1.shared, bf16[512,512]{1,0:T(8,128)(2,1)S(1)} %copy-done, s32[8,512]{1,0:T(8,128)S(1)} %get-tuple-element.23.indices, bf16[512,128]{1,0:T(8,128)(2,1)S(1)} %get-tuple-element.24.activation, ...), custom_call_target="tpu_custom_call" | custom-call | flops 134217728 | bytes 2371588 | tf_op jit(solution)/shard_map/pallas_call | solution.py:257
  53.7 4.8 %collective-permute-start = (f32[1024,128]{1,0:T(8,128)S(1)}, f32[1024,128]{1,0:T(8,128)S(1)}, u32[]{:S(2)}, u32[]{:S(2)}) collective-permute-start(f32[1024,128]{1,0:T(8,128)S(1)} %shard_map.150), channel_id=1, source_target_pairs={{0,4},{4,0},{8,12},{12,8},{16,20},{20,16},{24,28},{28,24},{32,36},... | collective-permute-start | bytes 1572872 | tf_op jit(solution)/shard_map/ppermute | solution.py:342
  58.6 0.6 shard_map.149.kept
  59.2 0.8 collective-permute-done.taken
  60.0 0.1 shard_map.151
  60.1 2.3 %collective-permute-start.1 = (bf16[512,128]{1,0:T(8,128)(2,1)S(1)}, bf16[512,128]{1,0:T(8,128)(2,1)S(1)}, u32[]{:S(2)}, u32[]{:S(2)}) collective-permute-start(bf16[512,128]{1,0:T(8,128)(2,1)S(1)} %get-tuple-element.27), channel_id=1, source_target_pairs={{0,8},{4,68},{8,0},{12,76},{16,24},{20,84},{24,16},{28,92},{32,40}... | collective-permute-start | bytes 393224 | tf_op jit(solution)/shard_map/ppermute | solution.py:350
  62.4 0.4 all-to-all-done.1.hidden
  62.8 1.0 %shard_map.152 = (bf16[128,4,128]{2,1,0:T(4,128)(2,1)S(1)}, f32[512,128]{1,0:T(8,128)S(1)}, f32[256,128]{1,0:T(8,128)S(1)}) custom-call(bf16[4,896,128]{2,1,0:T(8,128)(2,1)S(1)} %all-to-all-done.1.hidden, s32[8,512]{1,0:T(8,128)S(1)} %get-tuple-element.23.indices), custom_call_target="tpu_custom_call" | custom-call | flops 402653184 | bytes 1458176 | tf_op jit(solution)/shard_map/pallas_call | solution.py:257
  63.8 2.3 %collective-permute-done.1.taken = bf16[512,128]{1,0:T(8,128)(2,1)S(1)} collective-permute-done((bf16[512,128]{1,0:T(8,128)(2,1)S(1)}, bf16[512,128]{1,0:T(8,128)(2,1)S(1)}, u32[]{:S(2)}, u32[]{:S(2)}) %collective-permute-start.1) | collective-permute-done | bytes 131104 | tf_op jit(solution)/shard_map/ppermute | solution.py:350
  66.1 0.1 shard_map.153
  66.2 22.1 %all_to_all.15 = bf16[128,4,256]{2,1,0:T(4,128)(2,1)S(1)} all-to-all(bf16[128,4,256]{2,1,0:T(4,128)(2,1)S(1)} %shard_map.153), channel_id=1, replica_groups=mesh['space'=128,'feat'=4] {'space'}, dimensions={0} | all-to-all | bytes 524288 | tf_op jit(solution)/shard_map/all_to_all | solution.py:287
  88.3 0.1 reshape.45.arrived
  88.4 0.9 %shard_map.154 = (f32[512,128]{1,0:T(8,128)}, f32[256,128]{1,0:T(8,128)}, f32[4,128]{1,0:T(4,128)}, f32[4,128]{1,0:T(4,128)}, f32[4,128]{1,0:T(4,128)}, /*index=5*/f32[4,128]{1,0:T(4,128)}) custom-call(bf16[512,256]{1,0:T(8,128)(2,1)S(1)} %reshape.45.arrived, s32[8,512]{1,0:T(8,128)S(1)} %get-tuple-element.23.indices, ...), custom_call_target="tpu_custom_call" | custom-call | flops 35651584 | bytes 1073152 | tf_op jit(solution)/shard_map/pallas_call | solution.py:257
  (17 shorter events, 0.1 us)
Async XLA Ops:
  2.4 18.6 %copy-start.1 = (bf16[256,128]{1,0:T(8,128)(2,1)S(1)}, bf16[256,128]{1,0:T(8,128)(2,1)}, u32[]{:S(2)}) copy-start(bf16[256,128]{1,0:T(8,128)(2,1)} %node.3) | copy-start | bytes 196612
  2.4 18.6 %copy-start.2 = (bf16[256,128]{1,0:T(8,128)(2,1)S(1)}, bf16[256,128]{1,0:T(8,128)(2,1)}, u32[]{:S(2)}) copy-start(bf16[256,128]{1,0:T(8,128)(2,1)} %agg.1) | copy-start | bytes 196612
  2.4 31.3 %all-to-all-start = ((bf16[128,4,128]{2,1,0:T(4,128)(2,1)}), bf16[128,4,128]{2,1,0:T(4,128)(2,1)S(1)}, u32[]{:S(2)}, u32[]{:S(2)}) async-start(bf16[128,4,128]{2,1,0:T(4,128)(2,1)} %bitcast.10), calls=%async_computation | async-start | bytes 262144 | tf_op jit(solution)/shard_map/all_to_all | solution.py:287
  21.0 0.7 copy-start.5
  21.0 0.7 copy-start.4
  21.0 0.7 copy-start.3
  33.8 13.4 %copy-start = (bf16[512,512]{1,0:T(8,128)(2,1)S(1)}, bf16[512,512]{1,0:T(8,128)(2,1)}, u32[]{:S(2)}) copy-start(bf16[512,512]{1,0:T(8,128)(2,1)} %edge_feat.5) | copy-start | bytes 1572868
  33.8 13.4 %copy-start.6 = (bf16[512,128]{1,0:T(8,128)(2,1)S(1)}, bf16[512,128]{1,0:T(8,128)(2,1)}, u32[]{:S(2)}) copy-start(bf16[512,128]{1,0:T(8,128)(2,1)} %w_send.1) | copy-start | bytes 393220
  33.8 13.3 %copy-start.7 = (bf16[512,128]{1,0:T(8,128)(2,1)S(1)}, bf16[512,128]{1,0:T(8,128)(2,1)}, u32[]{:S(2)}) copy-start(bf16[512,128]{1,0:T(8,128)(2,1)} %w_recv.1) | copy-start | bytes 393220
  33.8 13.3 %copy-start.8 = (bf16[512,128]{1,0:T(8,128)(2,1)S(1)}, bf16[512,128]{1,0:T(8,128)(2,1)}, u32[]{:S(2)}) copy-start(bf16[512,128]{1,0:T(8,128)(2,1)} %w_edge.1) | copy-start | bytes 393220
  33.8 13.3 %copy-start.9 = (bf16[512,128]{1,0:T(8,128)(2,1)S(1)}, bf16[512,128]{1,0:T(8,128)(2,1)}, u32[]{:S(2)}) copy-start(bf16[512,128]{1,0:T(8,128)(2,1)} %w_out.1) | copy-start | bytes 393220
  49.2 13.6 %all-to-all-start.1 = ((bf16[4,896,128]{2,1,0:T(8,128)(2,1)}), bf16[4,896,128]{2,1,0:T(8,128)(2,1)S(1)}, u32[]{:S(2)}, u32[]{:S(2)}) async-start(bf16[4,896,128]{2,1,0:T(8,128)(2,1)} %get-tuple-element.28), calls=%async_computation.1 | async-start | bytes 1835008 | tf_op jit(solution)/shard_map/all_to_all | solution.py:284
  53.7 6.3 %collective-permute-start = (f32[1024,128]{1,0:T(8,128)S(1)}, f32[1024,128]{1,0:T(8,128)S(1)}, u32[]{:S(2)}, u32[]{:S(2)}) collective-permute-start(f32[1024,128]{1,0:T(8,128)S(1)} %shard_map.150), channel_id=1, source_target_pairs={{0,4},{4,0},{8,12},{12,8},{16,20},{20,16},{24,28},{28,24},{32,36},... | collective-permute-start | bytes 1572872 | tf_op jit(solution)/shard_map/ppermute | solution.py:342
  60.1 6.0 %collective-permute-start.1 = (bf16[512,128]{1,0:T(8,128)(2,1)S(1)}, bf16[512,128]{1,0:T(8,128)(2,1)S(1)}, u32[]{:S(2)}, u32[]{:S(2)}) collective-permute-start(bf16[512,128]{1,0:T(8,128)(2,1)S(1)} %get-tuple-element.27), channel_id=1, source_target_pairs={{0,8},{4,68},{8,0},{12,76},{16,24},{20,84},{24,16},{28,92},{32,40}... | collective-permute-start | bytes 393224 | tf_op jit(solution)/shard_map/ppermute | solution.py:350

commit v10 on v9

--- a/solution.py
+++ b/solution.py
@@ -235,7 +235,7 @@
     place = lax.broadcasted_iota(jnp.int32, shape, 1)
     source = place // CAPACITY
     core = source % 2
-    side = jnp.where(core == 0, source // 2, source // Z_STRIDE) % 2
+    side = jnp.where(core == 0, source // Z_STRIDE, source // 2) % 2
     row = (2 * core + side) * CAPACITY + place % CAPACITY
     sums = mm(hot(row == lax.broadcasted_iota(jnp.int32, shape, 0)), arrived[:, 0:quarter])
     outs = (grad_send, grad_recv, grad_edge, grad_out)
@@ -340,7 +340,7 @@
         for other in (1, 0)
     )
     taken = lax.ppermute(given, "space", [(i, i ^ 1) for i in range(spaces)])
-    side = jnp.where(core == 0, region // 2, region // Z_STRIDE) % 2
+    side = jnp.where(core == 0, region // Z_STRIDE, region // 2) % 2
     mine, given = call(
         pair_kernel,
         (sds((width, quarter), F32), sds((width, quarter), BF16)),
@@ -348,7 +348,7 @@
         places=[SMEM] + [VMEM] * 2,
     )
     taken = lax.ppermute(
-        given, "space", [(i, i ^ (Z_STRIDE if i % 2 else 2)) for i in range(spaces)]
+        given, "space", [(i, i ^ (2 if i % 2 else Z_STRIDE)) for i in range(spaces)]
     )
     terms, edge_part, recv_part = call(
         slot_kernel,

time: 89.7 us -> 89.7 us (level)
  no operation moved by 1% of the time
where the time goes in v10:
time: 89.7 us; the launch traced here: 89.3 us
  blocking collectives  35.4 us (39%)
  starting transfers between devices  29.4 us (33%)
  waiting for transfers between devices  15.3 us (17%)
  Pallas kernels  7.57 us (8%)
    all_to_all x1, blocking collectives, over_space(): moved = lax.all_to_all(x, 'space', split_axis=0, concat_axis=0, tiled=True)  22.1 us
    all_to_all x1, starting transfers between devices, over_space(): moved = lax.all_to_all(x, 'space', split_axis=0, concat_axis=0, tiled=True)  18.6 us
    all_gather x1, blocking collectives, local(): shared = lax.all_gather(packed, 'feat', axis=0, tiled=False)  13.3 us
    all_to_all x1, waiting for transfers between devices, over_space(): moved = lax.all_to_all(x, 'space', split_axis=0, concat_axis=0, tiled=True)  11.9 us
    pallas_call x10, Pallas kernels, call(): pl.pallas_call(kernel, out_shape=list(outs), in_specs=list(places or [VME...  7.57 us
    ppermute x1, starting transfers between devices, local(): taken = lax.ppermute(given, 'space', [(i, i ^ 1) for i in range(spaces)])  4.8 us
    all_to_all x1, starting transfers between devices, over_feat(): return lax.all_to_all(x, 'feat', split_axis=0, concat_axis=0, tiled=True)  3.52 us
    ppermute x1, starting transfers between devices, local(): lax.ppermute(given, 'space', [(i, i ^ (2 if i % 2 else Z_STRIDE)) for i i...  2.5 us
  transfers between devices with their start and end apart: 4, of which 4 were waited for; matrix products, arithmetic and copies ran while one was open for 0% of the time, Pallas kernels for 3%

profile of v10, /device:TPU:1, one launch (start us, length us, event | category | flops | bytes accessed | tf_op | source)
XLA Modules:
  0.0 89.3 jit_solution(13836562592565999059)
XLA Ops:
  0.6 1.8 %shard_map.145 = bf16[512,128]{1,0:T(8,128)(2,1)} custom-call(bf16[256,128]{1,0:T(8,128)(2,1)} %node.3, s32[1,512]{1,0:T(1,128)} %send_rows.1), custom_call_target="tpu_custom_call" | custom-call | flops 33554432 | bytes 198656 | tf_op jit(solution)/shard_map/pallas_call | solution.py:257
  2.4 18.6 %all-to-all-start = ((bf16[128,4,128]{2,1,0:T(4,128)(2,1)}), bf16[128,4,128]{2,1,0:T(4,128)(2,1)S(1)}, u32[]{:S(2)}, u32[]{:S(2)}) async-start(bf16[128,4,128]{2,1,0:T(4,128)(2,1)} %bitcast.10), calls=%async_computation | async-start | bytes 262144 | tf_op jit(solution)/shard_map/all_to_all | solution.py:287
  21.0 0.6 copy-done.5
  21.7 0.0 copy-done.4
  21.7 0.0 copy-done.3
  21.7 0.1 shard_map.146
  21.8 11.9 %all-to-all-done = bf16[128,4,128]{2,1,0:T(4,128)(2,1)S(1)} async-done(((bf16[128,4,128]{2,1,0:T(4,128)(2,1)}), bf16[128,4,128]{2,1,0:T(4,128)(2,1)S(1)}, u32[]{:S(2)}, u32[]{:S(2)}) %all-to-all-start) | async-done | bytes 131104 | tf_op jit(solution)/shard_map/all_to_all | solution.py:287
  33.7 0.1 shard_map.147
  33.8 13.3 %all-gather.1.shared = bf16[4,1020,128]{2,1,0:T(8,128)(2,1)S(1)} all-gather(bf16[1,1020,128]{2,1,0:T(8,128)(2,1)S(1)} %bitcast.6), channel_id=2, replica_groups=mesh['space'=128,'feat'=4] {'feat'}, dimensions={0}, use_global_device_ids=true | all-gather | bytes 1305600 | tf_op jit(solution)/shard_map/all_gather | solution.py:318
  47.2 2.0 %shard_map.148 = (bf16[512,128]{1,0:T(8,128)(2,1)S(1)}, bf16[4,896,128]{2,1,0:T(8,128)(2,1)}, bf16[512,128]{1,0:T(8,128)(2,1)S(1)}) custom-call(bf16[4,1020,128]{2,1,0:T(8,128)(2,1)S(1)} %all-gather.1.shared, bf16[512,512]{1,0:T(8,128)(2,1)S(1)} %copy-done, bf16[512,128]{1,0:T(8,128)(2,1)S(1)} %copy-done.6, bf16[512,128]{1,0:T(8,128)(2,1)S(1)} %copy-done.7, ...), custom_call_target="tpu_custom_call" | custom-call | flops 805306368 | bytes 3289088 | tf_op jit(solution)/shard_map/pallas_call | solution.py:257
  49.2 3.5 %all-to-all-start.1 = ((bf16[4,896,128]{2,1,0:T(8,128)(2,1)}), bf16[4,896,128]{2,1,0:T(8,128)(2,1)S(1)}, u32[]{:S(2)}, u32[]{:S(2)}) async-start(bf16[4,896,128]{2,1,0:T(8,128)(2,1)} %get-tuple-element.28), calls=%async_computation.1 | async-start | bytes 1835008 | tf_op jit(solution)/shard_map/all_to_all | solution.py:284
  52.7 1.0 %shard_map.150 = f32[1024,128]{1,0:T(8,128)S(1)} custom-call(s32[1]{0:T(128)S(6)} %select_n.22.core, bf16[4,1020,128]{2,1,0:T(8,128)(2,1)S(1)} %all-gather.1.shared, bf16[512,512]{1,0:T(8,128)(2,1)S(1)} %copy-done, s32[8,512]{1,0:T(8,128)S(1)} %get-tuple-element.23.indices, bf16[512,128]{1,0:T(8,128)(2,1)S(1)} %get-tuple-element.24.activation, ...), custom_call_target="tpu_custom_call" | custom-call | flops 134217728 | bytes 2371588 | tf_op jit(solution)/shard_map/pallas_call | solution.py:257
  53.7 4.8 %collective-permute-start = (f32[1024,128]{1,0:T(8,128)S(1)}, f32[1024,128]{1,0:T(8,128)S(1)}, u32[]{:S(2)}, u32[]{:S(2)}) collective-permute-start(f32[1024,128]{1,0:T(8,128)S(1)} %shard_map.150), channel_id=1, source_target_pairs={{0,4},{4,0},{8,12},{12,8},{16,20},{20,16},{24,28},{28,24},{32,36},... | collective-permute-start | bytes 1572872 | tf_op jit(solution)/shard_map/ppermute | solution.py:342
  58.6 0.6 shard_map.149.kept
  59.2 0.8 collective-permute-done.taken
  60.0 0.1 shard_map.151
  60.1 2.5 %collective-permute-start.1 = (bf16[512,128]{1,0:T(8,128)(2,1)S(1)}, bf16[512,128]{1,0:T(8,128)(2,1)S(1)}, u32[]{:S(2)}, u32[]{:S(2)}) collective-permute-start(bf16[512,128]{1,0:T(8,128)(2,1)S(1)} %get-tuple-element.27), channel_id=1, source_target_pairs={{0,64},{4,12},{8,72},{12,4},{16,80},{20,28},{24,88},{28,20},{32,96... | collective-permute-start | bytes 393224 | tf_op jit(solution)/shard_map/ppermute | solution.py:350
  62.6 0.2 all-to-all-done.1.hidden
  62.8 1.0 %shard_map.152 = (bf16[128,4,128]{2,1,0:T(4,128)(2,1)S(1)}, f32[512,128]{1,0:T(8,128)S(1)}, f32[256,128]{1,0:T(8,128)S(1)}) custom-call(bf16[4,896,128]{2,1,0:T(8,128)(2,1)S(1)} %all-to-all-done.1.hidden, s32[8,512]{1,0:T(8,128)S(1)} %get-tuple-element.23.indices), custom_call_target="tpu_custom_call" | custom-call | flops 402653184 | bytes 1458176 | tf_op jit(solution)/shard_map/pallas_call | solution.py:257
  63.8 2.3 %collective-permute-done.1.taken = bf16[512,128]{1,0:T(8,128)(2,1)S(1)} collective-permute-done((bf16[512,128]{1,0:T(8,128)(2,1)S(1)}, bf16[512,128]{1,0:T(8,128)(2,1)S(1)}, u32[]{:S(2)}, u32[]{:S(2)}) %collective-permute-start.1) | collective-permute-done | bytes 131104 | tf_op jit(solution)/shard_map/ppermute | solution.py:350
  66.1 0.1 shard_map.153
  66.2 22.1 %all_to_all.15 = bf16[128,4,256]{2,1,0:T(4,128)(2,1)S(1)} all-to-all(bf16[128,4,256]{2,1,0:T(4,128)(2,1)S(1)} %shard_map.153), channel_id=1, replica_groups=mesh['space'=128,'feat'=4] {'space'}, dimensions={0} | all-to-all | bytes 524288 | tf_op jit(solution)/shard_map/all_to_all | solution.py:287
  88.3 0.1 reshape.45.arrived
  88.4 0.9 %shard_map.154 = (f32[512,128]{1,0:T(8,128)}, f32[256,128]{1,0:T(8,128)}, f32[4,128]{1,0:T(4,128)}, f32[4,128]{1,0:T(4,128)}, f32[4,128]{1,0:T(4,128)}, /*index=5*/f32[4,128]{1,0:T(4,128)}) custom-call(bf16[512,256]{1,0:T(8,128)(2,1)S(1)} %reshape.45.arrived, s32[8,512]{1,0:T(8,128)S(1)} %get-tuple-element.23.indices, ...), custom_call_target="tpu_custom_call" | custom-call | flops 35651584 | bytes 1073152 | tf_op jit(solution)/shard_map/pallas_call | solution.py:257
  (17 shorter events, 0.1 us)
Async XLA Ops:
  2.4 18.6 %copy-start.1 = (bf16[256,128]{1,0:T(8,128)(2,1)S(1)}, bf16[256,128]{1,0:T(8,128)(2,1)}, u32[]{:S(2)}) copy-start(bf16[256,128]{1,0:T(8,128)(2,1)} %node.3) | copy-start | bytes 196612
  2.4 18.6 %copy-start.2 = (bf16[256,128]{1,0:T(8,128)(2,1)S(1)}, bf16[256,128]{1,0:T(8,128)(2,1)}, u32[]{:S(2)}) copy-start(bf16[256,128]{1,0:T(8,128)(2,1)} %agg.1) | copy-start | bytes 196612
  2.4 31.3 %all-to-all-start = ((bf16[128,4,128]{2,1,0:T(4,128)(2,1)}), bf16[128,4,128]{2,1,0:T(4,128)(2,1)S(1)}, u32[]{:S(2)}, u32[]{:S(2)}) async-start(bf16[128,4,128]{2,1,0:T(4,128)(2,1)} %bitcast.10), calls=%async_computation | async-start | bytes 262144 | tf_op jit(solution)/shard_map/all_to_all | solution.py:287
  21.0 0.7 copy-start.5
  21.0 0.7 copy-start.4
  21.0 0.7 copy-start.3
  33.8 13.4 %copy-start = (bf16[512,512]{1,0:T(8,128)(2,1)S(1)}, bf16[512,512]{1,0:T(8,128)(2,1)}, u32[]{:S(2)}) copy-start(bf16[512,512]{1,0:T(8,128)(2,1)} %edge_feat.5) | copy-start | bytes 1572868
  33.8 13.4 %copy-start.6 = (bf16[512,128]{1,0:T(8,128)(2,1)S(1)}, bf16[512,128]{1,0:T(8,128)(2,1)}, u32[]{:S(2)}) copy-start(bf16[512,128]{1,0:T(8,128)(2,1)} %w_send.1) | copy-start | bytes 393220
  33.8 13.3 %copy-start.7 = (bf16[512,128]{1,0:T(8,128)(2,1)S(1)}, bf16[512,128]{1,0:T(8,128)(2,1)}, u32[]{:S(2)}) copy-start(bf16[512,128]{1,0:T(8,128)(2,1)} %w_recv.1) | copy-start | bytes 393220
  33.8 13.3 %copy-start.8 = (bf16[512,128]{1,0:T(8,128)(2,1)S(1)}, bf16[512,128]{1,0:T(8,128)(2,1)}, u32[]{:S(2)}) copy-start(bf16[512,128]{1,0:T(8,128)(2,1)} %w_edge.1) | copy-start | bytes 393220
  33.8 13.3 %copy-start.9 = (bf16[512,128]{1,0:T(8,128)(2,1)S(1)}, bf16[512,128]{1,0:T(8,128)(2,1)}, u32[]{:S(2)}) copy-start(bf16[512,128]{1,0:T(8,128)(2,1)} %w_out.1) | copy-start | bytes 393220
  49.2 13.6 %all-to-all-start.1 = ((bf16[4,896,128]{2,1,0:T(8,128)(2,1)}), bf16[4,896,128]{2,1,0:T(8,128)(2,1)S(1)}, u32[]{:S(2)}, u32[]{:S(2)}) async-start(bf16[4,896,128]{2,1,0:T(8,128)(2,1)} %get-tuple-element.28), calls=%async_computation.1 | async-start | bytes 1835008 | tf_op jit(solution)/shard_map/all_to_all | solution.py:284
  53.7 6.3 %collective-permute-start = (f32[1024,128]{1,0:T(8,128)S(1)}, f32[1024,128]{1,0:T(8,128)S(1)}, u32[]{:S(2)}, u32[]{:S(2)}) collective-permute-start(f32[1024,128]{1,0:T(8,128)S(1)} %shard_map.150), channel_id=1, source_target_pairs={{0,4},{4,0},{8,12},{12,8},{16,20},{20,16},{24,28},{28,24},{32,36},... | collective-permute-start | bytes 1572872 | tf_op jit(solution)/shard_map/ppermute | solution.py:342
  60.1 6.0 %collective-permute-start.1 = (bf16[512,128]{1,0:T(8,128)(2,1)S(1)}, bf16[512,128]{1,0:T(8,128)(2,1)S(1)}, u32[]{:S(2)}, u32[]{:S(2)}) collective-permute-start(bf16[512,128]{1,0:T(8,128)(2,1)S(1)} %get-tuple-element.27), channel_id=1, source_target_pairs={{0,64},{4,12},{8,72},{12,4},{16,80},{20,28},{24,88},{28,20},{32,96... | collective-permute-start | bytes 393224 | tf_op jit(solution)/shard_map/ppermute | solution.py:350

commit v11 on v9

--- a/solution.py
+++ b/solution.py
@@ -148,11 +148,11 @@
         + mm(edge_feat[...], w_edge[...])
     )
     gate = jax.nn.sigmoid(pre_act)
-    activation[...] = (pre_act * gate).astype(BF16)
     hidden[...] = (act_grad * gate * (1.0 + pre_act * (1.0 - gate))).astype(BF16)
     rows = fetch(
         hidden_sems, *((hidden, spread.at[q, 0:edges, :]) for q in range(feats))
     )
+    activation[...] = (pre_act * gate).astype(BF16)
     for copy in (*rows, *blocks):
         copy.wait()
 

time: 89.7 us -> 89.7 us (level)
  no operation moved by 1% of the time
where the time goes in v11:
time: 89.7 us; the launch traced here: 89.3 us
  blocking collectives  35.4 us (39%)
  starting transfers between devices  29.2 us (33%)
  waiting for transfers between devices  15.5 us (17%)
  Pallas kernels  7.57 us (8%)
    all_to_all x1, blocking collectives, over_space(): moved = lax.all_to_all(x, 'space', split_axis=0, concat_axis=0, tiled=True)  22.1 us
    all_to_all x1, starting transfers between devices, over_space(): moved = lax.all_to_all(x, 'space', split_axis=0, concat_axis=0, tiled=True)  18.6 us
    all_gather x1, blocking collectives, local(): shared = lax.all_gather(packed, 'feat', axis=0, tiled=False)  13.3 us
    all_to_all x1, waiting for transfers between devices, over_space(): moved = lax.all_to_all(x, 'space', split_axis=0, concat_axis=0, tiled=True)  11.9 us
    pallas_call x10, Pallas kernels, call(): pl.pallas_call(kernel, out_shape=list(outs), in_specs=list(places or [VME...  7.57 us
    ppermute x1, starting transfers between devices, local(): taken = lax.ppermute(given, 'space', [(i, i ^ 1) for i in range(spaces)])  4.8 us
    all_to_all x1, starting transfers between devices, over_feat(): return lax.all_to_all(x, 'feat', split_axis=0, concat_axis=0, tiled=True)  3.52 us
    ppermute x1, waiting for transfers between devices, local(): lax.ppermute(given, 'space', [(i, i ^ (Z_STRIDE if i % 2 else 2)) for i i...  2.33 us
  transfers between devices with their start and end apart: 4, of which 4 were waited for; matrix products, arithmetic and copies ran while one was open for 0% of the time, Pallas kernels for 3%

profile of v11, /device:TPU:1, one launch (start us, length us, event | category | flops | bytes accessed | tf_op | source)
XLA Modules:
  0.0 89.3 jit_solution(17073707994602917779)
XLA Ops:
  0.6 1.8 %shard_map.145 = bf16[512,128]{1,0:T(8,128)(2,1)} custom-call(bf16[256,128]{1,0:T(8,128)(2,1)} %node.3, s32[1,512]{1,0:T(1,128)} %send_rows.1), custom_call_target="tpu_custom_call" | custom-call | flops 33554432 | bytes 198656 | tf_op jit(solution)/shard_map/pallas_call | solution.py:257
  2.4 18.6 %all-to-all-start = ((bf16[128,4,128]{2,1,0:T(4,128)(2,1)}), bf16[128,4,128]{2,1,0:T(4,128)(2,1)S(1)}, u32[]{:S(2)}, u32[]{:S(2)}) async-start(bf16[128,4,128]{2,1,0:T(4,128)(2,1)} %bitcast.10), calls=%async_computation | async-start | bytes 262144 | tf_op jit(solution)/shard_map/all_to_all | solution.py:287
  21.0 0.6 copy-done.5
  21.7 0.0 copy-done.4
  21.7 0.0 copy-done.3
  21.7 0.1 shard_map.146
  21.8 11.9 %all-to-all-done = bf16[128,4,128]{2,1,0:T(4,128)(2,1)S(1)} async-done(((bf16[128,4,128]{2,1,0:T(4,128)(2,1)}), bf16[128,4,128]{2,1,0:T(4,128)(2,1)S(1)}, u32[]{:S(2)}, u32[]{:S(2)}) %all-to-all-start) | async-done | bytes 131104 | tf_op jit(solution)/shard_map/all_to_all | solution.py:287
  33.7 0.1 shard_map.147
  33.8 13.3 %all-gather.1.shared = bf16[4,1020,128]{2,1,0:T(8,128)(2,1)S(1)} all-gather(bf16[1,1020,128]{2,1,0:T(8,128)(2,1)S(1)} %bitcast.6), channel_id=2, replica_groups=mesh['space'=128,'feat'=4] {'feat'}, dimensions={0}, use_global_device_ids=true | all-gather | bytes 1305600 | tf_op jit(solution)/shard_map/all_gather | solution.py:318
  47.2 2.0 %shard_map.148 = (bf16[512,128]{1,0:T(8,128)(2,1)S(1)}, bf16[4,896,128]{2,1,0:T(8,128)(2,1)}, bf16[512,128]{1,0:T(8,128)(2,1)S(1)}) custom-call(bf16[4,1020,128]{2,1,0:T(8,128)(2,1)S(1)} %all-gather.1.shared, bf16[512,512]{1,0:T(8,128)(2,1)S(1)} %copy-done, bf16[512,128]{1,0:T(8,128)(2,1)S(1)} %copy-done.6, bf16[512,128]{1,0:T(8,128)(2,1)S(1)} %copy-done.7, ...), custom_call_target="tpu_custom_call" | custom-call | flops 805306368 | bytes 3289088 | tf_op jit(solution)/shard_map/pallas_call | solution.py:257
  49.2 3.5 %all-to-all-start.1 = ((bf16[4,896,128]{2,1,0:T(8,128)(2,1)}), bf16[4,896,128]{2,1,0:T(8,128)(2,1)S(1)}, u32[]{:S(2)}, u32[]{:S(2)}) async-start(bf16[4,896,128]{2,1,0:T(8,128)(2,1)} %get-tuple-element.28), calls=%async_computation.1 | async-start | bytes 1835008 | tf_op jit(solution)/shard_map/all_to_all | solution.py:284
  52.7 1.0 %shard_map.150 = f32[1024,128]{1,0:T(8,128)S(1)} custom-call(s32[1]{0:T(128)S(6)} %select_n.22.core, bf16[4,1020,128]{2,1,0:T(8,128)(2,1)S(1)} %all-gather.1.shared, bf16[512,512]{1,0:T(8,128)(2,1)S(1)} %copy-done, s32[8,512]{1,0:T(8,128)S(1)} %get-tuple-element.23.indices, bf16[512,128]{1,0:T(8,128)(2,1)S(1)} %get-tuple-element.24.activation, ...), custom_call_target="tpu_custom_call" | custom-call | flops 134217728 | bytes 2371588 | tf_op jit(solution)/shard_map/pallas_call | solution.py:257
  53.7 4.8 %collective-permute-start = (f32[1024,128]{1,0:T(8,128)S(1)}, f32[1024,128]{1,0:T(8,128)S(1)}, u32[]{:S(2)}, u32[]{:S(2)}) collective-permute-start(f32[1024,128]{1,0:T(8,128)S(1)} %shard_map.150), channel_id=1, source_target_pairs={{0,4},{4,0},{8,12},{12,8},{16,20},{20,16},{24,28},{28,24},{32,36},... | collective-permute-start | bytes 1572872 | tf_op jit(solution)/shard_map/ppermute | solution.py:342
  58.6 0.6 shard_map.149.kept
  59.2 0.8 collective-permute-done.taken
  60.0 0.1 shard_map.151
  60.1 2.3 %collective-permute-start.1 = (bf16[512,128]{1,0:T(8,128)(2,1)S(1)}, bf16[512,128]{1,0:T(8,128)(2,1)S(1)}, u32[]{:S(2)}, u32[]{:S(2)}) collective-permute-start(bf16[512,128]{1,0:T(8,128)(2,1)S(1)} %get-tuple-element.27), channel_id=1, source_target_pairs={{0,8},{4,68},{8,0},{12,76},{16,24},{20,84},{24,16},{28,92},{32,40}... | collective-permute-start | bytes 393224 | tf_op jit(solution)/shard_map/ppermute | solution.py:350
  62.4 0.4 all-to-all-done.1.hidden
  62.8 1.0 %shard_map.152 = (bf16[128,4,128]{2,1,0:T(4,128)(2,1)S(1)}, f32[512,128]{1,0:T(8,128)S(1)}, f32[256,128]{1,0:T(8,128)S(1)}) custom-call(bf16[4,896,128]{2,1,0:T(8,128)(2,1)S(1)} %all-to-all-done.1.hidden, s32[8,512]{1,0:T(8,128)S(1)} %get-tuple-element.23.indices), custom_call_target="tpu_custom_call" | custom-call | flops 402653184 | bytes 1458176 | tf_op jit(solution)/shard_map/pallas_call | solution.py:257
  63.8 2.3 %collective-permute-done.1.taken = bf16[512,128]{1,0:T(8,128)(2,1)S(1)} collective-permute-done((bf16[512,128]{1,0:T(8,128)(2,1)S(1)}, bf16[512,128]{1,0:T(8,128)(2,1)S(1)}, u32[]{:S(2)}, u32[]{:S(2)}) %collective-permute-start.1) | collective-permute-done | bytes 131104 | tf_op jit(solution)/shard_map/ppermute | solution.py:350
  66.1 0.1 shard_map.153
  66.2 22.1 %all_to_all.15 = bf16[128,4,256]{2,1,0:T(4,128)(2,1)S(1)} all-to-all(bf16[128,4,256]{2,1,0:T(4,128)(2,1)S(1)} %shard_map.153), channel_id=1, replica_groups=mesh['space'=128,'feat'=4] {'space'}, dimensions={0} | all-to-all | bytes 524288 | tf_op jit(solution)/shard_map/all_to_all | solution.py:287
  88.3 0.1 reshape.45.arrived
  88.4 0.9 %shard_map.154 = (f32[512,128]{1,0:T(8,128)}, f32[256,128]{1,0:T(8,128)}, f32[4,128]{1,0:T(4,128)}, f32[4,128]{1,0:T(4,128)}, f32[4,128]{1,0:T(4,128)}, /*index=5*/f32[4,128]{1,0:T(4,128)}) custom-call(bf16[512,256]{1,0:T(8,128)(2,1)S(1)} %reshape.45.arrived, s32[8,512]{1,0:T(8,128)S(1)} %get-tuple-element.23.indices, ...), custom_call_target="tpu_custom_call" | custom-call | flops 35651584 | bytes 1073152 | tf_op jit(solution)/shard_map/pallas_call | solution.py:257
  (17 shorter events, 0.1 us)
Async XLA Ops:
  2.4 18.6 %copy-start.1 = (bf16[256,128]{1,0:T(8,128)(2,1)S(1)}, bf16[256,128]{1,0:T(8,128)(2,1)}, u32[]{:S(2)}) copy-start(bf16[256,128]{1,0:T(8,128)(2,1)} %node.3) | copy-start | bytes 196612
  2.4 18.6 %copy-start.2 = (bf16[256,128]{1,0:T(8,128)(2,1)S(1)}, bf16[256,128]{1,0:T(8,128)(2,1)}, u32[]{:S(2)}) copy-start(bf16[256,128]{1,0:T(8,128)(2,1)} %agg.1) | copy-start | bytes 196612
  2.4 31.3 %all-to-all-start = ((bf16[128,4,128]{2,1,0:T(4,128)(2,1)}), bf16[128,4,128]{2,1,0:T(4,128)(2,1)S(1)}, u32[]{:S(2)}, u32[]{:S(2)}) async-start(bf16[128,4,128]{2,1,0:T(4,128)(2,1)} %bitcast.10), calls=%async_computation | async-start | bytes 262144 | tf_op jit(solution)/shard_map/all_to_all | solution.py:287
  21.0 0.7 copy-start.5
  21.0 0.7 copy-start.4
  21.0 0.7 copy-start.3
  33.8 13.4 %copy-start = (bf16[512,512]{1,0:T(8,128)(2,1)S(1)}, bf16[512,512]{1,0:T(8,128)(2,1)}, u32[]{:S(2)}) copy-start(bf16[512,512]{1,0:T(8,128)(2,1)} %edge_feat.5) | copy-start | bytes 1572868
  33.8 13.4 %copy-start.6 = (bf16[512,128]{1,0:T(8,128)(2,1)S(1)}, bf16[512,128]{1,0:T(8,128)(2,1)}, u32[]{:S(2)}) copy-start(bf16[512,128]{1,0:T(8,128)(2,1)} %w_send.1) | copy-start | bytes 393220
  33.8 13.3 %copy-start.7 = (bf16[512,128]{1,0:T(8,128)(2,1)S(1)}, bf16[512,128]{1,0:T(8,128)(2,1)}, u32[]{:S(2)}) copy-start(bf16[512,128]{1,0:T(8,128)(2,1)} %w_recv.1) | copy-start | bytes 393220
  33.8 13.3 %copy-start.8 = (bf16[512,128]{1,0:T(8,128)(2,1)S(1)}, bf16[512,128]{1,0:T(8,128)(2,1)}, u32[]{:S(2)}) copy-start(bf16[512,128]{1,0:T(8,128)(2,1)} %w_edge.1) | copy-start | bytes 393220
  33.8 13.3 %copy-start.9 = (bf16[512,128]{1,0:T(8,128)(2,1)S(1)}, bf16[512,128]{1,0:T(8,128)(2,1)}, u32[]{:S(2)}) copy-start(bf16[512,128]{1,0:T(8,128)(2,1)} %w_out.1) | copy-start | bytes 393220
  49.2 13.6 %all-to-all-start.1 = ((bf16[4,896,128]{2,1,0:T(8,128)(2,1)}), bf16[4,896,128]{2,1,0:T(8,128)(2,1)S(1)}, u32[]{:S(2)}, u32[]{:S(2)}) async-start(bf16[4,896,128]{2,1,0:T(8,128)(2,1)} %get-tuple-element.28), calls=%async_computation.1 | async-start | bytes 1835008 | tf_op jit(solution)/shard_map/all_to_all | solution.py:284
  53.7 6.3 %collective-permute-start = (f32[1024,128]{1,0:T(8,128)S(1)}, f32[1024,128]{1,0:T(8,128)S(1)}, u32[]{:S(2)}, u32[]{:S(2)}) collective-permute-start(f32[1024,128]{1,0:T(8,128)S(1)} %shard_map.150), channel_id=1, source_target_pairs={{0,4},{4,0},{8,12},{12,8},{16,20},{20,16},{24,28},{28,24},{32,36},... | collective-permute-start | bytes 1572872 | tf_op jit(solution)/shard_map/ppermute | solution.py:342
  60.1 6.0 %collective-permute-start.1 = (bf16[512,128]{1,0:T(8,128)(2,1)S(1)}, bf16[512,128]{1,0:T(8,128)(2,1)S(1)}, u32[]{:S(2)}, u32[]{:S(2)}) collective-permute-start(bf16[512,128]{1,0:T(8,128)(2,1)S(1)} %get-tuple-element.27), channel_id=1, source_target_pairs={{0,8},{4,68},{8,0},{12,76},{16,24},{20,84},{24,16},{28,92},{32,40}... | collective-permute-start | bytes 393224 | tf_op jit(solution)/shard_map/ppermute | solution.py:350
